TPU v7x, 32 devices: a whole 2x2x4 slice. The times are simulated.
32 devices in a mesh: ctx: 8 (over y, x, core), fsdp: 4 (over z).
Axes of the slice: x: 2, y: 2, z: 4, core: 2. Of those that a mesh axis runs over, the one named last changes fastest.
Arguments:
- tokens: bfloat16 [4, 2048, 1536], P('fsdp', 'ctx'), may hold values from -6 to 6
- doc_ids: int32 [4, 2048], P('fsdp', 'ctx'), may hold values from 0 to 8, as said below
- routes: int32 [4, 2048, 8], P('fsdp', 'ctx'), may hold values from 0 to 39, all different within a row
- slot_order: int32 [4, 2048, 8], P('fsdp', 'ctx'), may hold values from 0 to 2047, as said below
- norm1_gain: float32 [1536], replicated, may hold values from 0.5 to 1.5
- norm2_gain: float32 [1536], replicated, may hold values from 0.5 to 1.5
- w_query: bfloat16 [1536, 1536], P('fsdp'), may hold values from -0.15625 to 0.15625
- key_matrix: bfloat16 [1536, 512], P('fsdp'), may hold values from -0.15625 to 0.15625
- value_matrix: bfloat16 [1536, 512], P('fsdp'), may hold values from -0.15625 to 0.15625
- w_out: bfloat16 [1536, 1536], P('fsdp'), may hold values from -2.5 to 2.5
- w_router: bfloat16 [1536, 40], P('fsdp'), may hold values from -0.078125 to 0.078125
- w_gate: bfloat16 [8, 1536, 512], P(None, 'fsdp'), may hold values from -0.15625 to 0.15625
- w_up: bfloat16 [8, 1536, 512], P(None, 'fsdp'), may hold values from -0.15625 to 0.15625
- w_down: bfloat16 [8, 512, 1536], P(None, 'fsdp'), may hold values from -2 to 2
- cotangent: bfloat16 [4, 2048, 1536], P('fsdp', 'ctx'), may hold values from -6 to 6
Outputs:
- output: bfloat16 [4, 2048, 1536], P('fsdp', 'ctx')
- input_grad: float32 [4, 2048, 1536], P('fsdp', 'ctx')
- grad_norm1: float32 [1536], P('fsdp')
- grad_norm2: float32 [1536], P('fsdp')
- grad_w_query: float32 [1536, 1536], P('fsdp')
- grad_w_key: float32 [1536, 512], P('fsdp')
- grad_w_value: float32 [1536, 512], P('fsdp')
- grad_w_out: float32 [1536, 1536], P('fsdp')
- grad_w_router: float32 [1536, 40], P('fsdp')
- grad_w_gate: float32 [8, 1536, 512], P(None, 'fsdp')
- grad_w_up: float32 [8, 1536, 512], P(None, 'fsdp')
- grad_w_down: float32 [8, 512, 1536], P(None, 'fsdp')
Inputs may be any that keep to these rules, and one draw needn't show every extreme that they name: `doc_ids`: along each stream the document numbers never fall and begin at 0; one document begins within the first 256 tokens and ends within the last 256 tokens. `slot_order`: within each aligned block of 256 tokens of a stream the 2048 entries are a permutation.
All inputs are finite; a program needn't handle non-finite values.
Results may differ from a plain program's by a relative error of at most 0.025.
Values may be sent and summed in bfloat16 or wider, within the bound.
A program may use at most 320 MiB of HBM per device.

v0:
```python
import functools

import jax
import jax.numpy as jnp
import numpy as np
from jax import lax
from jax.experimental import pallas as pl
from jax.experimental.pallas import tpu as pltpu
from jax.sharding import PartitionSpec as P

QUERY_HEADS = 24
KEY_VALUE_HEADS = 8
HEAD_DIM = 64
TOPK = 8
EXP_WIN = 8
TOK_DEV = 256
CAP = 64
GROUP = 8
HEADS = QUERY_HEADS // KEY_VALUE_HEADS
QW = HEADS * HEAD_DIM
HW = QW + 2 * HEAD_DIM
WIDE = HW + HEAD_DIM
ROUTER = HEAD_DIM
EXPERTS_MOST = 40
LANES = 128

epsilon = 1e-06
score_masked = -1e30
bf16 = jnp.bfloat16
f32 = jnp.float32
VMEM = pltpu.VMEM
MESH = pl.DeviceIdType.MESH
DMA = pltpu.SemaphoreType.DMA
IN_VMEM = pl.BlockSpec(memory_space=VMEM)
IN_ANY = pl.BlockSpec(memory_space=pl.ANY)


def dot(left, right, dims=((1,), (0,))):
    return lax.dot_general(left, right, (dims, ((), ())), preferred_element_type=f32)


def block(index, size=TOK_DEV):
    return pl.ds(pl.multiple_of(index * size, size), size)


def shape(dims, dtype):
    return jax.ShapeDtypeStruct(dims, dtype)


def params(collective_id=None, limit=56):
    return pltpu.CompilerParams(
        collective_id=collective_id,
        has_side_effects=collective_id is not None,
        vmem_limit_bytes=limit << 20,
    )


def flip(index, bit):
    return index + (1 - 2 * ((index // bit) % 2)) * bit


class Place:
    def __init__(self):
        ctx = lax.axis_index("ctx")
        self.base = (ctx // GROUP) * GROUP
        self.me = ctx - self.base
        self.z = lax.axis_index("fsdp")
        self.depth = lax.axis_size("fsdp")
        self.near = [flip(self.me, bit) for bit in (1, 2, 4)]

    def ctx(self, index):
        return {"ctx": self.base + index}

    def fsdp(self, index):
        return {"fsdp": index}

    def others(self):
        return [self.ctx(lax.rem(self.me + j, GROUP)) for j in range(1, GROUP)]

    def layers(self):
        return [self.fsdp(lax.rem(self.z + j, self.depth)) for j in range(1, self.depth)]


def greet(devices):
    ready = pltpu.get_barrier_semaphore()
    for device in devices:
        pl.semaphore_signal(ready, inc=1, device_id=device, device_id_type=MESH)
    pl.semaphore_wait(ready, len(devices))


def remote(source, target, send, receive, device):
    return pltpu.make_async_remote_copy(
        src_ref=source,
        dst_ref=target,
        send_sem=send,
        recv_sem=receive,
        device_id=device,
        device_id_type=MESH,
    )


class Spread:
    SEMS = 14

    def __init__(self, place, source, land, part, send, receive):
        me = place.me
        core, side, row = place.near
        across = flip(side, 4)

        def plan(slot, owner, half, device):
            target = part(land(owner), half)
            first = part(source, half) if slot < 6 else target
            return remote(first, target, send.at[slot], receive.at[slot], place.ctx(device))

        self.copies = [
            plan(0, me, 0, side), plan(1, me, 1, side), plan(2, me, 0, row), plan(3, me, 1, row),
            plan(4, me, 0, core), plan(5, me, 1, core), plan(6, side, 0, core),
            plan(7, side, 1, core), plan(8, row, 0, core), plan(9, row, 1, core),
            plan(10, side, 1, row), plan(11, row, 0, side), plan(12, across, 0, core),
            plan(13, across, 1, core),
        ]

    def go(self, *slots):
        for slot in slots:
            self.copies[slot].start()

    def wait(self, *slots):
        for slot in slots:
            self.copies[slot].wait_recv()

    def start(self):
        self.go(1, 2, 0, 3, 4, 5)

    def step1(self):
        self.wait(1)
        self.go(10, 7)
        self.wait(2)
        self.go(11, 8)

    def step2(self):
        self.wait(0)
        self.go(6)
        self.wait(3)
        self.go(9)

    def step3(self):
        self.wait(10)
        self.go(13)
        self.wait(11)
        self.go(12)

    def sent(self):
        for copy in self.copies:
            copy.wait_send()

    def last(self):
        self.wait(4, 5, 6, 7, 8, 9, 12, 13)


def turned(values, cosine, sine):
    lane = lax.broadcasted_iota(jnp.int32, values.shape, 1) % HEAD_DIM
    low = lane < HEAD_DIM // 2
    other = jnp.where(
        low, -pltpu.roll(values, LANES - HEAD_DIM // 2, 1), pltpu.roll(values, HEAD_DIM // 2, 1)
    )
    return values * cosine + other * sine


def project_kernel(
    tokens_ref, gain_ref, w_ref, w_out_ref, cos_ref, sin_ref, docs_ref,
    normed_ref, w_all_ref, w_out_all_ref, q_ref, k_ref, v_ref, docs_all_ref,
    z_send, z_recv, o_send, o_recv, d_send, d_recv, c_send, c_recv, local,
):
    place = Place()
    me, z = place.me, place.z
    strip = w_out_all_ref.shape[1]
    greet(place.others() + place.layers())
    own_out = w_out_ref.at[pl.ds(pl.multiple_of(me * strip, strip), strip), :]
    moves = [
        pltpu.make_async_copy(w_ref, w_all_ref.at[z], local.at[0]),
        pltpu.make_async_copy(own_out, w_out_all_ref.at[z], local.at[1]),
    ]
    for move in moves:
        move.start()
    weights = []
    for j, device in enumerate(place.layers()):
        weights.append(remote(w_ref, w_all_ref.at[z], z_send.at[j], z_recv.at[j], device))
        weights[-1].start()

    x = tokens_ref[...].astype(f32)
    scale = lax.rsqrt(jnp.mean(x * x, axis=-1, keepdims=True) + epsilon)
    normed_ref[me] = (x * scale * gain_ref[...]).astype(bf16)
    half = TOK_DEV // 2
    spread = Spread(
        place, normed_ref.at[me], lambda owner: normed_ref.at[owner],
        lambda ref, h: ref.at[pl.ds(h * half, half)], c_send, c_recv,
    )
    spread.start()
    docs_all_ref[me] = docs_ref[...]
    outs = []
    for j, device in enumerate(place.others()):
        outs.append(
            remote(docs_ref, docs_all_ref.at[me], d_send.at[j], d_recv.at[j], device)
        )
        outs[-1].start()
    for j, device in enumerate(place.layers()):
        outs.append(remote(own_out, w_out_all_ref.at[z], o_send.at[j], o_recv.at[j], device))
        outs[-1].start()
    for copy in weights:
        copy.wait_recv()
    moves[0].wait()

    def project(owner):
        weight = w_all_ref[...].reshape(-1, WIDE)
        linear = dot(normed_ref[owner], weight)
        cosine, sine = cos_ref[block(owner), :], sin_ref[block(owner), :]
        first = turned(linear[:, :LANES], cosine, sine) * HEAD_DIM ** (-0.5)
        second = turned(linear[:, LANES : 2 * LANES], cosine, sine)
        q_ref[block(owner), :LANES] = first.astype(bf16)
        q_ref[block(owner), LANES:] = (second[:, :HEAD_DIM] * HEAD_DIM ** (-0.5)).astype(bf16)
        k_ref[block(owner), :] = second[:, HEAD_DIM:].astype(bf16)
        v_ref[block(owner), :] = linear[:, 2 * LANES : HW].astype(bf16)

    core, side, row = place.near
    across = flip(side, 4)
    order = [me, core, side, row, flip(side, 1), flip(row, 1), across, flip(across, 1)]

    def step(i, _):
        @pl.when(i == 1)
        def _():
            spread.step1()
            spread.wait(4, 5)

        @pl.when(i == 2)
        def _():
            spread.step2()

        @pl.when(i == 4)
        def _():
            spread.wait(6, 7)

        @pl.when(i == 5)
        def _():
            spread.wait(8, 9)

        @pl.when(i == 6)
        def _():
            spread.step3()

        @pl.when(i == 7)
        def _():
            spread.wait(12, 13)

        owner = order[7]
        for at in range(7):
            owner = jnp.where(i == at, order[at], owner)
        project(owner)
        return 0

    lax.fori_loop(0, GROUP, step, 0)
    for copy in outs:
        copy.wait()
    for copy in weights:
        copy.wait_send()
    moves[1].wait()
    spread.sent()


def project_call(tokens, gain, w_h, w_out, cosine, sine, docs, depth):
    rows, width = tokens.shape
    span = GROUP * rows
    strip = w_out.shape[0] // GROUP
    sems = [DMA((depth - 1,))] * 4 + [DMA((GROUP - 1,))] * 2
    sems += [DMA((Spread.SEMS,))] * 2 + [DMA((2,))]
    return pl.pallas_call(
        project_kernel,
        out_shape=(
            shape((GROUP, rows, width), bf16),
            shape((depth,) + w_h.shape, bf16),
            shape((depth, strip, w_out.shape[1]), bf16),
            shape((span, QW), bf16),
            shape((span, HEAD_DIM), bf16),
            shape((span, HEAD_DIM), bf16),
            shape((GROUP,) + docs.shape, jnp.int32),
        ),
        in_specs=[IN_VMEM, IN_VMEM, IN_VMEM, IN_ANY, IN_VMEM, IN_VMEM, IN_VMEM],
        out_specs=(IN_VMEM, IN_VMEM, IN_ANY, IN_VMEM, IN_VMEM, IN_VMEM, IN_VMEM),
        scratch_shapes=sems,
        compiler_params=params(1),
        name="project",
    )(tokens, gain, w_h, w_out, cosine, sine, docs)


def docs_column(row):
    return jnp.broadcast_to(row.astype(f32), (8, row.shape[1])).T[:, :1]


def attend_kernel(
    n_blocks, q_ref, k_ref, v_ref, docs_ref, strips_ref,
    o_ref, lse_ref, attended_ref, out_weight_ref, staged_ref,
    vt_ref, docs_col_ref, top_ref, sum_ref, acc_ref, a_send, a_recv, w_send, w_recv, local,
):
    T = TOK_DEV
    place = Place()
    me = place.me
    first = place.base
    greet(place.others())
    depth = strips_ref.shape[0]
    move = pltpu.make_async_copy(strips_ref, out_weight_ref.at[:, me], local.at[0])
    move.start()
    spread = Spread(
        place, strips_ref, lambda owner: out_weight_ref.at[:, owner],
        lambda ref, h: ref.at[pl.ds(h * (depth // 2), depth // 2)], w_send, w_recv,
    )
    spread.start()

    def turn(i, _):
        vt_ref[:, block(i)] = v_ref[block(i), :].T
        docs_col_ref[i] = docs_column(docs_ref[i])
        return 0

    lax.fori_loop(0, n_blocks, turn, 0)

    def tile(kb, qb, mask):
        kt = k_ref[block(kb), :]
        vt = vt_ref[:, block(kb)]
        heads = range(HEADS)
        parts = [slice(h * 64, (h + 1) * 64) for h in heads]
        s = [dot(kt, q_ref[block(qb), parts[h]], ((1,), (1,))) for h in heads]
        if mask is not None:
            s = [jnp.where(mask, x, score_masked) for x in s]
        old = [top_ref[h : h + 1, :] for h in heads]
        new = [jnp.maximum(old[h], jnp.max(s[h], axis=0, keepdims=True)) for h in heads]
        p = [jnp.exp(s[h] - new[h]) for h in heads]
        factor = [jnp.exp(old[h] - new[h]) for h in heads]
        total = [
            sum_ref[h : h + 1, :] * factor[h] + jnp.sum(p[h], axis=0, keepdims=True) for h in heads
        ]
        mixed = [acc_ref[parts[h], :] * factor[h] + dot(vt, p[h].astype(bf16)) for h in heads]
        for h in heads:
            top_ref[h : h + 1, :] = new[h]
            sum_ref[h : h + 1, :] = total[h]
            acc_ref[parts[h], :] = mixed[h]

    def same(kb, gq):
        return docs_col_ref[kb] == docs_ref[gq].astype(f32)

    def attended_copy(j, qb):
        return remote(
            staged_ref.at[qb], attended_ref.at[me], a_send.at[j], a_recv.at[j], place.ctx(qb)
        )

    def q_block(j, _):
        @pl.when(j == 1)
        def _():
            spread.step1()

        @pl.when(j == 2)
        def _():
            spread.step2()

        @pl.when(j == 4)
        def _():
            spread.step3()

        qb = lax.rem(me + j, GROUP)
        gq = first + qb
        top_ref[...] = jnp.full_like(top_ref, score_masked)
        sum_ref[...] = jnp.ones_like(sum_ref)
        acc_ref[...] = jnp.zeros_like(acc_ref)
        last = gq == n_blocks - 1

        def k_block(kb, _):
            edge = jnp.logical_or(kb == 0, last)

            @pl.when(edge)
            def _():
                tile(kb, qb, same(kb, gq))

            @pl.when(jnp.logical_not(edge))
            def _():
                tile(kb, qb, None)

            return 0

        lax.fori_loop(0, gq, k_block, 0)
        keys = lax.broadcasted_iota(jnp.int32, (T, T), 0)
        queries = lax.broadcasted_iota(jnp.int32, (T, T), 1)
        tile(gq, qb, same(gq, gq) & (keys <= queries))
        lse_ref[qb] = top_ref[...] + jnp.log(sum_ref[...])
        for h in range(HEADS):
            part = slice(h * 64, (h + 1) * 64)
            acc_ref[part, :] = acc_ref[part, :] / sum_ref[h : h + 1, :]
        mixed = acc_ref[...].T
        o_ref[block(qb), :] = mixed
        staged_ref[qb] = mixed.astype(bf16)

        @pl.when(j > 0)
        def _():
            attended_copy(j, qb).start()

        return 0

    lax.fori_loop(0, GROUP, q_block, 0)
    own = pltpu.make_async_copy(staged_ref.at[me], attended_ref.at[me], local.at[1])
    own.start()
    own.wait()
    move.wait()
    for j in range(1, GROUP):
        attended_copy(j, lax.rem(me + j, GROUP)).wait()
    spread.last()
    spread.sent()


def attend_call(q, k, v, docs, strips):
    n = k.shape[0] // TOK_DEV
    span = q.shape[0]
    return pl.pallas_call(
        functools.partial(attend_kernel, n),
        out_shape=(
            shape((span, QW), f32),
            shape((GROUP, 8, TOK_DEV), f32),
            shape((GROUP, TOK_DEV, QW), bf16),
            shape((strips.shape[0], GROUP) + strips.shape[1:], bf16),
            shape((GROUP, TOK_DEV, QW), bf16),
        ),
        in_specs=[IN_VMEM] * 4 + [IN_ANY],
        out_specs=(IN_VMEM, IN_VMEM, IN_VMEM, IN_ANY, IN_VMEM),
        scratch_shapes=[
            VMEM((64, n * TOK_DEV), bf16),
            VMEM((n, TOK_DEV, 1), f32),
            VMEM((8, TOK_DEV), f32),
            VMEM((8, TOK_DEV), f32),
            VMEM((QW, TOK_DEV), f32),
            DMA((GROUP,)),
            DMA((GROUP,)),
            DMA((Spread.SEMS,)),
            DMA((Spread.SEMS,)),
            DMA((2,)),
        ],
        compiler_params=params(2),
        name="attend",
    )(q, k, v, docs, strips)


NEVER = 4096.0


def dispatch_kernel(
    attended_ref, weight_ref, tokens_ref, gain_ref, w_all_ref, routes_ref, order_ref,
    cotangent_ref,
    residual_ref, normed_ref, gates_ref, placed_ref, slot_gates_ref, rows_ref, grads_ref,
    mixed_ref, own_rows, own_grads, r_send, r_recv, g_send, g_recv, local,
):
    place = Place()
    me = place.me
    greet(place.others())
    rows, width = tokens_ref.shape
    for j in range(GROUP):
        mixed_ref[:, j * QW : (j + 1) * QW] = attended_ref[j]

    def out_columns(i, _):
        columns = block(i)
        residual_ref[:, columns] = tokens_ref[:, columns].astype(f32) + dot(
            mixed_ref[...], weight_ref[:, columns]
        )
        return 0

    lax.fori_loop(0, width // TOK_DEV, out_columns, 0)
    residual = residual_ref[...]
    scale = lax.rsqrt(jnp.mean(residual * residual, axis=-1, keepdims=True) + epsilon)
    normed_ref[...] = (residual * scale * gain_ref[...]).astype(bf16)
    router = w_all_ref[:, :, WIDE - LANES :].reshape(width, LANES)
    logits = dot(normed_ref[...], router)
    lane = lax.broadcasted_iota(jnp.int32, (rows, LANES), 1)
    chosen = lane < 0
    priority = jnp.full((rows, LANES), NEVER, f32)
    for k in range(TOPK):
        pick = lane == routes_ref[:, k : k + 1] + ROUTER
        chosen = chosen | pick
        priority = jnp.where(pick, order_ref[:, k : k + 1].astype(f32), priority)
    logits = jnp.where(chosen, logits, score_masked)
    top = jnp.max(logits, axis=-1, keepdims=True)
    gates = jnp.where(chosen, jnp.exp(logits - top), 0.0)
    gates = gates / jnp.sum(gates, axis=-1, keepdims=True)
    gates_ref[...] = gates
    gates_turned, priority_turned = gates.T, priority.T
    slot = lax.broadcasted_iota(jnp.int32, (CAP, rows), 0).astype(f32)
    for e in range(EXP_WIN):
        at = ROUTER + e
        mine = priority_turned[at : at + 1, :]
        before = jnp.where(priority[:, at : at + 1] < mine, 1.0, 0.0)
        before = jnp.sum(before, axis=0, keepdims=True)
        placed = (slot == before) & (mine < NEVER)
        placed_ref[e] = jnp.where(placed, 1.0, 0.0).astype(bf16)
        slot_gates_ref[e] = jnp.sum(
            jnp.where(placed, gates_turned[at : at + 1, :], 0.0), axis=1, keepdims=True
        )

    def copy(source, target, send, receive, j):
        to = lax.rem(me + j, GROUP)
        return remote(
            source.at[to], target.at[me], send.at[j], receive.at[j], place.ctx(to)
        )

    def send_rows(j, _):
        to = lax.rem(me + j, GROUP)
        own_rows[to] = dot(placed_ref[to], normed_ref[...]).astype(bf16)

        @pl.when(j < GROUP)
        def _():
            copy(own_rows, rows_ref, r_send, r_recv, j).start()

        return 0

    def send_grads(j, _):
        to = lax.rem(me + j, GROUP)
        routed = dot(placed_ref[to], cotangent_ref[...])
        own_grads[to] = (routed * slot_gates_ref[to]).astype(bf16)

        @pl.when(j < GROUP)
        def _():
            copy(own_grads, grads_ref, g_send, g_recv, j).start()

        return 0

    lax.fori_loop(1, GROUP + 1, send_rows, 0)
    lax.fori_loop(1, GROUP + 1, send_grads, 0)
    moves = [
        pltpu.make_async_copy(own_rows.at[me], rows_ref.at[me], local.at[0]),
        pltpu.make_async_copy(own_grads.at[me], grads_ref.at[me], local.at[1]),
    ]
    for move in moves:
        move.start()
    for j in range(1, GROUP):
        copy(own_rows, rows_ref, r_send, r_recv, j).wait()
    for j in range(1, GROUP):
        copy(own_grads, grads_ref, g_send, g_recv, j).wait()
    for move in moves:
        move.wait()


def dispatch_call(attended, weight, tokens, gain, w_all, routes, order, cotangent):
    rows, width = tokens.shape
    slots = (GROUP, CAP, width)
    return pl.pallas_call(
        dispatch_kernel,
        out_shape=(
            shape((rows, width), f32),
            shape((rows, width), bf16),
            shape((rows, LANES), f32),
            shape((EXP_WIN, CAP, rows), bf16),
            shape((EXP_WIN, CAP, 1), f32),
            shape(slots, bf16),
            shape(slots, bf16),
        ),
        in_specs=[IN_VMEM] * 8,
        out_specs=(IN_VMEM,) * 5 + (IN_ANY,) * 2,
        scratch_shapes=[
            VMEM((rows, GROUP * QW), bf16),
            VMEM(slots, bf16),
            VMEM(slots, bf16),
        ]
        + [DMA((GROUP,))] * 4
        + [DMA((2,))],
        compiler_params=params(3),
        name="dispatch",
    )(attended, weight, tokens, gain, w_all, routes, order, cotangent)


def combine_kernel(
    sent_out_ref, sent_grad_ref, residual_ref, normed_ref, gates_ref, placed_ref, slot_gates_ref,
    cotangent_ref, gain_ref, w_all_ref, weight_ref,
    output_ref, grad_residual_ref, heads_ref, grad_router_ref, grad_gain_ref,
    out_ref, back_ref, sum_ref, turned_ref, staged_ref, attn_ref, attended_ref,
    o_send, o_recv, b_send, b_recv, h_send, h_recv, local,
):
    place = Place()
    me = place.me
    greet(place.others())
    rows, width = residual_ref.shape

    def copy(source, target, send, receive, j):
        to = lax.rem(me + j, GROUP)
        return remote(
            source.at[to], target.at[me], send.at[j], receive.at[j], place.ctx(to)
        )

    outs = [copy(sent_out_ref, out_ref, o_send, o_recv, j) for j in range(1, GROUP)]
    backs = [copy(sent_grad_ref, back_ref, b_send, b_recv, j) for j in range(1, GROUP)]
    for one in outs + backs:
        one.start()
    moves = [
        pltpu.make_async_copy(sent_out_ref.at[me], out_ref.at[me], local.at[0]),
        pltpu.make_async_copy(sent_grad_ref.at[me], back_ref.at[me], local.at[1]),
    ]
    for move in moves:
        move.start()
    sum_ref[...] = residual_ref[...]
    turned_ref[...] = jnp.zeros_like(turned_ref)
    moves[0].wait()
    for one in outs:
        one.wait_recv()

    def add_expert(e, _):
        placed = placed_ref[e]
        came = out_ref[e].astype(f32)
        sum_ref[...] += dot(placed, (came * slot_gates_ref[e]).astype(bf16), ((0,), (0,)))
        routed = dot(placed, cotangent_ref[...])
        slot_grad = jnp.sum(routed * came, axis=1, keepdims=True)
        turned_ref[pl.ds(ROUTER + e, 1), :] = jnp.sum(
            placed.astype(f32) * slot_grad, axis=0, keepdims=True
        )
        return 0

    lax.fori_loop(0, EXP_WIN, add_expert, 0)
    output_ref[...] = sum_ref[...].astype(bf16)

    gates = gates_ref[...]
    grad_gates = turned_ref[...].T
    weighted = jnp.sum(gates * grad_gates, axis=-1, keepdims=True)
    grad_logits = (gates * (grad_gates - weighted)).astype(bf16)
    router = w_all_ref[:, :, WIDE - LANES :].reshape(width, LANES)
    sum_ref[...] = dot(grad_logits, router, ((1,), (1,)))
    grad_router_ref[...] = dot(normed_ref[...], grad_logits, ((0,), (0,)))
    moves[1].wait()
    for one in backs:
        one.wait_recv()

    def add_back(e, _):
        sum_ref[...] += dot(placed_ref[e], back_ref[e], ((0,), (0,)))
        return 0

    lax.fori_loop(0, EXP_WIN, add_back, 0)
    residual = residual_ref[...]
    grad_normed = sum_ref[...]
    scale = lax.rsqrt(jnp.mean(residual * residual, axis=-1, keepdims=True) + epsilon)
    scaled = grad_normed * gain_ref[...]
    inner = jnp.mean(scaled * residual, axis=-1, keepdims=True)
    grad = scale * scaled - residual * (scale * scale * scale * inner)
    grad_gain_ref[...] = jnp.sum(grad_normed * residual * scale, axis=0, keepdims=True)
    grad_residual = cotangent_ref[...].astype(f32) + grad
    grad_residual_ref[...] = grad_residual
    attn_ref[...] = grad_residual.astype(bf16)

    def out_rows(i, _):
        attended_ref[:, block(i)] = dot(attn_ref[...], weight_ref[block(i), :], ((1,), (1,))).astype(
            bf16
        )
        return 0

    lax.fori_loop(0, width // TOK_DEV, out_rows, 0)
    for h in range(GROUP):
        staged_ref[h, :, :QW] = attended_ref[:, h * QW : (h + 1) * QW]
        staged_ref[h, :, QW:] = attn_ref[:, h * QW : (h + 1) * QW]
    heads = [copy(staged_ref, heads_ref, h_send, h_recv, j) for j in range(1, GROUP)]
    for one in heads:
        one.start()
    move = pltpu.make_async_copy(staged_ref.at[me], heads_ref.at[me], local.at[2])
    move.start()
    for one in outs + backs:
        one.wait_send()
    for one in heads:
        one.wait()
    move.wait()


def combine_call(
    sent_out, sent_grad, residual, normed, gates, placed, slot_gates, cotangent, gain, w_all, weight
):
    rows, width = residual.shape
    slots = (GROUP, CAP, width)
    return pl.pallas_call(
        combine_kernel,
        out_shape=(
            shape((rows, width), bf16),
            shape((rows, width), f32),
            shape((GROUP, rows, 2 * QW), bf16),
            shape((width, LANES), f32),
            shape((1, width), f32),
        ),
        in_specs=[IN_ANY] * 2 + [IN_VMEM] * 9,
        out_specs=(IN_VMEM, IN_VMEM, IN_ANY, IN_VMEM, IN_VMEM),
        scratch_shapes=[
            VMEM(slots, bf16),
            VMEM(slots, bf16),
            VMEM((rows, width), f32),
            VMEM((LANES, rows), f32),
            VMEM((GROUP, rows, 2 * QW), bf16),
            VMEM((rows, width), bf16),
            VMEM((rows, GROUP * QW), bf16),
        ]
        + [DMA((GROUP,))] * 6
        + [DMA((3,))],
        compiler_params=params(4),
        name="combine",
    )(sent_out, sent_grad, residual, normed, gates, placed, slot_gates, cotangent, gain, w_all, weight)


def backward_kernel(
    n_blocks, q_ref, k_ref, v_ref, heads_ref, o_ref, lse_ref, docs_ref, staged_ref, w_all_ref,
    dq_ref, dk_ref, dv_ref, attended_ref, weights_ref,
    kt_ref, docs_col_ref, dqt_ref, delta_ref, a_send, a_recv, w_send, w_recv, local,
):
    T = TOK_DEV
    place = Place()
    me = place.me
    first = place.base
    greet([place.ctx(i) for i in place.near])
    moves = [
        pltpu.make_async_copy(staged_ref, attended_ref.at[me], local.at[0]),
        pltpu.make_async_copy(w_all_ref, weights_ref.at[me], local.at[1]),
    ]
    for move in moves:
        move.start()

    def halves(size):
        return lambda ref, h: ref.at[pl.ds(h * (size // 2), size // 2)]

    spreads = [
        Spread(
            place, staged_ref, lambda owner: attended_ref.at[owner], halves(GROUP), a_send, a_recv
        ),
        Spread(
            place, w_all_ref, lambda owner: weights_ref.at[owner],
            halves(w_all_ref.shape[0]), w_send, w_recv,
        ),
    ]
    for spread in spreads:
        spread.start()
    rows = lax.broadcasted_iota(jnp.int32, (8, QW), 0)
    lanes = lax.broadcasted_iota(jnp.int32, (8, QW), 1)
    pick = (lanes >= rows * HEAD_DIM) & (lanes < rows * HEAD_DIM + HEAD_DIM)
    pick = jnp.where(pick, 1.0, 0.0).astype(bf16)

    def turn(i, _):
        kt_ref[:, block(i)] = k_ref[block(i), :].T
        docs_col_ref[i] = docs_column(docs_ref[i])
        return 0

    lax.fori_loop(0, n_blocks, turn, 0)

    def prepare(i, _):
        product = o_ref[block(i), :] * heads_ref[i, :, :QW].astype(f32)
        high = product.astype(bf16)
        low = (product - high.astype(f32)).astype(bf16)
        delta_ref[i] = dot(pick, high, ((1,), (1,))) + dot(pick, low, ((1,), (1,)))
        return 0

    lax.fori_loop(0, GROUP, prepare, 0)
    dqt_ref[...] = jnp.zeros_like(dqt_ref)

    def tile(kb, qb, mask):
        kt = k_ref[block(kb), :]
        vt = v_ref[block(kb), :]
        k_turned = kt_ref[:, block(kb)]
        heads = range(HEADS)
        parts = [slice(h * 64, (h + 1) * 64) for h in heads]
        q = [q_ref[block(qb), part] for part in parts]
        do = [heads_ref[qb, :, part] for part in parts]
        s = [dot(kt, x, ((1,), (1,))) for x in q]
        dp = [dot(vt, x, ((1,), (1,))) for x in do]
        p = [jnp.exp(s[h] - lse_ref[qb, h : h + 1, :]) for h in heads]
        if mask is not None:
            p = [jnp.where(mask, x, 0.0) for x in p]
        ds = [(p[h] * (dp[h] - delta_ref[qb, h : h + 1, :])).astype(bf16) for h in heads]
        pb = [x.astype(bf16) for x in p]
        dv_ref[block(kb), :] += dot(pb[0], do[0]) + dot(pb[1], do[1]) + dot(pb[2], do[2])
        dk_ref[block(kb), :] += dot(ds[0], q[0]) + dot(ds[1], q[1]) + dot(ds[2], q[2])
        for h in heads:
            dqt_ref[parts[h], block(qb)] += dot(k_turned, ds[h])

    def same(kb, gq):
        return docs_col_ref[kb] == docs_ref[gq].astype(f32)

    def k_block(kb, _):
        for at, act in (
            (1, spreads[0].step1), (2, spreads[0].step2), (3, spreads[0].step3),
            (4, spreads[1].step1), (5, spreads[1].step2), (6, spreads[1].step3),
        ):
            pl.when(kb == first + at)(act)
        dk_ref[block(kb), :] = jnp.zeros((T, HEAD_DIM), f32)
        dv_ref[block(kb), :] = jnp.zeros((T, HEAD_DIM), f32)

        @pl.when(kb >= first)
        def _():
            keys = lax.broadcasted_iota(jnp.int32, (T, T), 0)
            queries = lax.broadcasted_iota(jnp.int32, (T, T), 1)
            tile(kb, kb - first, same(kb, kb) & (keys <= queries))

        def q_block(qb, _):
            gq = first + qb
            edge = jnp.logical_or(kb == 0, gq == n_blocks - 1)

            @pl.when(edge)
            def _():
                tile(kb, qb, same(kb, gq))

            @pl.when(jnp.logical_not(edge))
            def _():
                tile(kb, qb, None)

            return 0

        lax.fori_loop(jnp.maximum(kb - first + 1, 0), GROUP, q_block, 0)
        return 0

    lax.fori_loop(0, first + GROUP, k_block, 0)

    def finish(i, _):
        dq_ref[block(i), :] = dqt_ref[:, block(i)].T
        return 0

    lax.fori_loop(0, GROUP, finish, 0)

    def clear(kb, _):
        dk_ref[block(kb), :] = jnp.zeros((T, HEAD_DIM), f32)
        dv_ref[block(kb), :] = jnp.zeros((T, HEAD_DIM), f32)
        return 0

    lax.fori_loop(first + GROUP, n_blocks, clear, 0)
    for spread in spreads:
        spread.last()
        spread.sent()
    for move in moves:
        move.wait()


def backward_call(q, k, v, heads, o, lse, docs, staged, w_all):
    n = k.shape[0] // TOK_DEV
    span = q.shape[0]
    return pl.pallas_call(
        functools.partial(backward_kernel, n),
        out_shape=(
            shape((span, QW), f32),
            shape(k.shape, f32),
            shape(k.shape, f32),
            shape((GROUP,) + staged.shape, bf16),
            shape((GROUP,) + w_all.shape, bf16),
        ),
        in_specs=[IN_VMEM] * 7 + [IN_ANY] * 2,
        out_specs=(IN_VMEM,) * 3 + (IN_ANY,) * 2,
        scratch_shapes=[
            VMEM((64, n * TOK_DEV), bf16),
            VMEM((n, TOK_DEV, 1), f32),
            VMEM((QW, span), f32),
            VMEM((GROUP, 8, TOK_DEV), f32),
        ]
        + [DMA((Spread.SEMS,))] * 4
        + [DMA((2,))],
        compiler_params=params(5),
        name="backward",
    )(q, k, v, heads, o, lse, docs, staged, w_all)


def finish_kernel(
    dq_ref, dk_ref, dv_ref, cos_ref, sin_ref, normed_ref, attended_ref, heads_ref, weights_ref,
    tokens_ref, gain_ref, grad_residual_ref, grad_router_ref, grad_gain2_ref,
    input_grad_ref, grads_ref,
    linear_ref, came_ref, columns_ref, sum_ref, gains_ref, g_send, g_recv,
):
    place = Place()
    me = place.me
    greet(place.others())
    rows, width = tokens_ref.shape
    span = GROUP * rows

    def copy(j):
        to = lax.rem(me + j, GROUP)
        return remote(
            linear_ref.at[to], came_ref.at[me], g_send.at[j], g_recv.at[j], place.ctx(to)
        )

    def turn_back(j, _):
        to = lax.rem(me + j, GROUP)
        cosine, sine = cos_ref[block(to), :], -sin_ref[block(to), :]
        dq = dq_ref[block(to), :] * HEAD_DIM ** (-0.5)
        second = jnp.concatenate([dq[:, LANES:], dk_ref[block(to), :]], axis=1)
        third = jnp.concatenate([dv_ref[block(to), :], jnp.zeros((rows, HEAD_DIM), f32)], axis=1)
        linear_ref[to, :, :LANES] = turned(dq[:, :LANES], cosine, sine).astype(bf16)
        linear_ref[to, :, LANES : 2 * LANES] = turned(second, cosine, sine).astype(bf16)
        linear_ref[to, :, 2 * LANES :] = third.astype(bf16)

        @pl.when(j < GROUP)
        def _():
            copy(j).start()

        return 0

    lax.fori_loop(1, GROUP + 1, turn_back, 0)
    came_ref[me] = linear_ref[me]
    columns_ref[...] = heads_ref[:, :, QW:].reshape(span, QW)

    def own_weights(i, _):
        left = normed_ref[:, :, block(i)].reshape(span, TOK_DEV)
        grads_ref[block(i), : 3 * LANES] = dot(
            left, linear_ref[...].reshape(span, WIDE), ((0,), (0,))
        ).astype(bf16)
        return 0

    lax.fori_loop(0, width // TOK_DEV, own_weights, 0)

    def out_weights(j, _):
        left = attended_ref[j].reshape(span, QW)
        grads_ref[block(j, QW), 3 * LANES :] = dot(left, columns_ref[...], ((0,), (0,))).astype(bf16)
        return 0

    lax.fori_loop(0, GROUP, out_weights, 0)
    sum_ref[...] = jnp.zeros_like(sum_ref)
    for j in range(1, GROUP):
        copy(j).wait_recv()

    def add_head(j, _):
        sum_ref[...] += dot(came_ref[j], weights_ref[j].reshape(width, WIDE), ((1,), (1,)))
        return 0

    lax.fori_loop(0, GROUP, add_head, 0)
    x = tokens_ref[...].astype(f32)
    grad_normed = sum_ref[...]
    scale = lax.rsqrt(jnp.mean(x * x, axis=-1, keepdims=True) + epsilon)
    scaled = grad_normed * gain_ref[...]
    inner = jnp.mean(scaled * x, axis=-1, keepdims=True)
    grad = scale * scaled - x * (scale * scale * scale * inner)
    input_grad_ref[...] = grad_residual_ref[...] + grad
    gains_ref[...] = jnp.zeros_like(gains_ref)
    at = ROUTER + EXPERTS_MOST
    gains_ref[at : at + 1, :] = jnp.sum(grad_normed * x * scale, axis=0, keepdims=True)
    gains_ref[at + 1 : at + 2, :] = grad_gain2_ref[...]
    extra = grad_router_ref[...] + gains_ref[...].T
    lane = lax.broadcasted_iota(jnp.int32, extra.shape, 1)
    last = slice(2 * LANES, 3 * LANES)
    grads_ref[:, last] = jnp.where(lane < ROUTER, grads_ref[:, last].astype(f32), extra).astype(bf16)
    for j in range(1, GROUP):
        copy(j).wait_send()


def finish_call(
    dq, dk, dv, cosine, sine, normed, attended, heads, weights, tokens, gain, grad_residual,
    grad_router, grad_gain2,
):
    rows, width = tokens.shape
    return pl.pallas_call(
        finish_kernel,
        out_shape=(shape((rows, width), f32), shape((width, WIDE + QW), bf16)),
        in_specs=[IN_VMEM] * 14,
        out_specs=(IN_VMEM,) * 2,
        scratch_shapes=[
            VMEM((GROUP, rows, WIDE), bf16),
            VMEM((GROUP, rows, WIDE), bf16),
            VMEM((GROUP * rows, QW), bf16),
            VMEM((rows, width), f32),
            VMEM((LANES, width), f32),
            DMA((GROUP,)),
            DMA((GROUP,)),
        ],
        compiler_params=params(6),
        name="finish",
    )(
        dq, dk, dv, cosine, sine, normed, attended, heads, weights, tokens, gain, grad_residual,
        grad_router, grad_gain2,
    )


def share_kernel(count, *refs):
    sources, outs, sems = refs[:count], refs[count : 2 * count], refs[2 * count :]
    place = Place()
    greet([place.ctx(i) for i in place.near])
    spreads, moves = [], []
    for i in range(count):
        size = sources[i].shape[0] // 2
        spreads.append(
            Spread(
                place, sources[i], lambda owner, out=outs[i]: out.at[owner],
                lambda ref, h, size=size: ref.at[pl.ds(h * size, size)],
                sems[2 * i], sems[2 * i + 1],
            )
        )
        moves.append(
            pltpu.make_async_copy(sources[i], outs[i].at[place.me], sems[2 * count].at[i])
        )
        spreads[i].start()
        moves[i].start()
    for spread in spreads:
        spread.step1()
    for spread in spreads:
        spread.step2()
    for spread in spreads:
        spread.step3()
    for spread in spreads:
        spread.last()
        spread.sent()
    for move in moves:
        move.wait()


def share_call(collective_id, *values):
    count = len(values)
    return pl.pallas_call(
        functools.partial(share_kernel, count),
        out_shape=tuple(shape((GROUP,) + v.shape, v.dtype) for v in values),
        in_specs=[IN_ANY] * count,
        out_specs=(IN_ANY,) * count,
        scratch_shapes=[DMA((Spread.SEMS,))] * (2 * count) + [DMA((count,))],
        compiler_params=params(collective_id),
        name="share",
    )(*values)


def rotary_tables(length):
    frequencies = 10000.0 ** (-(np.arange(HEAD_DIM // 2) * 2.0) / HEAD_DIM)
    angles = np.arange(length)[:, None] * frequencies[None, :]
    repeat = LANES // (HEAD_DIM // 2)
    return (
        np.tile(np.cos(angles), (1, repeat)).astype(np.float32),
        np.tile(np.sin(angles), (1, repeat)).astype(np.float32),
    )


def shards(
    tables,
    tokens,
    doc_ids,
    routes,
    slot_order,
    norm1_gain,
    norm2_gain,
    w_query,
    key_matrix,
    value_matrix,
    w_out,
    w_router,
    w_gate,
    w_up,
    w_down,
    cotangent,
):
    rows, width = tokens.shape[1:]
    ctx, depth = lax.axis_size("ctx"), lax.axis_size("fsdp")
    place = lax.axis_index("ctx")
    parts = ctx // GROUP
    head, part = place % GROUP, place // GROUP
    far = [[p * GROUP + i for p in range(parts)] for i in range(GROUP)]
    span = GROUP * rows
    experts = w_router.shape[1]
    hidden = w_gate.shape[2]

    def gather_z(value):
        return lax.all_gather(value, "fsdp", axis=0, tiled=True)

    def reduce_z(value):
        value = lax.psum_scatter(value.astype(bf16), "fsdp", scatter_dimension=0, tiled=True)
        if parts > 1:
            value = lax.psum(value, "ctx", axis_index_groups=far)
        return value

    def own(weight, size):
        return lax.dynamic_slice_in_dim(weight, head * size, size, 1)

    w_h = jnp.concatenate(
        [
            own(w_query, QW), own(key_matrix, HEAD_DIM), own(value_matrix, HEAD_DIM),
            jnp.pad(w_router, ((0, 0), (0, HEAD_DIM - experts))),
        ],
        axis=1,
    )
    gate_up = gather_z(
        jnp.concatenate(
            [
                lax.dynamic_index_in_dim(w_gate, head, 0, False),
                lax.dynamic_index_in_dim(w_up, head, 0, False),
            ],
            axis=1,
        )
    )
    down = gather_z(lax.dynamic_index_in_dim(w_down, head, 0, False))
    cosine, sine = tables
    if parts > 1:
        cosine = lax.dynamic_slice_in_dim(cosine, part * span, span, 0)
        sine = lax.dynamic_slice_in_dim(sine, part * span, span, 0)
    own_tokens, own_cotangent = tokens[0], cotangent[0]
    gain1, gain2 = norm1_gain[None, :], norm2_gain[None, :]

    normed1, w_all, strips, queries, keys, values, docs = project_call(
        own_tokens, gain1, w_h, w_out, cosine, sine, doc_ids, depth
    )
    if parts > 1:
        keys = lax.all_gather(keys, "ctx", axis_index_groups=far, tiled=True)
        values = lax.all_gather(values, "ctx", axis_index_groups=far, tiled=True)
        docs = lax.all_gather(docs, "ctx", axis_index_groups=far, tiled=True)
    attended_f32, log_total, attended, out_weight, staged = attend_call(
        queries, keys, values, docs, strips
    )
    out_weight = out_weight.reshape(width, width)
    residual, normed2, gates, placed, slot_gates, sent_rows, sent_grads = dispatch_call(
        attended, out_weight, own_tokens, gain2, w_all, routes[0], slot_order[0], own_cotangent
    )
    buffer_rows = sent_rows.reshape(GROUP * CAP, width)
    grad_rows = sent_grads.reshape(GROUP * CAP, width)

    gate_up_in = dot(buffer_rows, gate_up)
    gate_in, up_in = gate_up_in[:, :hidden], gate_up_in[:, hidden:]
    sigmoid_gate = jax.nn.sigmoid(gate_in)
    activation = (gate_in * sigmoid_gate * up_in).astype(bf16)
    expert_out = dot(activation, down).astype(bf16)
    grad_activation = dot(grad_rows, down, ((1,), (1,)))
    grad_gate_in = grad_activation * up_in * sigmoid_gate * (1.0 + gate_in * (1.0 - sigmoid_gate))
    grad_up_in = grad_activation * gate_in * sigmoid_gate
    grad_gate_up = jnp.concatenate([grad_gate_in, grad_up_in], axis=1).astype(bf16)
    grad_buffer = dot(grad_gate_up, gate_up, ((1,), (1,))).astype(bf16)
    grad_w_down = reduce_z(dot(activation, grad_rows, ((0,), (0,))))
    grad_w_gate_up = reduce_z(dot(buffer_rows, grad_gate_up, ((0,), (0,))))

    output, grad_residual, heads, grad_router, grad_gain2 = combine_call(
        expert_out.reshape(sent_rows.shape), grad_buffer.reshape(sent_rows.shape), residual,
        normed2, gates, placed, slot_gates, own_cotangent, gain2, w_all, out_weight,
    )
    dq, dk, dv, attended_all, weights_all = backward_call(
        queries, keys, values, heads, attended_f32, log_total, docs, staged, w_all
    )
    if parts > 1:
        dk = lax.psum_scatter(dk, "ctx", axis_index_groups=far, tiled=True)
        dv = lax.psum_scatter(dv, "ctx", axis_index_groups=far, tiled=True)
    input_grad, grads = finish_call(
        dq, dk, dv, cosine, sine, normed1, attended_all, heads, weights_all, own_tokens, gain1,
        grad_residual, grad_router, grad_gain2,
    )
    gate_up_w, down_w = share_call(7, grad_w_gate_up, grad_w_down)
    (shared,) = share_call(8, reduce_z(grads))
    shared = shared.astype(f32)

    def columns(value):
        return jnp.transpose(value, (1, 0, 2)).reshape(value.shape[1], -1)

    small = jnp.sum(shared[:, :, HW : HW + experts + 2], axis=0)
    gate_up_w = gate_up_w.astype(f32)
    return (
        output[None],
        input_grad[None],
        small[:, experts],
        small[:, experts + 1],
        columns(shared[:, :, :QW]),
        columns(shared[:, :, QW : QW + HEAD_DIM]),
        columns(shared[:, :, QW + HEAD_DIM : HW]),
        columns(shared[:, :, WIDE:]),
        small[:, :experts],
        gate_up_w[:, :, :hidden],
        gate_up_w[:, :, hidden:],
        down_w.astype(f32),
    )


def solution(mesh):
    token_spec = P("fsdp", "ctx", None)
    row_spec, expert_spec = P("fsdp", None), P(None, "fsdp", None)
    tables = rotary_tables(mesh.shape["ctx"] * TOK_DEV)

    def program(*arguments):
        return jax.shard_map(
            functools.partial(shards, tuple(jnp.asarray(t) for t in tables)),
            mesh=mesh,
            in_specs=(
                token_spec,
                P("fsdp", "ctx"),
                token_spec,
                token_spec,
                P(),
                P(),
                row_spec,
                row_spec,
                row_spec,
                row_spec,
                row_spec,
                expert_spec,
                expert_spec,
                expert_spec,
                token_spec,
            ),
            out_specs=(
                token_spec,
                token_spec,
                P("fsdp"),
                P("fsdp"),
                row_spec,
                row_spec,
                row_spec,
                row_spec,
                row_spec,
                expert_spec,
                expert_spec,
                expert_spec,
            ),
            check_vma=False,
        )(*arguments)

    return program
```

profile of v0, /device:TPU:0, one launch (start us, length us, event | category | flops | bytes accessed | tf_op | source)
XLA Modules:
  0.0 620.6 jit_solution(17049083407684840373)
XLA Ops:
  16.6 86.7 %project.1 = (bf16[8,256,1536]{2,1,0:T(8,128)(2,1)}, bf16[4,384,384]{2,1,0:T(8,128)(2,1)}, bf16[4,48,1536]{2,1,0:T(8,128)(2,1)}, bf16[2048,192]{1,0:T(8,128)(2,1...) custom-call(bf16[256,1536]{1,0:T(8,128)(2,1)} %bitcast.47, ...), custom_call_target="tpu_custom_call" | custom-call | tf_op jit(solution)/shard_map/project/pallas_call | solution.py:275
  103.3 46.0 %attend.1 = (f32[2048,192]{1,0:T(8,128)}, f32[8,8,256]{2,1,0:T(8,128)}, bf16[8,256,192]{2,1,0:T(8,128)(2,1)}, bf16[4,8,48,1536]{3,2,1,0:T(8,128)(2,1)}, bf16[8,256,192]{2,1,0:T(8,128)(2,1)}) custom-call(bf16[2048,192]{1,0:T(8,128)(2,1)} %get-tuple-element.45.q_ref, bf16[2048,64]{1,0:T(8,128)(2,1)} %get-tuple-element.46.k_ref, ...), custom_call_target="tpu_custom_call" | custom-call | tf_op jit(solution)/shard_map/attend/pallas_call | solution.py:418
  149.3 47.8 %dispatch.1 = (f32[256,1536]{1,0:T(8,128)}, bf16[256,1536]{1,0:T(8,128)(2,1)}, f32[256,128]{1,0:T(8,128)}, bf16[8,64,256]{2,1,0:T(8,128)(2,1)}, f32[8,64,1]{2,1,...) custom-call(bf16[8,256,192]{2,1,0:T(8,128)(2,1)} %get-tuple-element.50.attended_ref, ...), custom_call_target="tpu_custom_call" | custom-call | tf_op jit(solution)/shard_map/dispatch/pallas_call | solution.py:546
  197.1 5.6 fusion.8
  202.7 3.5 multiply_convert_fusion.1
  209.3 3.0 convolution_convert_fusion.3
  212.2 65.5 %combine.1 = (bf16[256,1536]{1,0:T(8,128)(2,1)}, f32[256,1536]{1,0:T(8,128)}, bf16[8,256,384]{2,1,0:T(8,128)(2,1)}, f32[1536,128]{1,0:T(8,128)}, f32[1,1536]{1,0:T(1,128)}) custom-call(bf16[8,64,1536]{2,1,0:T(8,128)(2,1)} %bitcast.55, bf16[8,64,1536]{2,1,0:T(8,128)(2,1)} %bitcast.56, f32[256,1536]{1,0:T(8,128)} %get-tuple-element.55.residual_ref, ...), custom_call_target="tpu_custom_call" | custom-call | tf_op jit(solution)/shard_map/combine/pallas_call | solution.py:673
  277.7 90.7 %backward.1 = (f32[2048,192]{1,0:T(8,128)}, f32[2048,64]{1,0:T(8,128)}, f32[2048,64]{1,0:T(8,128)}, bf16[8,8,256,192]{3,2,1,0:T(8,128)(2,1)}, bf16[8,4,384,384]{3,2,1,0:T(8,128)(2,1)}) custom-call(bf16[2048,192]{1,0:T(8,128)(2,1)} %get-tuple-element.45.q_ref, bf16[2048,64]{1,0:T(8,128)(2,1)} %get-tuple-element.46.k_ref, ...), custom_call_target="tpu_custom_call" | custom-call | tf_op jit(solution)/shard_map/backward/pallas_call | solution.py:832
  368.5 36.1 %finish.1 = (f32[256,1536]{1,0:T(8,128)}, bf16[1536,576]{1,0:T(8,128)(2,1)}) custom-call(f32[2048,192]{1,0:T(8,128)} %get-tuple-element.65.dq_ref, f32[2048,64]{1,0:T(8,128)} %get-tuple-element.66.dk_ref, f32[2048,64]{1,0:T(8,128)} %get-tuple-element.67.dv_ref, f32[2048,128]{1,0:T(8,128)} %constant.48.clone.cos_ref, f32[2048,128]{1,0:T(8,128)} %constant.49.clone.sin_ref, ...), custom_call_target="tpu_custom_call" | custom-call | tf_op jit(solution)/shard_map/finish/pallas_call | solution.py:942
  404.7 3.3 convolution_convert_fusion.1
  408.1 4.7 convolution_convert_fusion
  412.8 42.5 %reduce-scatter.4.cloned.1.call-done.refs_0_ = bf16[384,576]{1,0:T(8,128)(2,1)} async-done(((bf16[1536,576]{1,0:T(8,128)(2,1)}), bf16[384,576]{1,0:T(8,128)(2,1)}) %reduce-scatter.4.cloned.1.call-update) | async-done | bytes 442384 | tf_op jit(solution)/shard_map/reduce_scatter | solution.py:1051
  455.3 21.4 %share.2 = bf16[8,384,576]{2,1,0:T(8,128)(2,1)} custom-call(bf16[384,576]{1,0:T(8,128)(2,1)} %reduce-scatter.4.cloned.1.call-done.refs_0_), custom_call_target="tpu_custom_call" | custom-call | tf_op jit(solution)/shard_map/share/pallas_call | solution.py:998
  479.4 2.8 slice_bitcast_fusion
  483.5 3.3 copy.66
  486.9 3.0 copy.70
  489.9 4.1 slice_bitcast_fusion.2
  494.0 2.7 copy.67
  499.0 2.9 copy.68
  506.4 3.0 copy.73
  512.9 41.6 %reduce-scatter.6.cloned.1.call-done.refs_0_ = bf16[384,1024]{1,0:T(8,128)(2,1)} async-done(((bf16[1536,1024]{1,0:T(8,128)(2,1)}), bf16[384,1024]{1,0:T(8,128)(2,1)}) %reduce-scatter.6.cloned.1.call-update) | async-done | bytes 786448 | tf_op jit(solution)/shard_map/reduce_scatter | solution.py:1051
  554.6 43.6 %share.3 = (bf16[8,384,1024]{2,1,0:T(8,128)(2,1)}, bf16[8,128,1536]{2,1,0:T(8,128)(2,1)}) custom-call(bf16[384,1024]{1,0:T(8,128)(2,1)} %reduce-scatter.6.cloned.1.call-done.refs_0_, bf16[128,1536]{1,0:T(8,128)(2,1)} %reduce-scatter.8.cloned.1.call-done.refs_1_), custom_call_target="tpu_custom_call" | custom-call | tf_op jit(solution)/shard_map/share/pallas_call | solution.py:998
  598.2 9.5 %fusion.7 = (f32[8,384,512]{2,1,0:T(8,128)}, f32[8,384,512]{2,1,0:T(8,128)}) fusion(bf16[8,384,1024]{2,1,0:T(8,128)(2,1)} %get-tuple-element.76), kind=kLoop, calls=%fused_computation.31 | loop fusion | bytes 25165824 | tf_op jit(solution)/shard_map/slice | solution.py:1147
  607.7 3.6 convert_element_type.34
  (72 shorter events, 29.5 us)
Async XLA Ops:
  7.2 2.5 copy-start
  7.2 189.9 %all-gather.4.cloned.1.call-start = ((), (), s32[]{:S(2)}) async-start(), calls=%async_computation.3 | async-start | bytes 3932160 | tf_op jit(solution)/shard_map/all_gather | solution.py:1048
  8.6 2.0 copy-start.9
  8.6 2.6 copy-start.6
  8.6 2.7 copy-start.10
  8.6 3.3 copy-start.7
  8.6 4.1 copy-start.8
  9.7 193.1 %all-gather.6.cloned.1.call-start = ((), (), s32[]{:S(2)}) async-start(), calls=%async_computation.7 | async-start | bytes 1966080 | tf_op jit(solution)/shard_map/all_gather | solution.py:1048
  10.5 444.8 %reduce-scatter.4.cloned.1.call-start = ((), (), s32[]{:S(2)}) async-start(), calls=%async_computation.4 | async-start | bytes 2457600 | tf_op jit(solution)/shard_map/reduce_scatter | solution.py:1051
  197.1 5.6 copy-start.14
  202.7 3.5 copy-start.13
  206.2 2.2 copy-start.16
  206.2 2.2 copy-start.17
  206.2 2.2 copy-start.18
  206.3 3.0 copy-start.11
  368.4 36.3 %copy-start.15 = (bf16[8,64,1536]{2,1,0:T(8,128)(2,1)S(1)}, bf16[8,64,1536]{2,1,0:T(8,128)(2,1)}, u32[]{:S(2)}) copy-start(bf16[8,64,1536]{2,1,0:T(8,128)(2,1)} %get-tuple-element.54) | copy-start | bytes 4718596
  404.6 3.4 copy-start.12
  404.6 108.3 %reduce-scatter.8.cloned.1.call-start = ((), (), s32[]{:S(2)}) async-start(), calls=%async_computation.6 | async-start | bytes 1966080 | tf_op jit(solution)/shard_map/reduce_scatter | solution.py:1051
  408.0 146.5 %reduce-scatter.6.cloned.1.call-start = ((), (), s32[]{:S(2)}) async-start(), calls=%async_computation.5 | async-start | bytes 3932160 | tf_op jit(solution)/shard_map/reduce_scatter | solution.py:1051
  479.4 4.1 copy-start.2
  598.2 9.5 %copy-start.3 = (bf16[8,128,1536]{2,1,0:T(8,128)(2,1)S(1)}, bf16[8,128,1536]{2,1,0:T(8,128)(2,1)}, u32[]{:S(2)}) copy-start(bf16[8,128,1536]{2,1,0:T(8,128)(2,1)} %get-tuple-element.77) | copy-start | bytes 9437188
  607.7 3.6 copy-start.5
  611.3 1.7 copy-start.4
  611.3 2.8 copy-start.1
Sparse Core Ops, SparseCore 0:
  10.2 103.6 all-gather.3
  116.0 35.6 all-gather.5
  404.8 50.4 reduce-scatter.3
  458.0 34.5 reduce-scatter.7
  495.3 59.2 reduce-scatter.5
where the time goes:
time: 621 us
  Pallas kernels  438 us (71%)
  waiting for transfers between devices  84.2 us (14%)
  local copies, waits for them, and re-layouts  52.1 us (8%)
  matrix products  22.2 us (4%)
  between operations  14.1 us (2%)
  other arithmetic  9.99 us (2%)
    pallas_call x1, Pallas kernels, backward_call(): pl.pallas_call(functools.partial(backward_kernel, n), out_shape=(shape((s...  90.7 us
    pallas_call x1, Pallas kernels, project_call(): pl.pallas_call(project_kernel, out_shape=(shape((GROUP, rows, width), bf1...  86.7 us
    reduce_scatter x3, waiting for transfers between devices, reduce_z(): lax.psum_scatter(value.astype(bf16), 'fsdp', scatter_dimension=0, tiled=T...  84.1 us
    pallas_call x1, Pallas kernels, combine_call(): pl.pallas_call(combine_kernel, out_shape=(shape((rows, width), bf16), sha...  65.5 us
    pallas_call x2, Pallas kernels, share_call(): pl.pallas_call(functools.partial(share_kernel, count), out_shape=tuple((s...  65 us
    pallas_call x1, Pallas kernels, dispatch_call(): pl.pallas_call(dispatch_kernel, out_shape=(shape((rows, width), f32), sha...  47.8 us
    pallas_call x1, Pallas kernels, attend_call(): pl.pallas_call(functools.partial(attend_kernel, n), out_shape=(shape((spa...  46 us
    pallas_call x1, Pallas kernels, finish_call(): pl.pallas_call(finish_kernel, out_shape=(shape((rows, width), f32), shape...  36.1 us
  transfers between devices with their start and end apart: 5, of which 2 were waited for; matrix products, arithmetic and copies ran while one was open for 9% of the time, Pallas kernels for 33%

commit v1 on v0

v1 whole, which is shorter than its diff:
```python
import functools

import jax
import jax.numpy as jnp
import numpy as np
from jax import lax
from jax.experimental import pallas as pl
from jax.experimental.pallas import tpu as pltpu
from jax.sharding import PartitionSpec as P

QUERY_HEADS = 24
KEY_VALUE_HEADS = 8
HEAD_DIM = 64
TOPK = 8
EXP_WIN = 8
TOK_DEV = 256
CAP = 64
GROUP = 8
HEADS = QUERY_HEADS // KEY_VALUE_HEADS
QW = HEADS * HEAD_DIM
HW = QW + 2 * HEAD_DIM
ROUTER = 48
ALL = HW + ROUTER
FIRST = 96

epsilon = 1e-06
score_masked = -1e30
bf16 = jnp.bfloat16
f32 = jnp.float32
VMEM = pltpu.VMEM
MESH = pl.DeviceIdType.MESH
DMA = pltpu.SemaphoreType.DMA
IN_VMEM = pl.BlockSpec(memory_space=VMEM)
IN_ANY = pl.BlockSpec(memory_space=pl.ANY)


def dot(left, right, dims=((1,), (0,))):
    return lax.dot_general(left, right, (dims, ((), ())), preferred_element_type=f32)


def block(index, size=TOK_DEV):
    return pl.ds(pl.multiple_of(index * size, size), size)


def shape(dims, dtype):
    return jax.ShapeDtypeStruct(dims, dtype)


def params(collective_id=None, limit=56):
    return pltpu.CompilerParams(
        collective_id=collective_id,
        has_side_effects=collective_id is not None,
        vmem_limit_bytes=limit << 20,
    )


def flip(index, bit):
    return index + (1 - 2 * ((index // bit) % 2)) * bit


class Place:
    def __init__(self):
        ctx = lax.axis_index("ctx")
        self.base = (ctx // GROUP) * GROUP
        self.me = ctx - self.base
        self.z = lax.axis_index("fsdp")
        self.depth = lax.axis_size("fsdp")
        self.near = [flip(self.me, bit) for bit in (1, 2, 4)]

    def ctx(self, index):
        return {"ctx": self.base + index}

    def fsdp(self, index):
        return {"fsdp": index}

    def others(self):
        return [self.ctx(lax.rem(self.me + j, GROUP)) for j in range(1, GROUP)]

    def layers(self):
        return [self.fsdp(lax.rem(self.z + j, self.depth)) for j in range(1, self.depth)]


def greet(devices):
    ready = pltpu.get_barrier_semaphore()
    for device in devices:
        pl.semaphore_signal(ready, inc=1, device_id=device, device_id_type=MESH)
    return lambda: pl.semaphore_wait(ready, len(devices))


def remote(source, target, send, receive, device):
    return pltpu.make_async_remote_copy(
        src_ref=source,
        dst_ref=target,
        send_sem=send,
        recv_sem=receive,
        device_id=device,
        device_id_type=MESH,
    )


def halves(count):
    cut = -(-count // 32) * 16

    def part(ref, half):
        return ref.at[pl.ds(0, cut)] if half == 0 else ref.at[pl.ds(cut, count - cut)]

    return part


class Spread:
    SEMS = 14

    def __init__(self, place, source, land, part, send, receive):
        me = place.me
        core, side, row = place.near
        across = flip(side, 4)

        def plan(slot, owner, half, device):
            target = part(land(owner), half)
            first = part(source, half) if slot < 6 else target
            return remote(first, target, send.at[slot], receive.at[slot], place.ctx(device))

        self.copies = [
            plan(0, me, 0, side), plan(1, me, 1, side), plan(2, me, 0, row), plan(3, me, 1, row),
            plan(4, me, 0, core), plan(5, me, 1, core), plan(6, side, 0, core),
            plan(7, side, 1, core), plan(8, row, 0, core), plan(9, row, 1, core),
            plan(10, side, 1, row), plan(11, row, 0, side), plan(12, across, 0, core),
            plan(13, across, 1, core),
        ]

    def go(self, *slots):
        for slot in slots:
            self.copies[slot].start()

    def wait(self, *slots):
        for slot in slots:
            self.copies[slot].wait_recv()

    def start(self):
        self.go(1, 2, 0, 3, 4, 5)

    def step1(self):
        self.wait(1)
        self.go(10, 7)
        self.wait(2)
        self.go(11, 8)

    def step2(self):
        self.wait(0)
        self.go(6)
        self.wait(3)
        self.go(9)

    def step3(self):
        self.wait(10)
        self.go(13)
        self.wait(11)
        self.go(12)

    def sent(self):
        for copy in self.copies:
            copy.wait_send()

    def last(self):
        self.wait(4, 5, 6, 7, 8, 9, 12, 13)


NEVER = 4096.0


def turned(values, cosine, sine):
    half = HEAD_DIM // 2
    out = []
    for at in range(0, values.shape[0], HEAD_DIM):
        low, high = values[at : at + half], values[at + half : at + HEAD_DIM]
        out += [low * cosine - high * sine, high * cosine + low * sine]
    return jnp.concatenate(out, axis=0)


def place_slots(routes_ref, order_ref, placed_ref):
    rows = routes_ref.shape[1]
    expert = lax.broadcasted_iota(jnp.int32, (EXP_WIN, rows), 0)
    priority = jnp.full((EXP_WIN, rows), NEVER, f32)
    for k in range(TOPK):
        pick = expert == routes_ref[k : k + 1, :]
        priority = jnp.where(pick, order_ref[k : k + 1, :].astype(f32), priority)
    priority_turned = priority.T
    slot = lax.broadcasted_iota(jnp.int32, (CAP, rows), 0).astype(f32)
    for e in range(EXP_WIN):
        mine = priority[e : e + 1, :]
        before = jnp.where(priority_turned[:, e : e + 1] < mine, 1.0, 0.0)
        before = jnp.sum(before, axis=0, keepdims=True)
        placed = (slot == before) & (mine < NEVER)
        placed_ref[e] = jnp.where(placed, 1.0, 0.0).astype(bf16)


def project_kernel(
    tokens_ref, gain_ref, router_ref, cos_ref, sin_ref, docs_ref, routes_ref, order_ref, w_out_ref,
    w_query_ref, key_matrix_ref, value_matrix_ref,
    w_all_ref, qt_ref, kt_ref, vt_ref, k_ref, v_ref, docs_all_ref, placed_ref, turned_ref, normed_ref,
    strips_ref, weights_ref,
    held_ref, own_out, query_held, key_held, value_held,
    w_send, w_recv, o_send, o_recv, d_send, d_recv, c_send, c_recv, q_send, q_recv, local,
):
    place = Place()
    me, z = place.me, place.z
    met = greet(place.others() + place.layers())
    strip = strips_ref.shape[1]
    odd = lax.rem(me, 2)

    def window(first, size):
        return pl.ds(pl.multiple_of(first * 128, 128), size)

    pair = lax.div(me, 2)
    fetches = [
        pltpu.make_async_copy(
            w_query_ref.at[:, window(pair * 3 + odd, 2 * 128)], query_held, local.at[GROUP]
        ),
        pltpu.make_async_copy(
            key_matrix_ref.at[:, window(pair, 128)], key_held, local.at[GROUP + 1]
        ),
        pltpu.make_async_copy(
            value_matrix_ref.at[:, window(pair, 128)], value_held, local.at[GROUP + 2]
        ),
        pltpu.make_async_copy(
            w_out_ref.at[pl.ds(pl.multiple_of(me * strip, strip), strip), :], own_out,
            local.at[GROUP + 3],
        ),
    ]
    for fetch in fetches:
        fetch.start()
    x = tokens_ref[...].astype(f32)
    scale = lax.rsqrt(jnp.mean(x * x, axis=-1, keepdims=True) + epsilon)
    held_ref[me] = (x * scale * gain_ref[...]).astype(bf16)
    for fetch in fetches:
        fetch.wait()

    def half(held, columns):
        turned_rows = held[...].T
        return jnp.where(odd == 1, turned_rows[HEAD_DIM:], turned_rows[:columns])

    own = w_all_ref.at[z]
    own[:QW, :] = half(query_held, QW)
    own[QW : QW + HEAD_DIM, :] = half(key_held, HEAD_DIM)
    own[QW + HEAD_DIM : HW, :] = half(value_held, HEAD_DIM)
    own[HW:, :] = router_ref[...]
    met()
    spread = Spread(
        place, held_ref.at[me], lambda owner: held_ref.at[owner],
        halves(TOK_DEV), c_send, c_recv,
    )
    sent = []
    for j, device in enumerate(place.layers()):
        sent.append(remote(own, own, w_send.at[j], w_recv.at[j], device))
        sent[-1].start()
    spread.start()
    docs_all_ref[me] = docs_ref[...]
    others = []
    for j, device in enumerate(place.others()):
        others.append(remote(docs_ref, docs_all_ref.at[me], d_send.at[j], d_recv.at[j], device))
        others[-1].start()
    place_slots(routes_ref, order_ref, placed_ref)
    turned_ref[...] = placed_ref[...].reshape(EXP_WIN * CAP, -1).T
    spread.step1()
    spread.step2()
    spread.step3()
    for copy in sent:
        copy.wait_recv()
    for j, device in enumerate(place.layers()):
        others.append(remote(own_out, strips_ref.at[z], o_send.at[j], o_recv.at[j], device))
        others[-1].start()
    depth = w_all_ref.shape[0]
    weights = Spread(
        place, w_all_ref.at[:, :FIRST], lambda owner: weights_ref.at[owner],
        lambda ref, h: ref.at[pl.ds(h * (depth // 2), depth // 2)], q_send, q_recv,
    )
    weights.start()
    own_moves = [
        pltpu.make_async_copy(own_out, strips_ref.at[z], local.at[GROUP]),
        pltpu.make_async_copy(w_all_ref.at[:, :FIRST], weights_ref.at[me], local.at[GROUP + 1]),
    ]
    for move in own_moves:
        move.start()
    core, side, row = place.near
    across = flip(side, 4)
    order = [me, side, row, across, core, flip(side, 1), flip(row, 1), flip(across, 1)]

    def to_normed(owner):
        return pltpu.make_async_copy(held_ref.at[owner], normed_ref.at[owner], local.at[owner])

    def project(i, _):
        for at, slots in ((4, (4, 5)), (5, (6, 7)), (6, (8, 9)), (7, (12, 13))):

            @pl.when(i == at)
            def _(slots=slots):
                spread.wait(*slots)

        pl.when(i == 5)(weights.step1)
        pl.when(i == 7)(weights.step2)
        owner = order[-1]
        for at in range(GROUP - 1):
            owner = jnp.where(i == at, order[at], owner)
        to_normed(owner).start()
        linear = None
        for s in range(w_all_ref.shape[0]):
            size = w_all_ref.shape[2]
            term = dot(
                w_all_ref[s, :HW, :], held_ref[owner, :, s * size : (s + 1) * size], ((1,), (1,))
            )
            linear = term if linear is None else linear + term
        tokens = block(owner)
        cosine, sine = cos_ref[:, tokens], sin_ref[:, tokens]
        queries = turned(linear[:QW], cosine, sine) * HEAD_DIM ** (-0.5)
        qt_ref[:, tokens] = queries.astype(bf16)
        keys = turned(linear[QW : QW + HEAD_DIM], cosine, sine)
        kt_ref[:, tokens] = keys.astype(bf16)
        k_ref[tokens, :] = keys.T.astype(bf16)
        values = linear[QW + HEAD_DIM :]
        vt_ref[:, tokens] = values.astype(bf16)
        v_ref[tokens, :] = values.T.astype(bf16)
        return 0

    lax.fori_loop(0, GROUP, project, 0)
    weights.step3()
    for copy in sent:
        copy.wait_send()
    for copy in others:
        copy.wait()
    for move in own_moves:
        move.wait()
    for owner in range(GROUP):
        to_normed(owner).wait()
    spread.sent()
    weights.last()
    weights.sent()


def project_call(
    tokens, gain, router, cosine, sine, docs, routes, order, w_out, w_query, key_matrix,
    value_matrix, depth,
):
    rows, width = tokens.shape
    span = GROUP * rows
    strip = w_out.shape[0] // GROUP
    size = w_out.shape[0]
    return pl.pallas_call(
        project_kernel,
        out_shape=(
            shape((depth, ALL, size), bf16),
            shape((QW, span), bf16),
            shape((HEAD_DIM, span), bf16),
            shape((HEAD_DIM, span), bf16),
            shape((span, HEAD_DIM), bf16),
            shape((span, HEAD_DIM), bf16),
            shape((GROUP,) + docs.shape, jnp.int32),
            shape((EXP_WIN, CAP, rows), bf16),
            shape((rows, EXP_WIN * CAP), bf16),
            shape((GROUP, rows, width), bf16),
            shape((depth, strip, w_out.shape[1]), bf16),
            shape((GROUP, depth, FIRST, size), bf16),
        ),
        in_specs=[IN_VMEM] * 8 + [IN_ANY] * 4,
        out_specs=(IN_VMEM,) * 9 + (IN_ANY,) * 3,
        scratch_shapes=[
            VMEM((GROUP, rows, width), bf16),
            VMEM((strip, width), bf16),
            VMEM((size, 2 * 128), bf16),
            VMEM((size, 128), bf16),
            VMEM((size, 128), bf16),
        ]
        + [DMA((depth - 1,))] * 4
        + [DMA((GROUP - 1,))] * 2
        + [DMA((Spread.SEMS,))] * 4
        + [DMA((GROUP + 4,))],
        compiler_params=params(1),
        name="project",
    )(
        tokens, gain, router, cosine, sine, docs, routes, order, w_out, w_query, key_matrix,
        value_matrix,
    )


def docs_column(row):
    return jnp.broadcast_to(row.astype(f32), (8, row.shape[1])).T[:, :1]


def attend_kernel(
    n_blocks, qt_ref, k_ref, vt_ref, docs_ref, strips_ref, w_all_ref,
    o_ref, lse_ref, attended_ref, out_weight_ref, weights_ref,
    staged_ref, docs_col_ref, top_ref, sum_ref, acc_ref,
    a_send, a_recv, s_send, s_recv, w_send, w_recv, local,
):
    T = TOK_DEV
    place = Place()
    me = place.me
    first = place.base
    met = greet(place.others())
    depth = strips_ref.shape[0]
    moves = [
        pltpu.make_async_copy(strips_ref, out_weight_ref.at[:, me], local.at[0]),
        pltpu.make_async_copy(w_all_ref.at[:, FIRST:HW], weights_ref.at[me], local.at[1]),
    ]

    def layers(ref, h):
        return ref.at[pl.ds(h * (depth // 2), depth // 2)]

    spreads = [
        Spread(place, strips_ref, lambda owner: out_weight_ref.at[:, owner], layers, s_send, s_recv),
        Spread(
            place, w_all_ref.at[:, FIRST:HW], lambda owner: weights_ref.at[owner], layers, w_send, w_recv
        ),
    ]

    def turn(i, _):
        docs_col_ref[i] = docs_column(docs_ref[i])
        return 0

    lax.fori_loop(0, n_blocks, turn, 0)
    met()
    spreads[0].start()
    for move in moves:
        move.start()

    def tile(kb, qb, mask):
        kt = k_ref[block(kb), :]
        vt = vt_ref[:, block(kb)]
        heads = range(HEADS)
        parts = [slice(h * HEAD_DIM, (h + 1) * HEAD_DIM) for h in heads]
        s = [dot(kt, qt_ref[parts[h], block(qb)]) for h in heads]
        if mask is not None:
            s = [jnp.where(mask, x, score_masked) for x in s]
        old = [top_ref[h : h + 1, :] for h in heads]
        new = [jnp.maximum(old[h], jnp.max(s[h], axis=0, keepdims=True)) for h in heads]
        p = [jnp.exp(s[h] - new[h]) for h in heads]
        factor = [jnp.exp(old[h] - new[h]) for h in heads]
        total = [
            sum_ref[h : h + 1, :] * factor[h] + jnp.sum(p[h], axis=0, keepdims=True) for h in heads
        ]
        mixed = [acc_ref[parts[h], :] * factor[h] + dot(vt, p[h].astype(bf16)) for h in heads]
        for h in heads:
            top_ref[h : h + 1, :] = new[h]
            sum_ref[h : h + 1, :] = total[h]
            acc_ref[parts[h], :] = mixed[h]

    def same(kb, gq):
        return docs_col_ref[kb] == docs_ref[gq].astype(f32)

    def attended_copy(to, slot):
        return remote(
            staged_ref.at[to], attended_ref.at[slot], a_send.at[to], a_recv.at[slot], place.ctx(to)
        )

    def q_block(j, _):
        for at, act in (
            (2, spreads[0].step1), (4, spreads[0].step2), (4, spreads[1].start),
            (6, spreads[0].step3),
        ):
            pl.when(j == at)(act)
        qb = GROUP - 1 - j
        gq = first + qb
        top_ref[...] = jnp.full_like(top_ref, score_masked)
        sum_ref[...] = jnp.ones_like(sum_ref)
        acc_ref[...] = jnp.zeros_like(acc_ref)
        last = gq == n_blocks - 1

        def k_block(kb, _):
            edge = jnp.logical_or(kb == 0, last)

            @pl.when(edge)
            def _():
                tile(kb, qb, same(kb, gq))

            @pl.when(jnp.logical_not(edge))
            def _():
                tile(kb, qb, None)

            return 0

        lax.fori_loop(0, gq, k_block, 0)
        keys = lax.broadcasted_iota(jnp.int32, (T, T), 0)
        queries = lax.broadcasted_iota(jnp.int32, (T, T), 1)
        tile(gq, qb, same(gq, gq) & (keys <= queries))
        lse_ref[qb] = top_ref[...] + jnp.log(sum_ref[...])
        for h in range(HEADS):
            part = slice(h * HEAD_DIM, (h + 1) * HEAD_DIM)
            mixed = acc_ref[part, :] / sum_ref[h : h + 1, :]
            o_ref[part, block(qb)] = mixed
            staged_ref[qb, part, :] = mixed.astype(bf16)

        @pl.when(qb != me)
        def _():
            attended_copy(qb, me).start()

        return 0

    lax.fori_loop(0, GROUP, q_block, 0)
    own = pltpu.make_async_copy(staged_ref.at[me], attended_ref.at[me], local.at[2])
    own.start()
    spreads[1].step1()
    spreads[1].step2()
    spreads[1].step3()
    for j in range(1, GROUP):
        other = lax.rem(me + j, GROUP)
        attended_copy(other, other).wait()
    for spread in spreads:
        spread.last()
        spread.sent()
    for move in moves:
        move.wait()
    own.wait()


def attend_call(qt, k, vt, docs, strips, w_all):
    n = k.shape[0] // TOK_DEV
    span = qt.shape[1]
    depth, _, size = w_all.shape
    return pl.pallas_call(
        functools.partial(attend_kernel, n),
        out_shape=(
            shape((QW, span), f32),
            shape((GROUP, 8, TOK_DEV), f32),
            shape((GROUP, QW, TOK_DEV), bf16),
            shape((depth, GROUP) + strips.shape[1:], bf16),
            shape((GROUP, depth, HW - FIRST, size), bf16),
        ),
        in_specs=[IN_VMEM] * 6,
        out_specs=(IN_VMEM, IN_VMEM, IN_ANY, IN_ANY, IN_ANY),
        scratch_shapes=[
            VMEM((GROUP, QW, TOK_DEV), bf16),
            VMEM((n, TOK_DEV, 1), f32),
            VMEM((8, TOK_DEV), f32),
            VMEM((8, TOK_DEV), f32),
            VMEM((QW, TOK_DEV), f32),
            DMA((GROUP,)),
            DMA((GROUP,)),
        ]
        + [DMA((Spread.SEMS,))] * 4
        + [DMA((3,))],
        compiler_params=params(2),
        name="attend",
    )(qt, k, vt, docs, strips, w_all)


def router_of(w_all_ref):
    return [w_all_ref[s, HW:, :] for s in range(w_all_ref.shape[0])]


def dispatch_kernel(
    attended_ref, weight_ref, gate_up_ref, tokens_ref, gain_ref, w_all_ref, routes_ref, placed_ref,
    cotangent_ref,
    residual_ref, normed_ref, gates_ref, slot_gates_ref, rows_ref, grads_ref, gate_ref, up_ref,
    active_ref, grad_down_ref, columns_ref,
    held_ref, weight_held, gate_up_held, mixed_ref, own_rows, own_grads,
    r_send, r_recv, g_send, g_recv, c_send, c_recv, local,
):
    place = Place()
    me = place.me
    fetches = [
        pltpu.make_async_copy(attended_ref, held_ref, local.at[0]),
        pltpu.make_async_copy(weight_ref, weight_held, local.at[1]),
        pltpu.make_async_copy(gate_up_ref, gate_up_held, local.at[3]),
    ]
    met = greet(place.others())
    for fetch in fetches:
        fetch.start()
    rows, width = tokens_ref.shape
    experts_wide = gates_ref.shape[0]

    def copy(source, target, send, receive, j):
        to = lax.rem(me + j, GROUP)
        return remote(source.at[to], target.at[me], send.at[j], receive.at[j], place.ctx(to))

    def strip_copy(j):
        to = lax.rem(me + j, GROUP)
        return remote(
            attended_ref.at[:, to], columns_ref.at[me], c_send.at[j], c_recv.at[j], place.ctx(to)
        )

    fetches[0].wait()
    met()
    for j in range(1, GROUP):
        strip_copy(j).start()
    own_strip = pltpu.make_async_copy(held_ref.at[:, me], columns_ref.at[me], local.at[2])
    own_strip.start()
    mixed_ref[...] = held_ref[...].reshape(width, rows).T
    fetches[1].wait()

    def out_columns(i, _):
        columns = block(i)
        residual_ref[:, columns] = tokens_ref[:, columns].astype(f32) + dot(
            mixed_ref[...], weight_held[:, columns]
        )
        return 0

    lax.fori_loop(0, width // TOK_DEV, out_columns, 0)
    residual = residual_ref[...]
    scale = lax.rsqrt(jnp.mean(residual * residual, axis=-1, keepdims=True) + epsilon)
    normed_ref[...] = (residual * scale * gain_ref[...]).astype(bf16)
    logits = None
    for s, router in enumerate(router_of(w_all_ref)):
        size = router.shape[1]
        term = dot(router, normed_ref[:, s * size : (s + 1) * size], ((1,), (1,)))
        logits = term if logits is None else logits + term
    expert = lax.broadcasted_iota(jnp.int32, (experts_wide, rows), 0)
    chosen = expert < 0
    for k in range(TOPK):
        chosen = chosen | (expert == routes_ref[k : k + 1, :])
    logits = jnp.where(chosen, logits, score_masked)
    top = jnp.max(logits, axis=0, keepdims=True)
    gates = jnp.where(chosen, jnp.exp(logits - top), 0.0)
    gates = gates / jnp.sum(gates, axis=0, keepdims=True)
    gates_ref[...] = gates
    for e in range(EXP_WIN):
        slot_gates_ref[e] = jnp.sum(
            placed_ref[e].astype(f32) * gates[e : e + 1, :], axis=1, keepdims=True
        )

    def send_rows(j, _):
        to = lax.rem(me + j, GROUP)
        own_rows[to] = dot(placed_ref[to], normed_ref[...]).astype(bf16)

        @pl.when(j < GROUP)
        def _():
            copy(own_rows, rows_ref, r_send, r_recv, j).start()

        return 0

    def send_grads(j, _):
        to = lax.rem(me + j, GROUP)
        routed = dot(placed_ref[to], cotangent_ref[...])
        own_grads[to] = (routed * slot_gates_ref[to]).astype(bf16)

        @pl.when(j < GROUP)
        def _():
            copy(own_grads, grads_ref, g_send, g_recv, j).start()

        return 0

    lax.fori_loop(1, GROUP + 1, send_rows, 0)
    lax.fori_loop(1, GROUP + 1, send_grads, 0)
    rows_ref[me] = own_rows[me]
    grads_ref[me] = own_grads[me]
    fetches[2].wait()
    for j in range(1, GROUP):
        copy(own_rows, rows_ref, r_send, r_recv, j).wait_recv()
    slots = GROUP * CAP
    hidden = gate_ref.shape[1]
    tiles = hidden // TOK_DEV

    def expert_up(i, _):
        came = rows_ref[...].reshape(slots, width)
        gate = dot(came, gate_up_held[:, block(i)])
        up = dot(came, gate_up_held[:, block(tiles + i)])
        gate_ref[:, block(i)] = gate
        up_ref[:, block(i)] = up
        active_ref[:, block(i)] = (gate * jax.nn.sigmoid(gate) * up).astype(bf16)
        return 0

    lax.fori_loop(0, tiles, expert_up, 0)
    for j in range(1, GROUP):
        copy(own_grads, grads_ref, g_send, g_recv, j).wait_recv()

    def expert_over(i, _):
        grad_down_ref[:, block(i)] = dot(
            active_ref[...], grads_ref[:, :, block(i)].reshape(slots, TOK_DEV), ((0,), (0,))
        ).astype(bf16)
        return 0

    lax.fori_loop(0, width // TOK_DEV, expert_over, 0)
    for j in range(1, GROUP):
        strip_copy(j).wait()
        copy(own_rows, rows_ref, r_send, r_recv, j).wait_send()
        copy(own_grads, grads_ref, g_send, g_recv, j).wait_send()
    own_strip.wait()


def dispatch_call(attended, weight, gate_up, tokens, gain, w_all, routes, placed, cotangent):
    rows, width = tokens.shape
    hidden = gate_up.shape[1] // 2
    count = GROUP * CAP
    slots = (GROUP, CAP, width)
    depth = w_all.shape[0]
    attended = attended.reshape(depth, GROUP, -1, rows)
    return pl.pallas_call(
        dispatch_kernel,
        out_shape=(
            shape((rows, width), f32),
            shape((rows, width), bf16),
            shape((ROUTER, rows), f32),
            shape((EXP_WIN, CAP, 1), f32),
            shape(slots, bf16),
            shape(slots, bf16),
            shape((count, hidden), f32),
            shape((count, hidden), f32),
            shape((count, hidden), bf16),
            shape((hidden, width), bf16),
            shape((GROUP, depth) + attended.shape[2:], bf16),
        ),
        in_specs=[IN_ANY] * 3 + [IN_VMEM] * 6,
        out_specs=(IN_VMEM,) * 10 + (IN_ANY,),
        scratch_shapes=[
            VMEM(attended.shape, bf16),
            VMEM(weight.shape, bf16),
            VMEM(gate_up.shape, bf16),
            VMEM((rows, width), bf16),
            VMEM(slots, bf16),
            VMEM(slots, bf16),
        ]
        + [DMA((GROUP,))] * 6
        + [DMA((4,))],
        compiler_params=params(3),
        name="dispatch",
    )(attended, weight, gate_up, tokens, gain, w_all, routes, placed, cotangent)


def expert_kernel(
    active_ref, down_ref, grads_ref, rows_ref, gate_ref, up_ref, gate_up_ref,
    out_ref, back_ref, grad_gate_up_ref,
    grads_held, rows_held, gate_up_held, own_ref, grad_ref, send, receive, local,
):
    place = Place()
    me = place.me
    met = greet(place.others())
    fetches = [
        pltpu.make_async_copy(grads_ref, grads_held, local.at[0]),
        pltpu.make_async_copy(rows_ref, rows_held, local.at[1]),
        pltpu.make_async_copy(gate_up_ref, gate_up_held, local.at[2]),
    ]
    for fetch in fetches:
        fetch.start()
    count, hidden = active_ref.shape
    width = down_ref.shape[1]
    T = TOK_DEV
    tiles = hidden // T

    def copy(j):
        to = lax.rem(me + j, GROUP)
        return remote(own_ref.at[to], out_ref.at[me], send.at[j], receive.at[j], place.ctx(to))

    def out(i, _):
        value = dot(active_ref[...], down_ref[:, block(i)]).astype(bf16)
        own_ref[:, :, block(i)] = value.reshape(GROUP, CAP, T)
        return 0

    lax.fori_loop(0, width // T, out, 0)
    met()
    for j in range(1, GROUP):
        copy(j).start()
    move = pltpu.make_async_copy(own_ref.at[me], out_ref.at[me], local.at[3])
    move.start()
    fetches[0].wait()

    def back(i, _):
        grad = dot(grads_held[...], down_ref[block(i), :], ((1,), (1,)))
        gate, up = gate_ref[:, block(i)], up_ref[:, block(i)]
        sigmoid = jax.nn.sigmoid(gate)
        grad_gate = grad * up * sigmoid * (1.0 + gate * (1.0 - sigmoid))
        grad_ref[:, block(i)] = grad_gate.astype(bf16)
        grad_ref[:, block(tiles + i)] = (grad * gate * sigmoid).astype(bf16)
        return 0

    lax.fori_loop(0, tiles, back, 0)
    fetches[1].wait()
    fetches[2].wait()

    def over(i, _):
        grad_gate_up_ref[block(i), :] = dot(
            rows_held[:, block(i)], grad_ref[...], ((0,), (0,))
        ).astype(bf16)
        back_ref[:, block(i)] = dot(
            grad_ref[...], gate_up_held[block(i), :], ((1,), (1,))
        ).astype(bf16)
        return 0

    lax.fori_loop(0, width // T, over, 0)
    for j in range(1, GROUP):
        copy(j).wait()
    move.wait()


def expert_call(active, down, grads, rows, gate, up, gate_up):
    count, width = rows.shape
    hidden = down.shape[0]
    slots = (GROUP, CAP, width)
    return pl.pallas_call(
        expert_kernel,
        out_shape=(
            shape(slots, bf16),
            shape((count, width), bf16),
            shape((width, 2 * hidden), bf16),
        ),
        in_specs=[IN_VMEM] * 2 + [IN_ANY] * 2 + [IN_VMEM] * 2 + [IN_ANY],
        out_specs=(IN_ANY,) + (IN_VMEM,) * 2,
        scratch_shapes=[
            VMEM(grads.shape, bf16),
            VMEM(rows.shape, bf16),
            VMEM(gate_up.shape, bf16),
            VMEM(slots, bf16),
            VMEM((count, 2 * hidden), bf16),
            DMA((GROUP,)),
            DMA((GROUP,)),
            DMA((4,)),
        ],
        compiler_params=params(7),
        name="expert",
    )(active, down, grads, rows, gate, up, gate_up)


def combine_kernel(
    out_ref, sent_grad_ref, weight_ref, residual_ref, normed_ref, gates_ref, placed_ref,
    placed_t_ref, slot_gates_ref, cotangent_ref, gain_ref, w_all_ref,
    output_ref, grad_residual_ref, heads_ref, attn_ref, grad_router_ref, grad_gain_ref,
    back_ref, weight_held, sum_ref, turned_ref, staged_ref, scaled_ref,
    b_send, b_recv, h_send, h_recv, local,
):
    place = Place()
    me = place.me
    met = greet(place.others())
    fetch = pltpu.make_async_copy(weight_ref, weight_held, local.at[0])
    fetch.start()
    rows, width = residual_ref.shape

    def copy(source, target, send, receive, j):
        to = lax.rem(me + j, GROUP)
        return remote(source.at[to], target.at[me], send.at[j], receive.at[j], place.ctx(to))

    backs = [copy(sent_grad_ref, back_ref, b_send, b_recv, j) for j in range(1, GROUP)]
    met()
    for one in backs:
        one.start()
    move = pltpu.make_async_copy(sent_grad_ref.at[me], back_ref.at[me], local.at[1])
    move.start()
    turned_ref[...] = jnp.zeros_like(turned_ref)

    def add_expert(e, _):
        came = out_ref[e].astype(f32)
        scaled_ref[e] = (came * slot_gates_ref[e]).astype(bf16)
        routed = dot(placed_ref[e], cotangent_ref[...])
        slot_grad = jnp.sum(routed * came, axis=1, keepdims=True)
        turned_ref[pl.ds(e, 1), :] = jnp.sum(
            placed_ref[e].astype(f32) * slot_grad, axis=0, keepdims=True
        )
        return 0

    lax.fori_loop(0, EXP_WIN, add_expert, 0)
    slots = EXP_WIN * CAP

    def mix(i, _):
        columns = block(i)
        mixed = dot(placed_t_ref[...], scaled_ref[:, :, columns].reshape(slots, TOK_DEV))
        output_ref[:, columns] = (residual_ref[:, columns] + mixed).astype(bf16)
        return 0

    lax.fori_loop(0, width // TOK_DEV, mix, 0)
    gates = gates_ref[...]
    grad_gates = turned_ref[...]
    weighted = jnp.sum(gates * grad_gates, axis=0, keepdims=True)
    grad_logits = (gates * (grad_gates - weighted)).astype(bf16)
    for s, router in enumerate(router_of(w_all_ref)):
        size = router.shape[1]
        sum_ref[:, s * size : (s + 1) * size] = dot(grad_logits, router, ((0,), (0,)))
    grad_router_ref[...] = dot(grad_logits, normed_ref[...])
    fetch.wait()
    move.wait()
    for one in backs:
        one.wait_recv()

    def add_back(i, _):
        columns = block(i)
        sum_ref[:, columns] += dot(
            placed_t_ref[...], back_ref[:, :, columns].reshape(slots, TOK_DEV)
        )
        return 0

    lax.fori_loop(0, width // TOK_DEV, add_back, 0)
    residual = residual_ref[...]
    grad_normed = sum_ref[...]
    scale = lax.rsqrt(jnp.mean(residual * residual, axis=-1, keepdims=True) + epsilon)
    scaled = grad_normed * gain_ref[...]
    inner = jnp.mean(scaled * residual, axis=-1, keepdims=True)
    grad = scale * scaled - residual * (scale * scale * scale * inner)
    grad_gain_ref[...] = jnp.sum(grad_normed * residual * scale, axis=0, keepdims=True)
    grad_residual = cotangent_ref[...].astype(f32) + grad
    grad_residual_ref[...] = grad_residual
    attn_ref[...] = grad_residual.astype(bf16)

    def head_rows(j, _):
        to = lax.rem(me + j, GROUP)
        staged_ref[to] = dot(weight_held[block(to, QW), :], attn_ref[...], ((1,), (1,))).astype(bf16)

        @pl.when(j < GROUP)
        def _():
            copy(staged_ref, heads_ref, h_send, h_recv, j).start()

        return 0

    lax.fori_loop(1, GROUP + 1, head_rows, 0)
    move = pltpu.make_async_copy(staged_ref.at[me], heads_ref.at[me], local.at[2])
    move.start()
    for one in backs:
        one.wait_send()
    for j in range(1, GROUP):
        copy(staged_ref, heads_ref, h_send, h_recv, j).wait()
    move.wait()


def combine_call(
    out, sent_grad, weight, residual, normed, gates, placed, placed_t, slot_gates, cotangent,
    gain, w_all,
):
    rows, width = residual.shape
    slots = (GROUP, CAP, width)
    return pl.pallas_call(
        combine_kernel,
        out_shape=(
            shape((rows, width), bf16),
            shape((rows, width), f32),
            shape((GROUP, QW, rows), bf16),
            shape((rows, width), bf16),
            shape((ROUTER, width), f32),
            shape((1, width), f32),
        ),
        in_specs=[IN_VMEM] + [IN_ANY] * 2 + [IN_VMEM] * 9,
        out_specs=(IN_VMEM, IN_VMEM, IN_ANY, IN_VMEM, IN_VMEM, IN_VMEM),
        scratch_shapes=[
            VMEM(slots, bf16),
            VMEM(weight.shape, bf16),
            VMEM((rows, width), f32),
            VMEM((ROUTER, rows), f32),
            VMEM((GROUP, QW, rows), bf16),
            VMEM(slots, bf16),
        ]
        + [DMA((GROUP,))] * 4
        + [DMA((3,))],
        compiler_params=params(4),
        name="combine",
    )(
        out, sent_grad, weight, residual, normed, gates, placed, placed_t, slot_gates, cotangent,
        gain, w_all,
    )


def backward_kernel(
    n_blocks, qt_ref, k_ref, kt_ref, v_ref, heads_ref, o_ref, lse_ref, docs_ref, attn_ref,
    columns_ref, down_ref,
    dq_ref, dk_ref, dv_ref, out_shard_ref, down_all_ref,
    grad_out_ref, out_in, attn_all_ref, docs_col_ref, delta_ref, dk_acc, dv_acc, a_send, a_recv, e_send, e_recv, o_send, o_recv,
    local,
):
    T = TOK_DEV
    place = Place()
    me = place.me
    first = place.base
    met = greet([place.ctx(i) for i in place.near] + place.layers())
    z, layers = place.z, place.depth
    move = pltpu.make_async_copy(attn_ref, attn_all_ref.at[me], local.at[0])
    move.start()
    spread = Spread(
        place, attn_ref, lambda owner: attn_all_ref.at[owner],
        halves(T), a_send, a_recv,
    )
    met()
    spread.start()
    down_move = pltpu.make_async_copy(down_ref, down_all_ref.at[me], local.at[1])
    down_move.start()
    down_spread = Spread(
        place, down_ref, lambda owner: down_all_ref.at[owner],
        halves(down_ref.shape[0]), e_send, e_recv,
    )

    def turn(i, _):
        docs_col_ref[i] = docs_column(docs_ref[i])
        return 0

    lax.fori_loop(0, n_blocks, turn, 0)
    heads = range(HEADS)
    parts = [slice(h * HEAD_DIM, (h + 1) * HEAD_DIM) for h in heads]

    def prepare(i, _):
        for h in heads:
            product = o_ref[parts[h], block(i)] * heads_ref[i, parts[h], :].astype(f32)
            delta_ref[i, h : h + 1, :] = jnp.sum(product, axis=0, keepdims=True)
        return 0

    lax.fori_loop(0, GROUP, prepare, 0)
    dq_ref[...] = jnp.zeros_like(dq_ref)

    def tile(kb, qb, mask):
        k = k_ref[block(kb), :]
        v = v_ref[block(kb), :]
        kt = kt_ref[:, block(kb)]
        q = [qt_ref[part, block(qb)] for part in parts]
        do = [heads_ref[qb, part, :] for part in parts]
        s = [dot(k, x) for x in q]
        dp = [dot(v, x) for x in do]
        p = [jnp.exp(s[h] - lse_ref[qb, h : h + 1, :]) for h in heads]
        if mask is not None:
            p = [jnp.where(mask, x, 0.0) for x in p]
        ds = [(p[h] * (dp[h] - delta_ref[qb, h : h + 1, :])).astype(bf16) for h in heads]
        pb = [x.astype(bf16) for x in p]
        turn = ((1,), (1,))
        dv_acc[...] += dot(pb[0], do[0], turn) + dot(pb[1], do[1], turn) + dot(pb[2], do[2], turn)
        dk_acc[...] += dot(ds[0], q[0], turn) + dot(ds[1], q[1], turn) + dot(ds[2], q[2], turn)
        for h in heads:
            dq_ref[parts[h], block(qb)] += dot(kt, ds[h])

    def same(kb, gq):
        return docs_col_ref[kb] == docs_ref[gq].astype(f32)

    depth, strip, width = grad_out_ref.shape

    def down_copy(j):
        to = lax.rem(z + j, layers)
        return remote(
            grad_out_ref.at[to], out_in.at[z], o_send.at[j], o_recv.at[j], place.fsdp(to)
        )

    def out_weights():
        move.wait()
        spread.last()

        def columns(i, _):
            total = None
            for b in range(GROUP):
                term = dot(columns_ref[b].reshape(depth * strip, T), attn_all_ref[b, :, block(i)])
                total = term if total is None else total + term
            grad_out_ref[:, :, block(i)] = total.astype(bf16).reshape(depth, strip, T)
            return 0

        lax.fori_loop(0, width // T, columns, 0)
        for j in range(1, layers):
            down_copy(j).start()

    def k_block(kb, _):
        for at, act in (
            (2, spread.step1), (3, spread.step2), (3, down_spread.start), (5, spread.step3),
            (6, down_spread.step1), (7, out_weights),
        ):
            pl.when(kb == first + at)(act)
        dk_acc[...] = jnp.zeros_like(dk_acc)
        dv_acc[...] = jnp.zeros_like(dv_acc)

        @pl.when(kb >= first)
        def _():
            keys = lax.broadcasted_iota(jnp.int32, (T, T), 0)
            queries = lax.broadcasted_iota(jnp.int32, (T, T), 1)
            tile(kb, kb - first, same(kb, kb) & (keys <= queries))

        def q_block(qb, _):
            gq = first + qb
            edge = jnp.logical_or(kb == 0, gq == n_blocks - 1)

            @pl.when(edge)
            def _():
                tile(kb, qb, same(kb, gq))

            @pl.when(jnp.logical_not(edge))
            def _():
                tile(kb, qb, None)

            return 0

        lax.fori_loop(jnp.maximum(kb - first + 1, 0), GROUP, q_block, 0)
        dk_ref[:, block(kb)] = dk_acc[...].T
        dv_ref[:, block(kb)] = dv_acc[...].T
        return 0

    lax.fori_loop(0, first + GROUP, k_block, 0)

    def clear(kb, _):
        dk_ref[:, block(kb)] = jnp.zeros((HEAD_DIM, T), f32)
        dv_ref[:, block(kb)] = jnp.zeros((HEAD_DIM, T), f32)
        return 0

    lax.fori_loop(first + GROUP, n_blocks, clear, 0)
    down_spread.step2()
    down_spread.step3()
    for j in range(1, layers):
        down_copy(j).wait()
    out_in[z] = grad_out_ref[z]
    total = out_in[0].astype(f32)
    for s in range(1, layers):
        total = total + out_in[s].astype(f32)
    out_shard_ref[...] = total.astype(bf16)
    down_spread.last()
    down_spread.sent()
    down_move.wait()
    spread.sent()


def backward_call(qt, k, kt, v, heads, o, lse, docs, attn, columns, down):
    n = k.shape[0] // TOK_DEV
    span = qt.shape[1]
    rows, width = attn.shape
    _, depth, strip, _ = columns.shape
    return pl.pallas_call(
        functools.partial(backward_kernel, n),
        out_shape=(
            shape((QW, span), f32),
            shape(kt.shape, f32),
            shape(kt.shape, f32),
            shape((strip, width), bf16),
            shape((GROUP,) + down.shape, bf16),
        ),
        in_specs=[IN_VMEM] * 11,
        out_specs=(IN_VMEM,) * 4 + (IN_ANY,),
        scratch_shapes=[
            VMEM((depth, strip, width), bf16),
            VMEM((depth, strip, width), bf16),
            VMEM((GROUP, rows, width), bf16),
            VMEM((n, TOK_DEV, 1), f32),
            VMEM((GROUP, 8, TOK_DEV), f32),
            VMEM((TOK_DEV, HEAD_DIM), f32),
            VMEM((TOK_DEV, HEAD_DIM), f32),
        ]
        + [DMA((Spread.SEMS,))] * 4
        + [DMA((depth,))] * 2
        + [DMA((2,))],
        compiler_params=params(5),
        name="backward",
    )(qt, k, kt, v, heads, o, lse, docs, attn, columns, down)


def finish_kernel(
    normed_ref, first_ref, others_ref, gate_up_ref, out_shard_ref, dq_ref, dk_ref, dv_ref, cos_ref,
    sin_ref, tokens_ref, gain_ref, grad_residual_ref, grad_router_ref, grad_gain2_ref,
    input_grad_ref, shared_ref, small_all_ref, out_all_ref, gate_up_all_ref,
    normed_held, first_held, others_held, linear_ref, came_ref, first_t, others_t, sum_ref, part_ref,
    small_ref, head_in, small_in, shard_ref, small_shard_ref,
    g_send, g_recv, h_send, h_recv, s_send, s_recv, e_send, e_recv, f_send, f_recv, m_send, m_recv,
    c_send, c_recv, local,
):
    place = Place()
    me, z, depth = place.me, place.z, place.depth
    met = greet(place.others() + place.layers())
    fetches = [
        pltpu.make_async_copy(normed_ref, normed_held, local.at[0]),
        pltpu.make_async_copy(first_ref, first_held, local.at[1]),
        pltpu.make_async_copy(others_ref, others_held, local.at[2]),
    ]
    for fetch in fetches:
        fetch.start()
    rows, width = tokens_ref.shape
    size = width // depth

    def spread_of(source, out, send, receive):
        return Spread(
            place, source, lambda owner: out.at[owner], halves(source.shape[0]), send, receive
        )

    expert_spread = spread_of(gate_up_ref, gate_up_all_ref, e_send, e_recv)
    head_spread = spread_of(shard_ref, shared_ref, f_send, f_recv)
    small_spread = spread_of(small_shard_ref, small_all_ref, m_send, m_recv)
    out_spread = spread_of(out_shard_ref, out_all_ref, c_send, c_recv)
    moves = [
        pltpu.make_async_copy(gate_up_ref, gate_up_all_ref.at[me], local.at[3]),
        pltpu.make_async_copy(out_shard_ref, out_all_ref.at[me], local.at[4]),
        pltpu.make_async_copy(shard_ref, shared_ref.at[me], local.at[5]),
        pltpu.make_async_copy(small_shard_ref, small_all_ref.at[me], local.at[6]),
    ]
    moves[0].start()
    moves[1].start()

    def copy(j):
        to = lax.rem(me + j, GROUP)
        return remote(
            linear_ref.at[to], came_ref.at[me], g_send.at[j], g_recv.at[j], place.ctx(to)
        )

    def down(source, target, send, receive, j):
        to = lax.rem(z + j, depth)
        return remote(source.at[to], target.at[z], send.at[j], receive.at[j], place.fsdp(to))

    def turn_back(j, _):
        to = lax.rem(me + j, GROUP)
        cosine, sine = cos_ref[:, block(to)], -sin_ref[:, block(to)]
        dq = turned(dq_ref[:, block(to)], cosine, sine) * HEAD_DIM ** (-0.5)
        dk = turned(dk_ref[:, block(to)], cosine, sine)
        linear_ref[to, :QW, :] = dq.astype(bf16)
        linear_ref[to, QW : QW + HEAD_DIM, :] = dk.astype(bf16)
        linear_ref[to, QW + HEAD_DIM :, :] = dv_ref[:, block(to)].astype(bf16)
        pl.when(j == 1)(met)

        @pl.when(j < GROUP)
        def _():
            copy(j).start()

        return 0

    lax.fori_loop(1, GROUP + 1, turn_back, 0)
    came_ref[me] = linear_ref[me]
    out_spread.start()
    fetches[0].wait()

    def own_weights(j, _):
        to = lax.rem(z + j, depth)
        columns = block(to, size)
        total = None
        for b in range(GROUP):
            term = dot(linear_ref[b], normed_held[b, :, columns])
            total = term if total is None else total + term
        part_ref[to] = total.astype(bf16)

        @pl.when(j < depth)
        def _():
            down(part_ref, head_in, h_send, h_recv, j).start()

        return 0

    lax.fori_loop(1, depth + 1, own_weights, 0)
    for j in range(1, GROUP):
        copy(j).wait_send()
    expert_spread.start()
    fetches[1].wait()
    fetches[2].wait()
    for j in range(1, GROUP):
        copy(j).wait_recv()

    def turn(j, _):
        first_t[j] = came_ref[j, :FIRST, :].T
        others_t[j] = came_ref[j, FIRST:, :].T
        return 0

    lax.fori_loop(0, GROUP, turn, 0)

    def add_heads(s, _):
        total = None
        for j in range(GROUP):
            term = dot(first_t[j], first_held[j, s]) + dot(others_t[j], others_held[j, s])
            total = term if total is None else total + term
        sum_ref[:, block(s, size)] = total
        return 0

    lax.fori_loop(0, depth, add_heads, 0)
    out_spread.step1()
    x = tokens_ref[...].astype(f32)
    grad_normed = sum_ref[...]
    scale = lax.rsqrt(jnp.mean(x * x, axis=-1, keepdims=True) + epsilon)
    scaled = grad_normed * gain_ref[...]
    inner = jnp.mean(scaled * x, axis=-1, keepdims=True)
    grad = scale * scaled - x * (scale * scale * scale * inner)
    input_grad_ref[...] = grad_residual_ref[...] + grad
    gain1 = jnp.sum(grad_normed * x * scale, axis=0, keepdims=True)
    row = lax.broadcasted_iota(jnp.int32, (ROUTER, width), 0)
    small = jnp.where(row == ROUTER - 2, gain1, grad_router_ref[...])
    small = jnp.where(row == ROUTER - 1, grad_gain2_ref[...], small).astype(bf16)
    for s in range(depth):
        small_ref[s] = small[:, s * size : (s + 1) * size]
    smalls = [down(small_ref, small_in, s_send, s_recv, j) for j in range(1, depth)]
    heads = [down(part_ref, head_in, h_send, h_recv, j) for j in range(1, depth)]
    for one in smalls:
        one.start()
    expert_spread.step1()
    head_in[z] = part_ref[z]
    small_in[z] = small_ref[z]

    def total(ref):
        value = ref[0].astype(f32)
        for s in range(1, depth):
            value = value + ref[s].astype(f32)
        return value.astype(bf16)

    for one in heads:
        one.wait_recv()
    shard_ref[...] = total(head_in)
    head_spread.start()
    out_spread.step2()
    expert_spread.step2()
    for one in smalls:
        one.wait_recv()
    small_shard_ref[...] = total(small_in)
    small_spread.start()
    moves[2].start()
    moves[3].start()
    out_spread.step3()
    expert_spread.step3()
    spreads = (head_spread, small_spread)
    for spread in spreads:
        spread.step1()
    for spread in spreads:
        spread.step2()
    for spread in spreads:
        spread.step3()
    for spread in (out_spread, expert_spread, head_spread, small_spread):
        spread.last()
        spread.sent()
    for one in heads + smalls:
        one.wait_send()
    for move in moves:
        move.wait()


def finish_call(
    normed, first, others, gate_up, out_shard, dq, dk, dv, cosine, sine, tokens, gain, grad_residual,
    grad_router, grad_gain2, depth,
):
    rows, width = tokens.shape
    size = width // depth
    return pl.pallas_call(
        finish_kernel,
        out_shape=(
            shape((rows, width), f32),
            shape((GROUP, HW, size), bf16),
            shape((GROUP, ROUTER, size), bf16),
            shape((GROUP,) + out_shard.shape, bf16),
            shape((GROUP,) + gate_up.shape, bf16),
        ),
        in_specs=[IN_ANY] * 3 + [IN_VMEM] * 12,
        out_specs=(IN_VMEM,) + (IN_ANY,) * 4,
        scratch_shapes=[
            VMEM(normed.shape, bf16),
            VMEM(first.shape, bf16),
            VMEM(others.shape, bf16),
            VMEM((GROUP, HW, rows), bf16),
            VMEM((GROUP, HW, rows), bf16),
            VMEM((GROUP, rows, FIRST), bf16),
            VMEM((GROUP, rows, HW - FIRST), bf16),
            VMEM((rows, width), f32),
            VMEM((depth, HW, size), bf16),
            VMEM((depth, ROUTER, size), bf16),
            VMEM((depth, HW, size), bf16),
            VMEM((depth, ROUTER, size), bf16),
            VMEM((HW, size), bf16),
            VMEM((ROUTER, size), bf16),
        ]
        + [DMA((GROUP,))] * 2
        + [DMA((depth,))] * 4
        + [DMA((Spread.SEMS,))] * 8
        + [DMA((7,))],
        compiler_params=params(6),
        name="finish",
    )(
        normed, first, others, gate_up, out_shard, dq, dk, dv, cosine, sine, tokens, gain,
        grad_residual, grad_router, grad_gain2,
    )


def output_kernel(
    shared_ref, small_ref, out_ref, gate_up_ref, output_ref, input_grad_ref,
    q_ref, k_ref, v_ref, w_out_ref, router_ref, gain1_ref, gain2_ref, gate_ref, up_ref, final_ref,
    final_grad_ref, sum_ref,
):
    pair, i = shared_ref.shape[0], pl.program_id(0)
    hidden = gate_ref.shape[2]

    def rows(first, last):
        both = [shared_ref[p, first:last, :].astype(f32) for p in range(pair)]
        return jnp.concatenate(both, axis=0).T

    q_ref[...] = rows(0, QW)
    k_ref[...] = rows(QW, QW + HEAD_DIM)
    v_ref[...] = rows(QW + HEAD_DIM, HW)
    w_out_ref[...] = out_ref[...].astype(f32)
    final_ref[...] = output_ref[...]
    final_grad_ref[...] = input_grad_ref[...]
    gate_ref[...] = gate_up_ref[:, :, :hidden].astype(f32)
    up_ref[...] = gate_up_ref[:, :, hidden:].astype(f32)

    @pl.when(i == 0)
    def _():
        sum_ref[...] = jnp.zeros_like(sum_ref)

    for p in range(pair):
        sum_ref[...] += small_ref[p].astype(f32)

    @pl.when(i == pl.num_programs(0) - 1)
    def _():
        router_ref[...] = sum_ref[: router_ref.shape[0], :]
        gain1_ref[...] = sum_ref[ROUTER - 2, :]
        gain2_ref[...] = sum_ref[ROUTER - 1, :]


def output_call(shared, small, out, gate_up, output, input_grad, experts):
    count, _, size = shared.shape
    _, strip, width = out.shape
    hidden = gate_up.shape[2] // 2
    pair = 2
    rows = output.shape[0] // (count // pair)
    token = pl.BlockSpec((rows, width), lambda i: (i, 0))

    def first(*dims):
        return pl.BlockSpec((pair,) + dims, lambda i: (i,) + (0,) * len(dims))

    def columns(columns):
        return pl.BlockSpec((size, columns), lambda i: (0, i))

    def whole(*dims):
        return pl.BlockSpec(dims, lambda i: (0,) * len(dims))

    return pl.pallas_call(
        output_kernel,
        grid=(count // pair,),
        out_shape=(
            shape((size, count * QW), f32),
            shape((size, count * HEAD_DIM), f32),
            shape((size, count * HEAD_DIM), f32),
            shape(out.shape, f32),
            shape((experts, size), f32),
            shape((size,), f32),
            shape((size,), f32),
            shape((count, size, hidden), f32),
            shape((count, size, hidden), f32),
            shape(output.shape, bf16),
            shape(input_grad.shape, f32),
        ),
        in_specs=[
            first(*shared.shape[1:]), first(*small.shape[1:]), first(strip, width),
            first(*gate_up.shape[1:]), token, token,
        ],
        out_specs=(
            columns(pair * QW),
            columns(pair * HEAD_DIM),
            columns(pair * HEAD_DIM),
            first(strip, width),
            whole(experts, size),
            whole(size),
            whole(size),
            first(size, hidden),
            first(size, hidden),
            token,
            token,
        ),
        scratch_shapes=[VMEM((ROUTER, size), f32)],
        compiler_params=params(),
        name="output",
    )(shared, small, out, gate_up, output, input_grad)


def rotary_tables(length):
    frequencies = 10000.0 ** (-(np.arange(HEAD_DIM // 2) * 2.0) / HEAD_DIM)
    angles = frequencies[:, None] * np.arange(length)[None, :]
    return np.cos(angles).astype(np.float32), np.sin(angles).astype(np.float32)


def shards(
    tables,
    tokens,
    doc_ids,
    routes,
    slot_order,
    norm1_gain,
    norm2_gain,
    w_query,
    key_matrix,
    value_matrix,
    w_out,
    w_router,
    w_gate,
    w_up,
    w_down,
    cotangent,
):
    rows, width = tokens.shape[1:]
    ctx, depth = lax.axis_size("ctx"), lax.axis_size("fsdp")
    place = lax.axis_index("ctx")
    parts = ctx // GROUP
    head, part = place % GROUP, place // GROUP
    far = [[p * GROUP + i for p in range(parts)] for i in range(GROUP)]
    span = GROUP * rows
    experts = w_router.shape[1]
    hidden = w_gate.shape[2]

    def gather_z(value):
        return lax.all_gather(value, "fsdp", axis=0, tiled=True)

    def reduce_z(value):
        value = lax.psum_scatter(value.astype(bf16), "fsdp", scatter_dimension=0, tiled=True)
        if parts > 1:
            value = lax.psum(value, "ctx", axis_index_groups=far)
        return value

    cosine, sine = tables
    if parts > 1:
        cosine = lax.dynamic_slice_in_dim(cosine, part * span, span, 1)
        sine = lax.dynamic_slice_in_dim(sine, part * span, span, 1)
    own_tokens, own_cotangent = tokens[0], cotangent[0]
    gain1, gain2 = norm1_gain[None, :], norm2_gain[None, :]

    route_rows, order_rows = routes[0].T, slot_order[0].T
    (
        w_all, queries, keys_t, values_t, keys, values, docs, placed, placed_t, normed1, strips,
        first_all,
    ) = project_call(
        own_tokens, gain1, jnp.pad(w_router.T, ((0, ROUTER - experts), (0, 0))), cosine, sine, doc_ids,
        route_rows, order_rows, w_out, w_query, key_matrix, value_matrix, depth,
    )
    w_gate, w_up, w_down, docs = lax.optimization_barrier((w_gate, w_up, w_down, docs))
    gate_up = gather_z(
        jnp.concatenate(
            [
                lax.dynamic_index_in_dim(w_gate, head, 0, False),
                lax.dynamic_index_in_dim(w_up, head, 0, False),
            ],
            axis=1,
        )
    )
    down = gather_z(lax.dynamic_index_in_dim(w_down, head, 0, False))
    if parts > 1:

        def gather_far(value, axis):
            return lax.all_gather(value, "ctx", axis=axis, axis_index_groups=far, tiled=True)

        keys, values, docs = gather_far(keys, 0), gather_far(values, 0), gather_far(docs, 0)
        keys_t, values_t = gather_far(keys_t, 1), gather_far(values_t, 1)
    attended_f32, log_total, attended, out_weight, others_all = attend_call(
        queries, keys, values_t, docs, strips, w_all
    )
    out_weight = out_weight.reshape(width, width)
    (
        residual, normed2, gates, slot_gates, sent_rows, sent_grads, gate, up, active, grad_w_down,
        columns,
    ) = dispatch_call(
        attended, out_weight, gate_up, own_tokens, gain2, w_all, route_rows, placed, own_cotangent
    )
    grad_w_down = reduce_z(grad_w_down)
    expert_out, grad_buffer, grad_w_gate_up = expert_call(
        active, down, sent_grads.reshape(GROUP * CAP, width), sent_rows.reshape(GROUP * CAP, width),
        gate, up, gate_up,
    )
    grad_w_gate_up = reduce_z(grad_w_gate_up)
    output, grad_residual, heads, attn, grad_router, grad_gain2 = combine_call(
        expert_out, grad_buffer.reshape(sent_rows.shape), out_weight,
        residual, normed2, gates, placed, placed_t, slot_gates, own_cotangent, gain2, w_all,
    )
    dq, dk, dv, out_shard, down_w = backward_call(
        queries, keys, keys_t, values, heads, attended_f32, log_total, docs, attn, columns,
        grad_w_down,
    )
    if parts > 1:
        dk = lax.psum_scatter(dk, "ctx", scatter_dimension=1, axis_index_groups=far, tiled=True)
        dv = lax.psum_scatter(dv, "ctx", scatter_dimension=1, axis_index_groups=far, tiled=True)
    if parts > 1:
        out_shard = lax.psum(out_shard, "ctx", axis_index_groups=far)
    input_grad, shared, small, out_w, gate_up_w = finish_call(
        normed1, first_all, others_all, grad_w_gate_up, out_shard, dq, dk, dv, cosine, sine,
        own_tokens, gain1, grad_residual, grad_router, grad_gain2, depth,
    )
    if parts > 1:
        shared, small = lax.psum((shared, small), "ctx", axis_index_groups=far)

    q_w, k_w, v_w, out_w, router_w, gain1_w, gain2_w, gate_w, up_w, output, input_grad = output_call(
        shared, small, out_w, gate_up_w, output, input_grad, experts
    )
    return (
        output[None],
        input_grad[None],
        gain1_w,
        gain2_w,
        q_w,
        k_w,
        v_w,
        out_w.reshape(-1, width),
        router_w.T,
        gate_w,
        up_w,
        down_w.astype(f32),
    )


def solution(mesh):
    token_spec = P("fsdp", "ctx", None)
    row_spec, expert_spec = P("fsdp", None), P(None, "fsdp", None)
    tables = rotary_tables(mesh.shape["ctx"] * TOK_DEV)

    def program(*arguments):
        return jax.shard_map(
            functools.partial(shards, tuple(jnp.asarray(t) for t in tables)),
            mesh=mesh,
            in_specs=(
                token_spec,
                P("fsdp", "ctx"),
                token_spec,
                token_spec,
                P(),
                P(),
                row_spec,
                row_spec,
                row_spec,
                row_spec,
                row_spec,
                expert_spec,
                expert_spec,
                expert_spec,
                token_spec,
            ),
            out_specs=(
                token_spec,
                token_spec,
                P("fsdp"),
                P("fsdp"),
                row_spec,
                row_spec,
                row_spec,
                row_spec,
                row_spec,
                expert_spec,
                expert_spec,
                expert_spec,
            ),
            check_vma=False,
        )(*arguments)

    return program
```

time: 621 us -> 387 us (0.62)
  waiting for transfers between devices: 84.2 us -> 2.8 us
  Pallas kernels: 438 us -> 358 us
  local copies, waits for them, and re-layouts: 52.1 us -> 5.39 us
  matrix products: 22.2 us -> 0 us
    pallas_call x5, Pallas kernels: 288 us -> 202 us  [the longest x1 59.2 us: attend_call(): pl.pallas_call(functools.partial(attend_kernel, n), out_shape=(shape((QW,...]
    reduce_scatter x3 -> x2, waiting for transfers between devices: 84.1 us -> 0.02 us  [reduce_z(): lax.psum_scatter(value.astype(bf16), 'fsdp', scatter_dimension=0, tiled=T...]
    pallas_call x1, Pallas kernels: 36.1 us -> 67.7 us  [finish_call(): pl.pallas_call(finish_kernel, out_shape=(shape((rows, width), f32), shape...]
    pallas_call x1, Pallas kernels: 65.5 us -> 36.9 us  [combine_call(): pl.pallas_call(combine_kernel, out_shape=(shape((rows, width), bf16), sha...]
    dot_general x6 -> x0, matrix products: 22.2 us -> none  [dot(): lax.dot_general(left, right, (dims, ((), ())), preferred_element_type=f32)]
    unnamed x48 -> x6, local copies, waits for them, and re-layouts: 18.2 us -> 0.02 us
    transpose x6 -> x0, local copies, waits for them, and re-layouts: 18 us -> none  [columns(): return jnp.transpose(value, (1, 0, 2)).reshape(value.shape[1], -1)]
    slice x2 -> x0, local copies, waits for them, and re-layouts: 10.4 us -> none  [the longest x1 9.49 us: shards(): gate_up_w[:, :, hidden:]]
  transfers between devices with their start and end apart: 5 -> 4, of which waited for: 2 -> 1; matrix products, arithmetic and copies ran while one was open for 9% -> 2% of each run, Pallas kernels for 33% -> 59%
where the time goes in v1:
time: 387 us; the launch traced here: 386 us
  Pallas kernels  358 us (93%)
  between operations  13.9 us (4%)
  other arithmetic  6.45 us (2%)
  local copies, waits for them, and re-layouts  5.39 us (1%)
    pallas_call x1, Pallas kernels, finish_call(): pl.pallas_call(finish_kernel, out_shape=(shape((rows, width), f32), shape...  67.7 us
    pallas_call x1, Pallas kernels, attend_call(): pl.pallas_call(functools.partial(attend_kernel, n), out_shape=(shape((QW,...  59.2 us
    pallas_call x1, Pallas kernels, backward_call(): pl.pallas_call(functools.partial(backward_kernel, n), out_shape=(shape((Q...  53.7 us
    pallas_call x1, Pallas kernels, dispatch_call(): pl.pallas_call(dispatch_kernel, out_shape=(shape((rows, width), f32), sha...  51.4 us
    pallas_call x1, Pallas kernels, project_call(): pl.pallas_call(project_kernel, out_shape=(shape((depth, ALL, size), bf16)...  48.9 us
    pallas_call x1, Pallas kernels, combine_call(): pl.pallas_call(combine_kernel, out_shape=(shape((rows, width), bf16), sha...  36.9 us
    pallas_call x1, Pallas kernels, expert_call(): pl.pallas_call(expert_kernel, out_shape=(shape(slots, bf16), shape((count...  26.9 us
    pallas_call x1, Pallas kernels, output_call(): pl.pallas_call(output_kernel, grid=(count // pair,), out_shape=(shape((si...  12.9 us
  transfers between devices with their start and end apart: 4, of which 1 were waited for; matrix products, arithmetic and copies ran while one was open for 2% of the time, Pallas kernels for 59%

profile of v1, /device:TPU:0, one launch (start us, length us, event | category | flops | bytes accessed | tf_op | source)
XLA Modules:
  0.0 386.5 jit_solution(14044565383997105780)
XLA Ops:
  7.2 0.0 all-gather.4.cloned.1.call-start
  7.3 1.4 broadcast_in_dim.12.gain_ref
  8.7 1.4 pad.4.router_ref
  10.1 48.9 %project.1 = (bf16[4,368,384]{2,1,0:T(8,128)(2,1)}, bf16[192,2048]{1,0:T(8,128)(2,1)}, bf16[64,2048]{1,0:T(8,128)(2,1)}, bf16[64,2048]{1,0:T(8,128)(2,1)}, bf16[...) custom-call(bf16[256,1536]{1,0:T(8,128)(2,1)} %bitcast.25, ...), custom_call_target="tpu_custom_call" | custom-call | tf_op jit(solution)/shard_map/project/pallas_call | solution.py:346
  59.0 1.2 dynamic-slice_bitcast_fusion
  60.1 1.0 pad_maximum_fusion
  61.2 0.0 all-gather.6.cloned.1.call-start
  61.2 0.8 constant_dynamic-slice_fusion
  62.0 0.0 reduce-scatter.5.cloned.1.call-start
  62.1 0.6 broadcast_in_dim.13.gain_ref
  62.7 59.2 %attend.1 = (f32[192,2048]{1,0:T(8,128)}, f32[8,8,256]{2,1,0:T(8,128)}, bf16[8,192,256]{2,1,0:T(8,128)(2,1)}, bf16[4,8,48,1536]{3,2,1,0:T(8,128)(2,1)}, bf16[8,4,224,384]{3,2,1,0:T(8,128)(2,1)}) custom-call(bf16[192,2048]{1,0:T(8,128)(2,1)} %get-tuple-element.76.qt_ref, bf16[2048,64]{1,0:T(8,128)(2,1)} %get-tuple-element.77.k_ref, ...), custom_call_target="tpu_custom_call" | custom-call | tf_op jit(solution)/shard_map/attend/pallas_call | solution.py:517
  121.9 2.7 all-gather.4.cloned.1.call-done.gate_up_ref
  124.6 51.4 %dispatch.1 = (f32[256,1536]{1,0:T(8,128)}, bf16[256,1536]{1,0:T(8,128)(2,1)}, f32[48,256]{1,0:T(8,128)}, f32[8,64,1]{2,1,0:T(8,128)}, bf16[8,64,1536]{2,1,0:T(8...) custom-call(bf16[4,8,48,256]{3,2,1,0:T(8,128)(2,1)} %bitcast.34, ...), custom_call_target="tpu_custom_call" | custom-call | tf_op jit(solution)/shard_map/dispatch/pallas_call | solution.py:684
  176.1 0.0 reduce-scatter.5.cloned.1.call-update
  176.1 0.0 reduce-scatter.3.cloned.1.call-start
  176.1 0.0 all-gather.6.cloned.1.call-done
  176.2 26.9 %expert.1 = (bf16[8,64,1536]{2,1,0:T(8,128)(2,1)}, bf16[512,1536]{1,0:T(8,128)(2,1)}, bf16[1536,1024]{1,0:T(8,128)(2,1)}) custom-call(bf16[512,512]{1,0:T(8,128)(2,1)} %get-tuple-element.89.active_ref, bf16[512,1536]{1,0:T(8,128)(2,1)} %bitcast.30, bf16[512,1536]{1,0:T(8,128)(2,1)} %bitcast.33, bf16[512,1536]{1,0:T(8,128)(2,1)} %bitcast.32, ...), custom_call_target="tpu_custom_call" | custom-call | tf_op jit(solution)/shard_map/expert/pallas_call | solution.py:785
  203.1 0.0 reduce-scatter.3.cloned.1.call-update
  203.1 36.9 %combine.1 = (bf16[256,1536]{1,0:T(8,128)(2,1)}, f32[256,1536]{1,0:T(8,128)}, bf16[8,192,256]{2,1,0:T(8,128)(2,1)}, bf16[256,1536]{1,0:T(8,128)(2,1)}, f32[48,1536]{1,0:T(8,128)}, /*index=5*/f32[1,1536]{1,0:T(1,128)}) custom-call(bf16[8,64,1536]{2,1,0:T(8,128)(2,1)} %get-tuple-element.98.out_ref, bf16[8,64,1536]{2,1,0:T(8,128)(2,1)} %bitcast.31, ...), custom_call_target="tpu_custom_call" | custom-call | tf_op jit(solution)/shard_map/combine/pallas_call | solution.py:913
  240.1 0.0 reduce-scatter.5.cloned.1.call-done.down_ref
  240.1 53.7 %backward.1 = (f32[192,2048]{1,0:T(8,128)}, f32[64,2048]{1,0:T(8,128)}, f32[64,2048]{1,0:T(8,128)}, bf16[48,1536]{1,0:T(8,128)(2,1)}, bf16[8,128,1536]{2,1,0:T(8,128)(2,1)}) custom-call(bf16[192,2048]{1,0:T(8,128)(2,1)} %get-tuple-element.76.qt_ref, bf16[2048,64]{1,0:T(8,128)(2,1)} %get-tuple-element.77.k_ref, bf16[64,2048]{1,0:T(8,128)(2,1)} %get-tuple-element.96.kt_ref, ...), custom_call_target="tpu_custom_call" | custom-call | tf_op jit(solution)/shard_map/backward/pallas_call | solution.py:1096
  293.8 5.5 %convert_element_type.5 = f32[8,128,1536]{2,1,0:T(8,128)} convert(bf16[8,128,1536]{2,1,0:T(8,128)(2,1)} %get-tuple-element.135) | non-fusion elementwise | flops 1572864 | bytes 9437184 | tf_op jit(solution)/shard_map/convert_element_type | solution.py:1556
  299.3 67.7 %finish.1 = (f32[256,1536]{1,0:T(8,128)}, bf16[8,320,384]{2,1,0:T(8,128)(2,1)}, bf16[8,48,384]{2,1,0:T(8,128)(2,1)}, bf16[8,48,1536]{2,1,0:T(8,128)(2,1)}, bf16[8,384,1024]{2,1,0:T(8,128)(2,1)}) custom-call(bf16[8,256,1536]{2,1,0:T(8,128)(2,1)} %get-tuple-element.74.normed_ref, bf16[8,4,96,384]{3,2,1,0:T(8,128)(2,1)} %get-tuple-element.75.first_ref, ...), custom_call_target="tpu_custom_call" | custom-call | tf_op jit(solution)/shard_map/finish/pallas_call | solution.py:1299
  367.0 12.9 %output.1 = (f32[384,1536]{1,0:T(8,128)}, f32[384,512]{1,0:T(8,128)}, f32[384,512]{1,0:T(8,128)}, f32[8,48,1536]{2,1,0:T(8,128)}, f32[40,384]{1,0:T(8,128)}, /*i...) custom-call(bf16[8,320,384]{2,1,0:T(8,128)(2,1)} %get-tuple-element., ...), custom_call_target="tpu_custom_call" | custom-call | tf_op jit(solution)/shard_map/output/pallas_call | solution.py:1390
  (9 shorter events, 0.1 us)
Async XLA Ops:
  7.2 54.0 %copy-start = (bf16[8,128,1536]{2,1,0:T(8,128)(2,1)S(1)}, bf16[8,128,1536]{2,1,0:T(8,128)(2,1)}, u32[]{:S(2)}) copy-start(bf16[8,128,1536]{2,1,0:T(8,128)(2,1)} %param.30) | copy-start | bytes 9437188
  7.2 117.4 %all-gather.4.cloned.1.call-start = ((), (), s32[]{:S(2)}) async-start(), calls=%async_computation.2 | async-start | bytes 3932160 | tf_op jit(solution)/shard_map/all_gather | solution.py:1464
  60.1 1.9 copy-start.2
  61.2 115.0 %all-gather.6.cloned.1.call-start = ((), (), s32[]{:S(2)}) async-start(), calls=%async_computation.5 | async-start | bytes 1966080 | tf_op jit(solution)/shard_map/all_gather | solution.py:1464
  62.0 178.1 %reduce-scatter.5.cloned.1.call-start = ((), (), s32[]{:S(2)}) async-start(), calls=%async_computation.4 | async-start | bytes 1966080 | tf_op jit(solution)/shard_map/reduce_scatter | solution.py:1467
  176.1 123.2 %reduce-scatter.3.cloned.1.call-start = ((), (), s32[]{:S(2)}) async-start(), calls=%async_computation.3 | async-start | bytes 3932160 | tf_op jit(solution)/shard_map/reduce_scatter | solution.py:1467
  367.0 13.0 %copy-start.1 = (bf16[8,128,1536]{2,1,0:T(8,128)(2,1)S(1)}, bf16[8,128,1536]{2,1,0:T(8,128)(2,1)}, u32[]{:S(2)}) copy-start(bf16[8,128,1536]{2,1,0:T(8,128)(2,1)} %param.30) | copy-start | bytes 9437188
Sparse Core Ops, SparseCore 0:
  61.3 63.3 all-gather.3
  126.8 35.7 all-gather.5
  176.2 36.5 reduce-scatter.4
  215.0 59.2 reduce-scatter.2

commit v2 on v1

--- a/solution.py
+++ b/solution.py
@@ -52,6 +52,67 @@
         has_side_effects=collective_id is not None,
         vmem_limit_bytes=limit << 20,
     )
+
+
+class Staged:
+    def __init__(self, fetches, puts):
+        self.fetches, self.puts, self.out = fetches, puts, []
+
+    def need(self, *refs):
+        for ref in refs:
+            self.fetches.pop(id(ref)).wait()
+
+    def put(self, *refs):
+        for ref in refs:
+            copy = self.puts.pop(id(ref))
+            copy.start()
+            self.out.append(copy)
+
+    def finish(self):
+        for copy in self.fetches.values():
+            copy.wait()
+        for copy in self.puts.values():
+            copy.start()
+        for copy in self.out + list(self.puts.values()):
+            copy.wait()
+
+
+def staged_call(body, name, collective_id, ins, outs, scratch):
+    held_in = [i for i, (how, _) in enumerate(ins) if how == "h"]
+    held_out = [i for i, (how, _) in enumerate(outs) if how == "h"]
+
+    def kernel(*refs):
+        refs = list(refs)
+        given, refs = refs[: len(ins)], refs[len(ins) :]
+        results, refs = refs[: len(outs)], refs[len(outs) :]
+        own, refs = refs[: len(scratch)], refs[len(scratch) :]
+        in_held, refs = refs[: len(held_in)], refs[len(held_in) :]
+        out_held, (in_sems, out_sems) = refs[: len(held_out)], refs[len(held_out) :]
+        fetches, puts = {}, {}
+        for n, i in enumerate(held_in):
+            copy = pltpu.make_async_copy(given[i], in_held[n], in_sems.at[n])
+            copy.start()
+            given[i] = in_held[n]
+            fetches[id(given[i])] = copy
+        for n, i in enumerate(held_out):
+            puts[id(out_held[n])] = pltpu.make_async_copy(out_held[n], results[i], out_sems.at[n])
+            results[i] = out_held[n]
+        stage = Staged(fetches, puts)
+        body(stage, *given, *results, *own)
+        stage.finish()
+
+    return pl.pallas_call(
+        kernel,
+        out_shape=tuple(one for _, one in outs),
+        in_specs=[IN_VMEM if how == "v" else IN_ANY for how, _ in ins],
+        out_specs=tuple(IN_VMEM if how == "v" else IN_ANY for how, _ in outs),
+        scratch_shapes=list(scratch)
+        + [VMEM(ins[i][1].shape, ins[i][1].dtype) for i in held_in]
+        + [VMEM(outs[i][1].shape, outs[i][1].dtype) for i in held_out]
+        + [DMA((max(len(held_in), 1),)), DMA((max(len(held_out), 1),))],
+        compiler_params=params(collective_id),
+        name=name,
+    )(*(array for _, array in ins))
 
 
 def flip(index, bit):
@@ -195,7 +256,7 @@
 
 
 def project_kernel(
-    tokens_ref, gain_ref, router_ref, cos_ref, sin_ref, docs_ref, routes_ref, order_ref, w_out_ref,
+    stage, tokens_ref, gain_ref, router_ref, cos_ref, sin_ref, docs_ref, routes_ref, order_ref, w_out_ref,
     w_query_ref, key_matrix_ref, value_matrix_ref,
     w_all_ref, qt_ref, kt_ref, vt_ref, k_ref, v_ref, docs_all_ref, placed_ref, turned_ref, normed_ref,
     strips_ref, weights_ref,
@@ -229,9 +290,10 @@
     ]
     for fetch in fetches:
         fetch.start()
+    stage.need(tokens_ref)
     x = tokens_ref[...].astype(f32)
     scale = lax.rsqrt(jnp.mean(x * x, axis=-1, keepdims=True) + epsilon)
-    held_ref[me] = (x * scale * gain_ref[...]).astype(bf16)
+    held_ref[me] = (x * scale * gain_ref[...].reshape(1, -1)).astype(bf16)
     for fetch in fetches:
         fetch.wait()
 
@@ -243,7 +305,9 @@
     own[:QW, :] = half(query_held, QW)
     own[QW : QW + HEAD_DIM, :] = half(key_held, HEAD_DIM)
     own[QW + HEAD_DIM : HW, :] = half(value_held, HEAD_DIM)
-    own[HW:, :] = router_ref[...]
+    router = router_ref[...].astype(f32)
+    empty = jnp.zeros((ROUTER - router.shape[0], router.shape[1]), f32)
+    own[HW:, :] = jnp.concatenate([router, empty], axis=0).astype(bf16)
     met()
     spread = Spread(
         place, held_ref.at[me], lambda owner: held_ref.at[owner],
@@ -261,6 +325,7 @@
         others[-1].start()
     place_slots(routes_ref, order_ref, placed_ref)
     turned_ref[...] = placed_ref[...].reshape(EXP_WIN * CAP, -1).T
+    stage.put(placed_ref, turned_ref)
     spread.step1()
     spread.step2()
     spread.step3()
@@ -269,6 +334,8 @@
     for j, device in enumerate(place.layers()):
         others.append(remote(own_out, strips_ref.at[z], o_send.at[j], o_recv.at[j], device))
         others[-1].start()
+    stage.put(w_all_ref)
+    stage.need(cos_ref, sin_ref)
     depth = w_all_ref.shape[0]
     weights = Spread(
         place, w_all_ref.at[:, :FIRST], lambda owner: weights_ref.at[owner],
@@ -321,6 +388,7 @@
         return 0
 
     lax.fori_loop(0, GROUP, project, 0)
+    stage.put(qt_ref, kt_ref, vt_ref, k_ref, v_ref)
     weights.step3()
     for copy in sent:
         copy.wait_send()
@@ -343,25 +411,39 @@
     span = GROUP * rows
     strip = w_out.shape[0] // GROUP
     size = w_out.shape[0]
-    return pl.pallas_call(
+    return staged_call(
         project_kernel,
-        out_shape=(
-            shape((depth, ALL, size), bf16),
-            shape((QW, span), bf16),
-            shape((HEAD_DIM, span), bf16),
-            shape((HEAD_DIM, span), bf16),
-            shape((span, HEAD_DIM), bf16),
-            shape((span, HEAD_DIM), bf16),
-            shape((GROUP,) + docs.shape, jnp.int32),
-            shape((EXP_WIN, CAP, rows), bf16),
-            shape((rows, EXP_WIN * CAP), bf16),
-            shape((GROUP, rows, width), bf16),
-            shape((depth, strip, w_out.shape[1]), bf16),
-            shape((GROUP, depth, FIRST, size), bf16),
-        ),
-        in_specs=[IN_VMEM] * 8 + [IN_ANY] * 4,
-        out_specs=(IN_VMEM,) * 9 + (IN_ANY,) * 3,
-        scratch_shapes=[
+        "project",
+        1,
+        [
+            ("h", tokens),
+            ("v", gain),
+            ("v", router),
+            ("h", cosine),
+            ("h", sine),
+            ("v", docs),
+            ("v", routes),
+            ("v", order),
+            ("a", w_out),
+            ("a", w_query),
+            ("a", key_matrix),
+            ("a", value_matrix),
+        ],
+        [
+            ("h", shape((depth, ALL, size), bf16)),
+            ("h", shape((QW, span), bf16)),
+            ("h", shape((HEAD_DIM, span), bf16)),
+            ("h", shape((HEAD_DIM, span), bf16)),
+            ("h", shape((span, HEAD_DIM), bf16)),
+            ("h", shape((span, HEAD_DIM), bf16)),
+            ("v", shape((GROUP,) + docs.shape, jnp.int32)),
+            ("h", shape((EXP_WIN, CAP, rows), bf16)),
+            ("h", shape((rows, EXP_WIN * CAP), bf16)),
+            ("a", shape((GROUP, rows, width), bf16)),
+            ("a", shape((depth, strip, w_out.shape[1]), bf16)),
+            ("a", shape((GROUP, depth, FIRST, size), bf16)),
+        ],
+        [
             VMEM((GROUP, rows, width), bf16),
             VMEM((strip, width), bf16),
             VMEM((size, 2 * 128), bf16),
@@ -372,11 +454,6 @@
         + [DMA((GROUP - 1,))] * 2
         + [DMA((Spread.SEMS,))] * 4
         + [DMA((GROUP + 4,))],
-        compiler_params=params(1),
-        name="project",
-    )(
-        tokens, gain, router, cosine, sine, docs, routes, order, w_out, w_query, key_matrix,
-        value_matrix,
     )
 
 
@@ -385,7 +462,7 @@
 
 
 def attend_kernel(
-    n_blocks, qt_ref, k_ref, vt_ref, docs_ref, strips_ref, w_all_ref,
+    n_blocks, stage, qt_ref, k_ref, vt_ref, docs_ref, strips_ref, w_all_ref,
     o_ref, lse_ref, attended_ref, out_weight_ref, weights_ref,
     staged_ref, docs_col_ref, top_ref, sum_ref, acc_ref,
     a_send, a_recv, s_send, s_recv, w_send, w_recv, local,
@@ -416,10 +493,12 @@
         return 0
 
     lax.fori_loop(0, n_blocks, turn, 0)
+    stage.need(strips_ref, w_all_ref)
     met()
     spreads[0].start()
     for move in moves:
         move.start()
+    stage.need(qt_ref, k_ref, vt_ref)
 
     def tile(kb, qb, mask):
         kt = k_ref[block(kb), :]
@@ -494,6 +573,7 @@
         return 0
 
     lax.fori_loop(0, GROUP, q_block, 0)
+    stage.put(o_ref, lse_ref)
     own = pltpu.make_async_copy(staged_ref.at[me], attended_ref.at[me], local.at[2])
     own.start()
     spreads[1].step1()
@@ -514,18 +594,26 @@
     n = k.shape[0] // TOK_DEV
     span = qt.shape[1]
     depth, _, size = w_all.shape
-    return pl.pallas_call(
+    return staged_call(
         functools.partial(attend_kernel, n),
-        out_shape=(
-            shape((QW, span), f32),
-            shape((GROUP, 8, TOK_DEV), f32),
-            shape((GROUP, QW, TOK_DEV), bf16),
-            shape((depth, GROUP) + strips.shape[1:], bf16),
-            shape((GROUP, depth, HW - FIRST, size), bf16),
-        ),
-        in_specs=[IN_VMEM] * 6,
-        out_specs=(IN_VMEM, IN_VMEM, IN_ANY, IN_ANY, IN_ANY),
-        scratch_shapes=[
+        "attend",
+        2,
+        [
+            ("h", qt),
+            ("h", k),
+            ("h", vt),
+            ("v", docs),
+            ("h", strips),
+            ("h", w_all),
+        ],
+        [
+            ("h", shape((QW, span), f32)),
+            ("h", shape((GROUP, 8, TOK_DEV), f32)),
+            ("a", shape((GROUP, QW, TOK_DEV), bf16)),
+            ("a", shape((depth, GROUP) + strips.shape[1:], bf16)),
+            ("a", shape((GROUP, depth, HW - FIRST, size), bf16)),
+        ],
+        [
             VMEM((GROUP, QW, TOK_DEV), bf16),
             VMEM((n, TOK_DEV, 1), f32),
             VMEM((8, TOK_DEV), f32),
@@ -536,9 +624,7 @@
         ]
         + [DMA((Spread.SEMS,))] * 4
         + [DMA((3,))],
-        compiler_params=params(2),
-        name="attend",
-    )(qt, k, vt, docs, strips, w_all)
+    )
 
 
 def router_of(w_all_ref):
@@ -546,7 +632,7 @@
 
 
 def dispatch_kernel(
-    attended_ref, weight_ref, gate_up_ref, tokens_ref, gain_ref, w_all_ref, routes_ref, placed_ref,
+    stage, attended_ref, weight_ref, gate_up_ref, tokens_ref, gain_ref, w_all_ref, routes_ref, placed_ref,
     cotangent_ref,
     residual_ref, normed_ref, gates_ref, slot_gates_ref, rows_ref, grads_ref, gate_ref, up_ref,
     active_ref, grad_down_ref, columns_ref,
@@ -584,6 +670,7 @@
     own_strip.start()
     mixed_ref[...] = held_ref[...].reshape(width, rows).T
     fetches[1].wait()
+    stage.need(tokens_ref)
 
     def out_columns(i, _):
         columns = block(i)
@@ -595,7 +682,9 @@
     lax.fori_loop(0, width // TOK_DEV, out_columns, 0)
     residual = residual_ref[...]
     scale = lax.rsqrt(jnp.mean(residual * residual, axis=-1, keepdims=True) + epsilon)
-    normed_ref[...] = (residual * scale * gain_ref[...]).astype(bf16)
+    normed_ref[...] = (residual * scale * gain_ref[...].reshape(1, -1)).astype(bf16)
+    stage.put(residual_ref, normed_ref)
+    stage.need(w_all_ref)
     logits = None
     for s, router in enumerate(router_of(w_all_ref)):
         size = router.shape[1]
@@ -610,6 +699,7 @@
     gates = jnp.where(chosen, jnp.exp(logits - top), 0.0)
     gates = gates / jnp.sum(gates, axis=0, keepdims=True)
     gates_ref[...] = gates
+    stage.need(placed_ref, cotangent_ref)
     for e in range(EXP_WIN):
         slot_gates_ref[e] = jnp.sum(
             placed_ref[e].astype(f32) * gates[e : e + 1, :], axis=1, keepdims=True
@@ -638,11 +728,13 @@
 
     lax.fori_loop(1, GROUP + 1, send_rows, 0)
     lax.fori_loop(1, GROUP + 1, send_grads, 0)
+    stage.put(gates_ref, slot_gates_ref)
     rows_ref[me] = own_rows[me]
     grads_ref[me] = own_grads[me]
     fetches[2].wait()
     for j in range(1, GROUP):
         copy(own_rows, rows_ref, r_send, r_recv, j).wait_recv()
+    stage.put(rows_ref)
     slots = GROUP * CAP
     hidden = gate_ref.shape[1]
     tiles = hidden // TOK_DEV
@@ -657,8 +749,10 @@
         return 0
 
     lax.fori_loop(0, tiles, expert_up, 0)
+    stage.put(gate_ref, up_ref, active_ref)
     for j in range(1, GROUP):
         copy(own_grads, grads_ref, g_send, g_recv, j).wait_recv()
+    stage.put(grads_ref)
 
     def expert_over(i, _):
         grad_down_ref[:, block(i)] = dot(
@@ -667,6 +761,7 @@
         return 0
 
     lax.fori_loop(0, width // TOK_DEV, expert_over, 0)
+    stage.put(grad_down_ref)
     for j in range(1, GROUP):
         strip_copy(j).wait()
         copy(own_rows, rows_ref, r_send, r_recv, j).wait_send()
@@ -681,24 +776,35 @@
     slots = (GROUP, CAP, width)
     depth = w_all.shape[0]
     attended = attended.reshape(depth, GROUP, -1, rows)
-    return pl.pallas_call(
+    return staged_call(
         dispatch_kernel,
-        out_shape=(
-            shape((rows, width), f32),
-            shape((rows, width), bf16),
-            shape((ROUTER, rows), f32),
-            shape((EXP_WIN, CAP, 1), f32),
-            shape(slots, bf16),
-            shape(slots, bf16),
-            shape((count, hidden), f32),
-            shape((count, hidden), f32),
-            shape((count, hidden), bf16),
-            shape((hidden, width), bf16),
-            shape((GROUP, depth) + attended.shape[2:], bf16),
-        ),
-        in_specs=[IN_ANY] * 3 + [IN_VMEM] * 6,
-        out_specs=(IN_VMEM,) * 10 + (IN_ANY,),
-        scratch_shapes=[
+        "dispatch",
+        3,
+        [
+            ("a", attended),
+            ("a", weight),
+            ("a", gate_up),
+            ("h", tokens),
+            ("v", gain),
+            ("h", w_all),
+            ("v", routes),
+            ("h", placed),
+            ("h", cotangent),
+        ],
+        [
+            ("h", shape((rows, width), f32)),
+            ("h", shape((rows, width), bf16)),
+            ("h", shape((ROUTER, rows), f32)),
+            ("h", shape((EXP_WIN, CAP, 1), f32)),
+            ("h", shape(slots, bf16)),
+            ("h", shape(slots, bf16)),
+            ("h", shape((count, hidden), f32)),
+            ("h", shape((count, hidden), f32)),
+            ("h", shape((count, hidden), bf16)),
+            ("h", shape((hidden, width), bf16)),
+            ("a", shape((GROUP, depth) + attended.shape[2:], bf16)),
+        ],
+        [
             VMEM(attended.shape, bf16),
             VMEM(weight.shape, bf16),
             VMEM(gate_up.shape, bf16),
@@ -708,13 +814,11 @@
         ]
         + [DMA((GROUP,))] * 6
         + [DMA((4,))],
-        compiler_params=params(3),
-        name="dispatch",
-    )(attended, weight, gate_up, tokens, gain, w_all, routes, placed, cotangent)
+    )
 
 
 def expert_kernel(
-    active_ref, down_ref, grads_ref, rows_ref, gate_ref, up_ref, gate_up_ref,
+    stage, active_ref, down_ref, grads_ref, rows_ref, gate_ref, up_ref, gate_up_ref,
     out_ref, back_ref, grad_gate_up_ref,
     grads_held, rows_held, gate_up_held, own_ref, grad_ref, send, receive, local,
 ):
@@ -737,6 +841,8 @@
         to = lax.rem(me + j, GROUP)
         return remote(own_ref.at[to], out_ref.at[me], send.at[j], receive.at[j], place.ctx(to))
 
+    stage.need(active_ref, down_ref)
+
     def out(i, _):
         value = dot(active_ref[...], down_ref[:, block(i)]).astype(bf16)
         own_ref[:, :, block(i)] = value.reshape(GROUP, CAP, T)
@@ -749,6 +855,7 @@
     move = pltpu.make_async_copy(own_ref.at[me], out_ref.at[me], local.at[3])
     move.start()
     fetches[0].wait()
+    stage.need(gate_ref, up_ref)
 
     def back(i, _):
         grad = dot(grads_held[...], down_ref[block(i), :], ((1,), (1,)))
@@ -773,6 +880,7 @@
         return 0
 
     lax.fori_loop(0, width // T, over, 0)
+    stage.put(back_ref, grad_gate_up_ref)
     for j in range(1, GROUP):
         copy(j).wait()
     move.wait()
@@ -782,16 +890,25 @@
     count, width = rows.shape
     hidden = down.shape[0]
     slots = (GROUP, CAP, width)
-    return pl.pallas_call(
+    return staged_call(
         expert_kernel,
-        out_shape=(
-            shape(slots, bf16),
-            shape((count, width), bf16),
-            shape((width, 2 * hidden), bf16),
-        ),
-        in_specs=[IN_VMEM] * 2 + [IN_ANY] * 2 + [IN_VMEM] * 2 + [IN_ANY],
-        out_specs=(IN_ANY,) + (IN_VMEM,) * 2,
-        scratch_shapes=[
+        "expert",
+        7,
+        [
+            ("h", active),
+            ("h", down),
+            ("a", grads),
+            ("a", rows),
+            ("h", gate),
+            ("h", up),
+            ("a", gate_up),
+        ],
+        [
+            ("a", shape(slots, bf16)),
+            ("h", shape((count, width), bf16)),
+            ("h", shape((width, 2 * hidden), bf16)),
+        ],
+        [
             VMEM(grads.shape, bf16),
             VMEM(rows.shape, bf16),
             VMEM(gate_up.shape, bf16),
@@ -801,13 +918,11 @@
             DMA((GROUP,)),
             DMA((4,)),
         ],
-        compiler_params=params(7),
-        name="expert",
-    )(active, down, grads, rows, gate, up, gate_up)
+    )
 
 
 def combine_kernel(
-    out_ref, sent_grad_ref, weight_ref, residual_ref, normed_ref, gates_ref, placed_ref,
+    stage, out_ref, sent_grad_ref, weight_ref, residual_ref, normed_ref, gates_ref, placed_ref,
     placed_t_ref, slot_gates_ref, cotangent_ref, gain_ref, w_all_ref,
     output_ref, grad_residual_ref, heads_ref, attn_ref, grad_router_ref, grad_gain_ref,
     back_ref, weight_held, sum_ref, turned_ref, staged_ref, scaled_ref,
@@ -831,6 +946,7 @@
     move = pltpu.make_async_copy(sent_grad_ref.at[me], back_ref.at[me], local.at[1])
     move.start()
     turned_ref[...] = jnp.zeros_like(turned_ref)
+    stage.need(out_ref, placed_ref, slot_gates_ref, cotangent_ref)
 
     def add_expert(e, _):
         came = out_ref[e].astype(f32)
@@ -843,6 +959,7 @@
         return 0
 
     lax.fori_loop(0, EXP_WIN, add_expert, 0)
+    stage.need(placed_t_ref, residual_ref, gates_ref, w_all_ref, normed_ref)
     slots = EXP_WIN * CAP
 
     def mix(i, _):
@@ -852,6 +969,7 @@
         return 0
 
     lax.fori_loop(0, width // TOK_DEV, mix, 0)
+    stage.put(output_ref)
     gates = gates_ref[...]
     grad_gates = turned_ref[...]
     weighted = jnp.sum(gates * grad_gates, axis=0, keepdims=True)
@@ -876,13 +994,14 @@
     residual = residual_ref[...]
     grad_normed = sum_ref[...]
     scale = lax.rsqrt(jnp.mean(residual * residual, axis=-1, keepdims=True) + epsilon)
-    scaled = grad_normed * gain_ref[...]
+    scaled = grad_normed * gain_ref[...].reshape(1, -1)
     inner = jnp.mean(scaled * residual, axis=-1, keepdims=True)
     grad = scale * scaled - residual * (scale * scale * scale * inner)
     grad_gain_ref[...] = jnp.sum(grad_normed * residual * scale, axis=0, keepdims=True)
     grad_residual = cotangent_ref[...].astype(f32) + grad
     grad_residual_ref[...] = grad_residual
     attn_ref[...] = grad_residual.astype(bf16)
+    stage.put(grad_residual_ref, attn_ref, grad_router_ref, grad_gain_ref)
 
     def head_rows(j, _):
         to = lax.rem(me + j, GROUP)
@@ -910,19 +1029,33 @@
 ):
     rows, width = residual.shape
     slots = (GROUP, CAP, width)
-    return pl.pallas_call(
+    return staged_call(
         combine_kernel,
-        out_shape=(
-            shape((rows, width), bf16),
-            shape((rows, width), f32),
-            shape((GROUP, QW, rows), bf16),
-            shape((rows, width), bf16),
-            shape((ROUTER, width), f32),
-            shape((1, width), f32),
-        ),
-        in_specs=[IN_VMEM] + [IN_ANY] * 2 + [IN_VMEM] * 9,
-        out_specs=(IN_VMEM, IN_VMEM, IN_ANY, IN_VMEM, IN_VMEM, IN_VMEM),
-        scratch_shapes=[
+        "combine",
+        4,
+        [
+            ("h", out),
+            ("a", sent_grad),
+            ("a", weight),
+            ("h", residual),
+            ("h", normed),
+            ("h", gates),
+            ("h", placed),
+            ("h", placed_t),
+            ("h", slot_gates),
+            ("h", cotangent),
+            ("v", gain),
+            ("h", w_all),
+        ],
+        [
+            ("h", shape((rows, width), bf16)),
+            ("h", shape((rows, width), f32)),
+            ("a", shape((GROUP, QW, rows), bf16)),
+            ("h", shape((rows, width), bf16)),
+            ("h", shape((ROUTER, width), f32)),
+            ("h", shape((1, width), f32)),
+        ],
+        [
             VMEM(slots, bf16),
             VMEM(weight.shape, bf16),
             VMEM((rows, width), f32),
@@ -932,27 +1065,21 @@
         ]
         + [DMA((GROUP,))] * 4
         + [DMA((3,))],
-        compiler_params=params(4),
-        name="combine",
-    )(
-        out, sent_grad, weight, residual, normed, gates, placed, placed_t, slot_gates, cotangent,
-        gain, w_all,
     )
 
 
 def backward_kernel(
-    n_blocks, qt_ref, k_ref, kt_ref, v_ref, heads_ref, o_ref, lse_ref, docs_ref, attn_ref,
+    n_blocks, stage, qt_ref, k_ref, kt_ref, v_ref, heads_ref, o_ref, lse_ref, docs_ref, attn_ref,
     columns_ref, down_ref,
-    dq_ref, dk_ref, dv_ref, out_shard_ref, down_all_ref,
-    grad_out_ref, out_in, attn_all_ref, docs_col_ref, delta_ref, dk_acc, dv_acc, a_send, a_recv, e_send, e_recv, o_send, o_recv,
-    local,
+    dq_ref, dk_ref, dv_ref, grad_out_ref, down_all_ref,
+    attn_all_ref, docs_col_ref, delta_ref, dk_acc, dv_acc, a_send, a_recv, e_send, e_recv, local,
 ):
     T = TOK_DEV
     place = Place()
     me = place.me
     first = place.base
-    met = greet([place.ctx(i) for i in place.near] + place.layers())
-    z, layers = place.z, place.depth
+    met = greet([place.ctx(i) for i in place.near])
+    stage.need(attn_ref)
     move = pltpu.make_async_copy(attn_ref, attn_all_ref.at[me], local.at[0])
     move.start()
     spread = Spread(
@@ -962,6 +1089,7 @@
     met()
     spread.start()
     down_move = pltpu.make_async_copy(down_ref, down_all_ref.at[me], local.at[1])
+    stage.need(down_ref)
     down_move.start()
     down_spread = Spread(
         place, down_ref, lambda owner: down_all_ref.at[owner],
@@ -975,6 +1103,8 @@
     lax.fori_loop(0, n_blocks, turn, 0)
     heads = range(HEADS)
     parts = [slice(h * HEAD_DIM, (h + 1) * HEAD_DIM) for h in heads]
+
+    stage.need(heads_ref, o_ref, lse_ref, qt_ref, k_ref, kt_ref, v_ref, columns_ref)
 
     def prepare(i, _):
         for h in heads:
@@ -1009,12 +1139,6 @@
 
     depth, strip, width = grad_out_ref.shape
 
-    def down_copy(j):
-        to = lax.rem(z + j, layers)
-        return remote(
-            grad_out_ref.at[to], out_in.at[z], o_send.at[j], o_recv.at[j], place.fsdp(to)
-        )
-
     def out_weights():
         move.wait()
         spread.last()
@@ -1028,8 +1152,6 @@
             return 0
 
         lax.fori_loop(0, width // T, columns, 0)
-        for j in range(1, layers):
-            down_copy(j).start()
 
     def k_block(kb, _):
         for at, act in (
@@ -1073,15 +1195,9 @@
         return 0
 
     lax.fori_loop(first + GROUP, n_blocks, clear, 0)
+    stage.put(dq_ref, dk_ref, dv_ref, grad_out_ref)
     down_spread.step2()
     down_spread.step3()
-    for j in range(1, layers):
-        down_copy(j).wait()
-    out_in[z] = grad_out_ref[z]
-    total = out_in[0].astype(f32)
-    for s in range(1, layers):
-        total = total + out_in[s].astype(f32)
-    out_shard_ref[...] = total.astype(bf16)
     down_spread.last()
     down_spread.sent()
     down_move.wait()
@@ -1093,20 +1209,31 @@
     span = qt.shape[1]
     rows, width = attn.shape
     _, depth, strip, _ = columns.shape
-    return pl.pallas_call(
+    return staged_call(
         functools.partial(backward_kernel, n),
-        out_shape=(
-            shape((QW, span), f32),
-            shape(kt.shape, f32),
-            shape(kt.shape, f32),
-            shape((strip, width), bf16),
-            shape((GROUP,) + down.shape, bf16),
-        ),
-        in_specs=[IN_VMEM] * 11,
-        out_specs=(IN_VMEM,) * 4 + (IN_ANY,),
-        scratch_shapes=[
-            VMEM((depth, strip, width), bf16),
-            VMEM((depth, strip, width), bf16),
+        "backward",
+        5,
+        [
+            ("h", qt),
+            ("h", k),
+            ("h", kt),
+            ("h", v),
+            ("h", heads),
+            ("h", o),
+            ("h", lse),
+            ("v", docs),
+            ("h", attn),
+            ("h", columns),
+            ("h", down),
+        ],
+        [
+            ("h", shape((QW, span), f32)),
+            ("h", shape(kt.shape, f32)),
+            ("h", shape(kt.shape, f32)),
+            ("h", shape((depth, strip, width), bf16)),
+            ("a", shape((GROUP,) + down.shape, bf16)),
+        ],
+        [
             VMEM((GROUP, rows, width), bf16),
             VMEM((n, TOK_DEV, 1), f32),
             VMEM((GROUP, 8, TOK_DEV), f32),
@@ -1114,21 +1241,18 @@
             VMEM((TOK_DEV, HEAD_DIM), f32),
         ]
         + [DMA((Spread.SEMS,))] * 4
-        + [DMA((depth,))] * 2
         + [DMA((2,))],
-        compiler_params=params(5),
-        name="backward",
-    )(qt, k, kt, v, heads, o, lse, docs, attn, columns, down)
+    )
 
 
 def finish_kernel(
-    normed_ref, first_ref, others_ref, gate_up_ref, out_shard_ref, dq_ref, dk_ref, dv_ref, cos_ref,
+    stage, normed_ref, first_ref, others_ref, gate_up_ref, grad_out_ref, dq_ref, dk_ref, dv_ref, cos_ref,
     sin_ref, tokens_ref, gain_ref, grad_residual_ref, grad_router_ref, grad_gain2_ref,
     input_grad_ref, shared_ref, small_all_ref, out_all_ref, gate_up_all_ref,
     normed_held, first_held, others_held, linear_ref, came_ref, first_t, others_t, sum_ref, part_ref,
-    small_ref, head_in, small_in, shard_ref, small_shard_ref,
-    g_send, g_recv, h_send, h_recv, s_send, s_recv, e_send, e_recv, f_send, f_recv, m_send, m_recv,
-    c_send, c_recv, local,
+    small_ref, head_in, small_in, out_in, shard_ref, small_shard_ref, out_shard_ref,
+    g_send, g_recv, h_send, h_recv, s_send, s_recv, o_send, o_recv, e_send, e_recv, f_send, f_recv,
+    m_send, m_recv, c_send, c_recv, local,
 ):
     place = Place()
     me, z, depth = place.me, place.z, place.depth
@@ -1158,8 +1282,8 @@
         pltpu.make_async_copy(shard_ref, shared_ref.at[me], local.at[5]),
         pltpu.make_async_copy(small_shard_ref, small_all_ref.at[me], local.at[6]),
     ]
+    stage.need(gate_up_ref)
     moves[0].start()
-    moves[1].start()
 
     def copy(j):
         to = lax.rem(me + j, GROUP)
@@ -1170,6 +1294,8 @@
     def down(source, target, send, receive, j):
         to = lax.rem(z + j, depth)
         return remote(source.at[to], target.at[z], send.at[j], receive.at[j], place.fsdp(to))
+
+    stage.need(dq_ref, dk_ref, dv_ref, cos_ref, sin_ref)
 
     def turn_back(j, _):
         to = lax.rem(me + j, GROUP)
@@ -1188,8 +1314,12 @@
         return 0
 
     lax.fori_loop(1, GROUP + 1, turn_back, 0)
+    stage.need(grad_out_ref)
+    outs = [down(grad_out_ref, out_in, o_send, o_recv, j) for j in range(1, depth)]
+    for one in outs:
+        one.start()
+    out_in[z] = grad_out_ref[z]
     came_ref[me] = linear_ref[me]
-    out_spread.start()
     fetches[0].wait()
 
     def own_weights(j, _):
@@ -1208,9 +1338,21 @@
         return 0
 
     lax.fori_loop(1, depth + 1, own_weights, 0)
+
+    def total(ref):
+        value = ref[0].astype(f32)
+        for s in range(1, depth):
+            value = value + ref[s].astype(f32)
+        return value.astype(bf16)
+
     for j in range(1, GROUP):
         copy(j).wait_send()
     expert_spread.start()
+    for one in outs:
+        one.wait_recv()
+    out_shard_ref[...] = total(out_in)
+    out_spread.start()
+    moves[1].start()
     fetches[1].wait()
     fetches[2].wait()
     for j in range(1, GROUP):
@@ -1233,13 +1375,15 @@
 
     lax.fori_loop(0, depth, add_heads, 0)
     out_spread.step1()
+    stage.need(tokens_ref, grad_residual_ref, grad_router_ref, grad_gain2_ref)
     x = tokens_ref[...].astype(f32)
     grad_normed = sum_ref[...]
     scale = lax.rsqrt(jnp.mean(x * x, axis=-1, keepdims=True) + epsilon)
-    scaled = grad_normed * gain_ref[...]
+    scaled = grad_normed * gain_ref[...].reshape(1, -1)
     inner = jnp.mean(scaled * x, axis=-1, keepdims=True)
     grad = scale * scaled - x * (scale * scale * scale * inner)
     input_grad_ref[...] = grad_residual_ref[...] + grad
+    stage.put(input_grad_ref)
     gain1 = jnp.sum(grad_normed * x * scale, axis=0, keepdims=True)
     row = lax.broadcasted_iota(jnp.int32, (ROUTER, width), 0)
     small = jnp.where(row == ROUTER - 2, gain1, grad_router_ref[...])
@@ -1253,12 +1397,6 @@
     expert_spread.step1()
     head_in[z] = part_ref[z]
     small_in[z] = small_ref[z]
-
-    def total(ref):
-        value = ref[0].astype(f32)
-        for s in range(1, depth):
-            value = value + ref[s].astype(f32)
-        return value.astype(bf16)
 
     for one in heads:
         one.wait_recv()
@@ -1284,30 +1422,48 @@
     for spread in (out_spread, expert_spread, head_spread, small_spread):
         spread.last()
         spread.sent()
-    for one in heads + smalls:
+    for one in heads + smalls + outs:
         one.wait_send()
     for move in moves:
         move.wait()
 
 
 def finish_call(
-    normed, first, others, gate_up, out_shard, dq, dk, dv, cosine, sine, tokens, gain, grad_residual,
-    grad_router, grad_gain2, depth,
+    normed, first, others, gate_up, grad_out, dq, dk, dv, cosine, sine, tokens, gain, grad_residual,
+    grad_router, grad_gain2,
 ):
     rows, width = tokens.shape
+    depth, strip, _ = grad_out.shape
     size = width // depth
-    return pl.pallas_call(
+    return staged_call(
         finish_kernel,
-        out_shape=(
-            shape((rows, width), f32),
-            shape((GROUP, HW, size), bf16),
-            shape((GROUP, ROUTER, size), bf16),
-            shape((GROUP,) + out_shard.shape, bf16),
-            shape((GROUP,) + gate_up.shape, bf16),
-        ),
-        in_specs=[IN_ANY] * 3 + [IN_VMEM] * 12,
-        out_specs=(IN_VMEM,) + (IN_ANY,) * 4,
-        scratch_shapes=[
+        "finish",
+        6,
+        [
+            ("a", normed),
+            ("a", first),
+            ("a", others),
+            ("h", gate_up),
+            ("h", grad_out),
+            ("h", dq),
+            ("h", dk),
+            ("h", dv),
+            ("h", cosine),
+            ("h", sine),
+            ("h", tokens),
+            ("v", gain),
+            ("h", grad_residual),
+            ("h", grad_router),
+            ("h", grad_gain2),
+        ],
+        [
+            ("h", shape((rows, width), f32)),
+            ("a", shape((GROUP, HW, size), bf16)),
+            ("a", shape((GROUP, ROUTER, size), bf16)),
+            ("a", shape((GROUP, strip, width), bf16)),
+            ("a", shape((GROUP,) + gate_up.shape, bf16)),
+        ],
+        [
             VMEM(normed.shape, bf16),
             VMEM(first.shape, bf16),
             VMEM(others.shape, bf16),
@@ -1320,25 +1476,22 @@
             VMEM((depth, ROUTER, size), bf16),
             VMEM((depth, HW, size), bf16),
             VMEM((depth, ROUTER, size), bf16),
+            VMEM((depth, strip, width), bf16),
             VMEM((HW, size), bf16),
             VMEM((ROUTER, size), bf16),
+            VMEM((strip, width), bf16),
         ]
         + [DMA((GROUP,))] * 2
-        + [DMA((depth,))] * 4
+        + [DMA((depth,))] * 6
         + [DMA((Spread.SEMS,))] * 8
         + [DMA((7,))],
-        compiler_params=params(6),
-        name="finish",
-    )(
-        normed, first, others, gate_up, out_shard, dq, dk, dv, cosine, sine, tokens, gain,
-        grad_residual, grad_router, grad_gain2,
     )
 
 
 def output_kernel(
-    shared_ref, small_ref, out_ref, gate_up_ref, output_ref, input_grad_ref,
-    q_ref, k_ref, v_ref, w_out_ref, router_ref, gain1_ref, gain2_ref, gate_ref, up_ref, final_ref,
-    final_grad_ref, sum_ref,
+    shared_ref, small_ref, out_ref, gate_up_ref, down_ref, output_ref, input_grad_ref,
+    q_ref, k_ref, v_ref, w_out_ref, router_ref, gain1_ref, gain2_ref, gate_ref, up_ref, w_down_ref,
+    final_ref, final_grad_ref,
 ):
     pair, i = shared_ref.shape[0], pl.program_id(0)
     hidden = gate_ref.shape[2]
@@ -1347,49 +1500,47 @@
         both = [shared_ref[p, first:last, :].astype(f32) for p in range(pair)]
         return jnp.concatenate(both, axis=0).T
 
-    q_ref[...] = rows(0, QW)
-    k_ref[...] = rows(QW, QW + HEAD_DIM)
-    v_ref[...] = rows(QW + HEAD_DIM, HW)
+    @pl.when(lax.rem(i, pair) == 0)
+    def _():
+        q_ref[...] = rows(0, QW)
+        k_ref[...] = rows(QW, QW + HEAD_DIM)
+        v_ref[...] = rows(QW + HEAD_DIM, HW)
+
     w_out_ref[...] = out_ref[...].astype(f32)
+    gate_ref[...] = gate_up_ref[:, :, :hidden].astype(f32)
+    up_ref[...] = gate_up_ref[:, :, hidden:].astype(f32)
+    w_down_ref[...] = down_ref[...].astype(f32)
     final_ref[...] = output_ref[...]
     final_grad_ref[...] = input_grad_ref[...]
-    gate_ref[...] = gate_up_ref[:, :, :hidden].astype(f32)
-    up_ref[...] = gate_up_ref[:, :, hidden:].astype(f32)
 
     @pl.when(i == 0)
     def _():
-        sum_ref[...] = jnp.zeros_like(sum_ref)
-
-    for p in range(pair):
-        sum_ref[...] += small_ref[p].astype(f32)
-
-    @pl.when(i == pl.num_programs(0) - 1)
-    def _():
-        router_ref[...] = sum_ref[: router_ref.shape[0], :]
-        gain1_ref[...] = sum_ref[ROUTER - 2, :]
-        gain2_ref[...] = sum_ref[ROUTER - 1, :]
-
-
-def output_call(shared, small, out, gate_up, output, input_grad, experts):
+        total = jnp.sum(small_ref[...].astype(f32), axis=0)
+        router_ref[...] = total[: router_ref.shape[0], :]
+        gain1_ref[...] = total[ROUTER - 2, :]
+        gain2_ref[...] = total[ROUTER - 1, :]
+
+
+def output_call(shared, small, out, gate_up, down, output, input_grad, experts):
     count, _, size = shared.shape
     _, strip, width = out.shape
     hidden = gate_up.shape[2] // 2
     pair = 2
-    rows = output.shape[0] // (count // pair)
+    rows = output.shape[0] // count
     token = pl.BlockSpec((rows, width), lambda i: (i, 0))
 
     def first(*dims):
-        return pl.BlockSpec((pair,) + dims, lambda i: (i,) + (0,) * len(dims))
+        return pl.BlockSpec((1,) + dims, lambda i: (i,) + (0,) * len(dims))
 
     def columns(columns):
-        return pl.BlockSpec((size, columns), lambda i: (0, i))
+        return pl.BlockSpec((size, columns), lambda i: (0, i // pair))
 
     def whole(*dims):
         return pl.BlockSpec(dims, lambda i: (0,) * len(dims))
 
     return pl.pallas_call(
         output_kernel,
-        grid=(count // pair,),
+        grid=(count,),
         out_shape=(
             shape((size, count * QW), f32),
             shape((size, count * HEAD_DIM), f32),
@@ -1400,12 +1551,14 @@
             shape((size,), f32),
             shape((count, size, hidden), f32),
             shape((count, size, hidden), f32),
+            shape(down.shape, f32),
             shape(output.shape, bf16),
             shape(input_grad.shape, f32),
         ),
         in_specs=[
-            first(*shared.shape[1:]), first(*small.shape[1:]), first(strip, width),
-            first(*gate_up.shape[1:]), token, token,
+            pl.BlockSpec((pair,) + shared.shape[1:], lambda i: (i // pair, 0, 0)),
+            whole(*small.shape), first(strip, width), first(*gate_up.shape[1:]),
+            first(*down.shape[1:]), token, token,
         ],
         out_specs=(
             columns(pair * QW),
@@ -1417,13 +1570,13 @@
             whole(size),
             first(size, hidden),
             first(size, hidden),
+            first(*down.shape[1:]),
             token,
             token,
         ),
-        scratch_shapes=[VMEM((ROUTER, size), f32)],
         compiler_params=params(),
         name="output",
-    )(shared, small, out, gate_up, output, input_grad)
+    )(shared, small, out, gate_up, down, output, input_grad)
 
 
 def rotary_tables(length):
@@ -1474,14 +1627,13 @@
         cosine = lax.dynamic_slice_in_dim(cosine, part * span, span, 1)
         sine = lax.dynamic_slice_in_dim(sine, part * span, span, 1)
     own_tokens, own_cotangent = tokens[0], cotangent[0]
-    gain1, gain2 = norm1_gain[None, :], norm2_gain[None, :]
 
     route_rows, order_rows = routes[0].T, slot_order[0].T
     (
         w_all, queries, keys_t, values_t, keys, values, docs, placed, placed_t, normed1, strips,
         first_all,
     ) = project_call(
-        own_tokens, gain1, jnp.pad(w_router.T, ((0, ROUTER - experts), (0, 0))), cosine, sine, doc_ids,
+        own_tokens, norm1_gain, w_router.T, cosine, sine, doc_ids,
         route_rows, order_rows, w_out, w_query, key_matrix, value_matrix, depth,
     )
     w_gate, w_up, w_down, docs = lax.optimization_barrier((w_gate, w_up, w_down, docs))
@@ -1510,7 +1662,7 @@
         residual, normed2, gates, slot_gates, sent_rows, sent_grads, gate, up, active, grad_w_down,
         columns,
     ) = dispatch_call(
-        attended, out_weight, gate_up, own_tokens, gain2, w_all, route_rows, placed, own_cotangent
+        attended, out_weight, gate_up, own_tokens, norm2_gain, w_all, route_rows, placed, own_cotangent
     )
     grad_w_down = reduce_z(grad_w_down)
     expert_out, grad_buffer, grad_w_gate_up = expert_call(
@@ -1520,27 +1672,25 @@
     grad_w_gate_up = reduce_z(grad_w_gate_up)
     output, grad_residual, heads, attn, grad_router, grad_gain2 = combine_call(
         expert_out, grad_buffer.reshape(sent_rows.shape), out_weight,
-        residual, normed2, gates, placed, placed_t, slot_gates, own_cotangent, gain2, w_all,
-    )
-    dq, dk, dv, out_shard, down_w = backward_call(
+        residual, normed2, gates, placed, placed_t, slot_gates, own_cotangent, norm2_gain, w_all,
+    )
+    dq, dk, dv, grad_out, down_w = backward_call(
         queries, keys, keys_t, values, heads, attended_f32, log_total, docs, attn, columns,
         grad_w_down,
     )
     if parts > 1:
         dk = lax.psum_scatter(dk, "ctx", scatter_dimension=1, axis_index_groups=far, tiled=True)
         dv = lax.psum_scatter(dv, "ctx", scatter_dimension=1, axis_index_groups=far, tiled=True)
+    input_grad, shared, small, out_w, gate_up_w = finish_call(
+        normed1, first_all, others_all, grad_w_gate_up, grad_out, dq, dk, dv, cosine, sine,
+        own_tokens, norm1_gain, grad_residual, grad_router, grad_gain2,
+    )
     if parts > 1:
-        out_shard = lax.psum(out_shard, "ctx", axis_index_groups=far)
-    input_grad, shared, small, out_w, gate_up_w = finish_call(
-        normed1, first_all, others_all, grad_w_gate_up, out_shard, dq, dk, dv, cosine, sine,
-        own_tokens, gain1, grad_residual, grad_router, grad_gain2, depth,
-    )
-    if parts > 1:
-        shared, small = lax.psum((shared, small), "ctx", axis_index_groups=far)
-
-    q_w, k_w, v_w, out_w, router_w, gain1_w, gain2_w, gate_w, up_w, output, input_grad = output_call(
-        shared, small, out_w, gate_up_w, output, input_grad, experts
-    )
+        shared, small, out_w = lax.psum((shared, small, out_w), "ctx", axis_index_groups=far)
+
+    (
+        q_w, k_w, v_w, out_w, router_w, gain1_w, gain2_w, gate_w, up_w, down_w, output, input_grad
+    ) = output_call(shared, small, out_w, gate_up_w, down_w, output, input_grad, experts)
     return (
         output[None],
         input_grad[None],
@@ -1553,7 +1703,7 @@
         router_w.T,
         gate_w,
         up_w,
-        down_w.astype(f32),
+        down_w,
     )
 
 

time: 387 us -> 358 us (0.925)
  Pallas kernels: 358 us -> 335 us
  other arithmetic: 6.45 us -> 0.99 us
    pallas_call x8, Pallas kernels: 358 us -> 335 us  [the longest x7 319 us: staged_call(): pl.pallas_call(kernel, out_shape=tuple((one for _, one in outs)), in_spec...]
    convert_element_type x1 -> x0, other arithmetic: 5.46 us -> none  [shards(): down_w.astype(f32)]
  transfers between devices with their start and end apart: 4 -> 4, of which waited for: 1 -> 1; matrix products, arithmetic and copies ran while one was open for 2% -> 0% of each run, Pallas kernels for 59% -> 58%
where the time goes in v2:
time: 358 us; the launch traced here: 357 us
  Pallas kernels  335 us (94%)
  between operations  13.9 us (4%)
  waiting for transfers between devices  5.41 us (2%)
    pallas_call x7, Pallas kernels, staged_call(): pl.pallas_call(kernel, out_shape=tuple((one for _, one in outs)), in_spec...  319 us
    pallas_call x1, Pallas kernels, output_call(): pl.pallas_call(output_kernel, grid=(count,), out_shape=(shape((size, coun...  16.2 us
  transfers between devices with their start and end apart: 4, of which 1 were waited for; matrix products, arithmetic and copies ran while one was open for 0% of the time, Pallas kernels for 58%

profile of v2, /device:TPU:0, one launch (start us, length us, event | category | flops | bytes accessed | tf_op | source)
XLA Modules:
  0.0 357.3 jit_solution(17925209575303938245)
XLA Ops:
  7.2 0.0 copy-start
  7.2 0.0 all-gather.4.cloned.1.call-start
  7.3 47.3 %project.1 = (bf16[4,368,384]{2,1,0:T(8,128)(2,1)}, bf16[192,2048]{1,0:T(8,128)(2,1)}, bf16[64,2048]{1,0:T(8,128)(2,1)}, bf16[64,2048]{1,0:T(8,128)(2,1)}, bf16[...) custom-call(bf16[256,1536]{1,0:T(8,128)(2,1)} %bitcast.25, ...), custom_call_target="tpu_custom_call" | custom-call | tf_op jit(solution)/shard_map/project/pallas_call | solution.py:104
  54.6 1.2 dynamic-slice_bitcast_fusion
  55.7 1.0 pad_maximum_fusion
  56.7 0.0 all-gather.4.cloned.1.call-update
  56.8 0.0 all-gather.6.cloned.1.call-start
  56.8 0.8 constant_dynamic-slice_fusion
  57.6 0.0 all-gather.6.cloned.1.call-update
  57.6 0.0 reduce-scatter.5.cloned.1.call-start
  57.7 57.3 %attend.1 = (f32[192,2048]{1,0:T(8,128)}, f32[8,8,256]{2,1,0:T(8,128)}, bf16[8,192,256]{2,1,0:T(8,128)(2,1)}, bf16[4,8,48,1536]{3,2,1,0:T(8,128)(2,1)}, bf16[8,4,224,384]{3,2,1,0:T(8,128)(2,1)}) custom-call(bf16[192,2048]{1,0:T(8,128)(2,1)} %get-tuple-element.77.refs_0_, bf16[2048,64]{1,0:T(8,128)(2,1)} %get-tuple-element.78.refs_1_, ...), custom_call_target="tpu_custom_call" | custom-call | tf_op jit(solution)/shard_map/attend/pallas_call | solution.py:104
  115.0 5.3 %all-gather.4.cloned.1.call-done.refs_2_.refs_6_ = bf16[1536,1024]{1,0:T(8,128)(2,1)} async-done(((bf16[384,1024]{1,0:T(8,128)(2,1)}), bf16[1536,1024]{1,0:T(8,128)(2,1)}) %all-gather.4.cloned.1.call-update) | async-done | bytes 3145744 | tf_op jit(solution)/shard_map/all_gather | solution.py:1617
  120.2 47.9 %dispatch.1 = (f32[256,1536]{1,0:T(8,128)}, bf16[256,1536]{1,0:T(8,128)(2,1)}, f32[48,256]{1,0:T(8,128)}, f32[8,64,1]{2,1,0:T(8,128)}, bf16[8,64,1536]{2,1,0:T(8...) custom-call(bf16[4,8,48,256]{3,2,1,0:T(8,128)(2,1)} %bitcast.34, ...), custom_call_target="tpu_custom_call" | custom-call | tf_op jit(solution)/shard_map/dispatch/pallas_call | solution.py:104
  168.2 0.0 reduce-scatter.5.cloned.1.call-update
  168.2 0.0 reduce-scatter.3.cloned.1.call-start
  168.2 0.0 all-gather.6.cloned.1.call-done
  168.3 22.7 %expert.1 = (bf16[8,64,1536]{2,1,0:T(8,128)(2,1)}, bf16[512,1536]{1,0:T(8,128)(2,1)}, bf16[1536,1024]{1,0:T(8,128)(2,1)}) custom-call(bf16[512,512]{1,0:T(8,128)(2,1)} %get-tuple-element.90.refs_0_, bf16[512,1536]{1,0:T(8,128)(2,1)} %bitcast.30, bf16[512,1536]{1,0:T(8,128)(2,1)} %bitcast.32, bf16[512,1536]{1,0:T(8,128)(2,1)} %bitcast.31, ...), custom_call_target="tpu_custom_call" | custom-call | tf_op jit(solution)/shard_map/expert/pallas_call | solution.py:104
  191.0 0.0 reduce-scatter.3.cloned.1.call-update
  191.0 33.5 %combine.1 = (bf16[256,1536]{1,0:T(8,128)(2,1)}, f32[256,1536]{1,0:T(8,128)}, bf16[8,192,256]{2,1,0:T(8,128)(2,1)}, bf16[256,1536]{1,0:T(8,128)(2,1)}, f32[48,1536]{1,0:T(8,128)}, /*index=5*/f32[1,1536]{1,0:T(1,128)}) custom-call(bf16[8,64,1536]{2,1,0:T(8,128)(2,1)} %get-tuple-element.99.refs_0_, bf16[8,64,1536]{2,1,0:T(8,128)(2,1)} %bitcast.33, ...), custom_call_target="tpu_custom_call" | custom-call | tf_op jit(solution)/shard_map/combine/pallas_call | solution.py:104
  224.5 0.0 reduce-scatter.5.cloned.1.call-done.refs_10_
  224.6 45.9 %backward.1 = (f32[192,2048]{1,0:T(8,128)}, f32[64,2048]{1,0:T(8,128)}, f32[64,2048]{1,0:T(8,128)}, bf16[4,48,1536]{2,1,0:T(8,128)(2,1)}, bf16[8,128,1536]{2,1,0:T(8,128)(2,1)}) custom-call(bf16[192,2048]{1,0:T(8,128)(2,1)} %get-tuple-element.77.refs_0_, bf16[2048,64]{1,0:T(8,128)(2,1)} %get-tuple-element.78.refs_1_, ...), custom_call_target="tpu_custom_call" | custom-call | tf_op jit(solution)/shard_map/backward/pallas_call | solution.py:104
  270.4 0.0 reduce-scatter.3.cloned.1.call-done.refs_3_
  270.5 64.1 %finish.1 = (f32[256,1536]{1,0:T(8,128)}, bf16[8,320,384]{2,1,0:T(8,128)(2,1)}, bf16[8,48,384]{2,1,0:T(8,128)(2,1)}, bf16[8,48,1536]{2,1,0:T(8,128)(2,1)}, bf16[8,384,1024]{2,1,0:T(8,128)(2,1)}) custom-call(bf16[8,256,1536]{2,1,0:T(8,128)(2,1)} %get-tuple-element.75.refs_0_, bf16[8,4,96,384]{3,2,1,0:T(8,128)(2,1)} %get-tuple-element.76.refs_1_, ...), custom_call_target="tpu_custom_call" | custom-call | tf_op jit(solution)/shard_map/finish/pallas_call | solution.py:104
  334.6 16.2 %output.1 = (f32[384,1536]{1,0:T(8,128)}, f32[384,512]{1,0:T(8,128)}, f32[384,512]{1,0:T(8,128)}, f32[8,48,1536]{2,1,0:T(8,128)}, f32[40,384]{1,0:T(8,128)}, /*i...) custom-call(bf16[8,320,384]{2,1,0:T(8,128)(2,1)} %get-tuple-element., ...), custom_call_target="tpu_custom_call" | custom-call | tf_op jit(solution)/shard_map/output/pallas_call | solution.py:1541
  (3 shorter events, 0.0 us)
Async XLA Ops:
  7.2 49.6 %copy-start = (bf16[8,128,1536]{2,1,0:T(8,128)(2,1)S(1)}, bf16[8,128,1536]{2,1,0:T(8,128)(2,1)}, u32[]{:S(2)}) copy-start(bf16[8,128,1536]{2,1,0:T(8,128)(2,1)} %param.30) | copy-start | bytes 9437188
  7.2 113.0 %all-gather.4.cloned.1.call-start = ((), (), s32[]{:S(2)}) async-start(), calls=%async_computation.2 | async-start | bytes 3932160 | tf_op jit(solution)/shard_map/all_gather | solution.py:1617
  56.8 111.5 %all-gather.6.cloned.1.call-start = ((), (), s32[]{:S(2)}) async-start(), calls=%async_computation.5 | async-start | bytes 1966080 | tf_op jit(solution)/shard_map/all_gather | solution.py:1617
  57.6 166.9 %reduce-scatter.5.cloned.1.call-start = ((), (), s32[]{:S(2)}) async-start(), calls=%async_computation.4 | async-start | bytes 1966080 | tf_op jit(solution)/shard_map/reduce_scatter | solution.py:1620
  168.2 102.3 %reduce-scatter.3.cloned.1.call-start = ((), (), s32[]{:S(2)}) async-start(), calls=%async_computation.3 | async-start | bytes 3932160 | tf_op jit(solution)/shard_map/reduce_scatter | solution.py:1620
  334.6 16.2 %copy-start.1 = (bf16[8,128,1536]{2,1,0:T(8,128)(2,1)S(1)}, bf16[8,128,1536]{2,1,0:T(8,128)(2,1)}, u32[]{:S(2)}) copy-start(bf16[8,128,1536]{2,1,0:T(8,128)(2,1)} %param.30) | copy-start | bytes 9437188
Sparse Core Ops, SparseCore 0:
  56.9 63.3 all-gather.3
  122.4 35.7 all-gather.5
  168.3 36.4 reduce-scatter.4
  207.0 59.2 reduce-scatter.2

commit v3 on v2

--- a/solution.py
+++ b/solution.py
@@ -21,8 +21,8 @@
 HW = QW + 2 * HEAD_DIM
 ROUTER = 48
 ALL = HW + ROUTER
-FIRST = 96
-
+
+NEVER = 4096.0
 epsilon = 1e-06
 score_masked = -1e30
 bf16 = jnp.bfloat16
@@ -226,16 +226,46 @@
         self.wait(4, 5, 6, 7, 8, 9, 12, 13)
 
 
-NEVER = 4096.0
-
-
-def turned(values, cosine, sine):
-    half = HEAD_DIM // 2
-    out = []
-    for at in range(0, values.shape[0], HEAD_DIM):
-        low, high = values[at : at + half], values[at + half : at + HEAD_DIM]
-        out += [low * cosine - high * sine, high * cosine + low * sine]
-    return jnp.concatenate(out, axis=0)
+class Line:
+    def __init__(self, place, land, send, receive):
+        self.z, self.depth = place.z, place.depth
+        z, most = self.z, place.depth - 1
+        ways = ((jnp.minimum(z + 1, most), -1), (jnp.maximum(z - 1, 0), 1))
+        self.copies = []
+        for way, (device, sign) in enumerate(ways):
+            self.copies.append([])
+            for step in range(most):
+                held = land(jnp.clip(z + sign * step, 0, most))
+                self.copies[way].append(
+                    remote(
+                        held, held, send.at[way, step], receive.at[way, step], place.fsdp(device)
+                    )
+                )
+
+    def each(self, step):
+        z, most = self.z, self.depth - 1
+        up, down = self.copies
+        at = min(step, most - 1)
+        return ((z + 1 <= most, z - step >= 0, up[at]), (z - 1 >= 0, z + step <= most, down[at]))
+
+    def start(self):
+        for open_way, _, copy in self.each(0):
+            pl.when(open_way)(copy.start)
+
+    def step(self, step):
+        before = self.each(step - 1)
+        for (open_way, here, copy), (_, _, came) in zip(self.each(step), before):
+            pl.when(here)(came.wait_recv)
+            if step < self.depth - 1:
+                pl.when(jnp.logical_and(open_way, here))(copy.start)
+
+    def last(self):
+        self.step(self.depth - 1)
+
+    def sent(self):
+        for step in range(self.depth - 1):
+            for open_way, here, copy in self.each(step):
+                pl.when(jnp.logical_and(open_way, here))(copy.wait_send)
 
 
 def place_slots(routes_ref, order_ref, placed_ref):
@@ -255,37 +285,32 @@
         placed_ref[e] = jnp.where(placed, 1.0, 0.0).astype(bf16)
 
 
-def project_kernel(
-    stage, tokens_ref, gain_ref, router_ref, cos_ref, sin_ref, docs_ref, routes_ref, order_ref, w_out_ref,
-    w_query_ref, key_matrix_ref, value_matrix_ref,
-    w_all_ref, qt_ref, kt_ref, vt_ref, k_ref, v_ref, docs_all_ref, placed_ref, turned_ref, normed_ref,
-    strips_ref, weights_ref,
-    held_ref, own_out, query_held, key_held, value_held,
-    w_send, w_recv, o_send, o_recv, d_send, d_recv, c_send, c_recv, q_send, q_recv, local,
+def gather_kernel(
+    stage, tokens_ref, gain_ref, router_ref, docs_ref, routes_ref, order_ref, w_query_ref,
+    key_matrix_ref, value_matrix_ref, w_out_ref,
+    docs_all_ref, placed_ref, turned_ref, normed_ref, w_all_ref, strips_ref,
+    held_ref, query_held, key_held, value_held,
+    w_send, w_recv, o_send, o_recv, d_send, d_recv, c_send, c_recv, local,
 ):
     place = Place()
     me, z = place.me, place.z
     met = greet(place.others() + place.layers())
-    strip = strips_ref.shape[1]
     odd = lax.rem(me, 2)
+    pair = lax.div(me, 2)
+    depth, strip, _ = strips_ref.shape
 
     def window(first, size):
         return pl.ds(pl.multiple_of(first * 128, 128), size)
 
-    pair = lax.div(me, 2)
     fetches = [
         pltpu.make_async_copy(
-            w_query_ref.at[:, window(pair * 3 + odd, 2 * 128)], query_held, local.at[GROUP]
+            w_query_ref.at[:, window(pair * 3 + odd, 2 * 128)], query_held, local.at[0]
         ),
+        pltpu.make_async_copy(key_matrix_ref.at[:, window(pair, 128)], key_held, local.at[1]),
+        pltpu.make_async_copy(value_matrix_ref.at[:, window(pair, 128)], value_held, local.at[2]),
         pltpu.make_async_copy(
-            key_matrix_ref.at[:, window(pair, 128)], key_held, local.at[GROUP + 1]
-        ),
-        pltpu.make_async_copy(
-            value_matrix_ref.at[:, window(pair, 128)], value_held, local.at[GROUP + 2]
-        ),
-        pltpu.make_async_copy(
-            w_out_ref.at[pl.ds(pl.multiple_of(me * strip, strip), strip), :], own_out,
-            local.at[GROUP + 3],
+            w_out_ref.at[pl.ds(pl.multiple_of(me * strip, strip), strip), :], strips_ref.at[z],
+            local.at[3],
         ),
     ]
     for fetch in fetches:
@@ -293,7 +318,12 @@
     stage.need(tokens_ref)
     x = tokens_ref[...].astype(f32)
     scale = lax.rsqrt(jnp.mean(x * x, axis=-1, keepdims=True) + epsilon)
-    held_ref[me] = (x * scale * gain_ref[...].reshape(1, -1)).astype(bf16)
+    held_ref[...] = (x * scale * gain_ref[...].reshape(1, -1)).astype(bf16)
+    met()
+    spread = Spread(
+        place, held_ref, lambda owner: normed_ref.at[owner], halves(TOK_DEV), c_send, c_recv
+    )
+    spread.start()
     for fetch in fetches:
         fetch.wait()
 
@@ -308,152 +338,146 @@
     router = router_ref[...].astype(f32)
     empty = jnp.zeros((ROUTER - router.shape[0], router.shape[1]), f32)
     own[HW:, :] = jnp.concatenate([router, empty], axis=0).astype(bf16)
-    met()
-    spread = Spread(
-        place, held_ref.at[me], lambda owner: held_ref.at[owner],
-        halves(TOK_DEV), c_send, c_recv,
-    )
+    lines = [
+        Line(place, lambda layer: w_all_ref.at[layer], w_send, w_recv),
+        Line(place, lambda layer: strips_ref.at[layer], o_send, o_recv),
+    ]
+    for line in lines:
+        line.start()
+    docs_all_ref[me] = docs_ref[...]
     sent = []
-    for j, device in enumerate(place.layers()):
-        sent.append(remote(own, own, w_send.at[j], w_recv.at[j], device))
-        sent[-1].start()
-    spread.start()
-    docs_all_ref[me] = docs_ref[...]
-    others = []
     for j, device in enumerate(place.others()):
-        others.append(remote(docs_ref, docs_all_ref.at[me], d_send.at[j], d_recv.at[j], device))
-        others[-1].start()
+        sent.append(remote(docs_ref, docs_all_ref.at[me], d_send.at[j], d_recv.at[j], device))
+    for copy in sent:
+        copy.start()
+    move = pltpu.make_async_copy(held_ref, normed_ref.at[me], local.at[4])
+    move.start()
     place_slots(routes_ref, order_ref, placed_ref)
     turned_ref[...] = placed_ref[...].reshape(EXP_WIN * CAP, -1).T
     stage.put(placed_ref, turned_ref)
-    spread.step1()
-    spread.step2()
+    steps = (spread.step1, spread.step2)
+    for step in range(1, depth - 1):
+        for act in steps[step - 1 : step]:
+            act()
+        for line in lines:
+            line.step(step)
+    for act in steps[depth - 2 :]:
+        act()
     spread.step3()
+    for line in lines:
+        line.last()
+    stage.put(w_all_ref, strips_ref)
+    spread.last()
     for copy in sent:
-        copy.wait_recv()
-    for j, device in enumerate(place.layers()):
-        others.append(remote(own_out, strips_ref.at[z], o_send.at[j], o_recv.at[j], device))
-        others[-1].start()
-    stage.put(w_all_ref)
-    stage.need(cos_ref, sin_ref)
-    depth = w_all_ref.shape[0]
-    weights = Spread(
-        place, w_all_ref.at[:, :FIRST], lambda owner: weights_ref.at[owner],
-        lambda ref, h: ref.at[pl.ds(h * (depth // 2), depth // 2)], q_send, q_recv,
-    )
-    weights.start()
-    own_moves = [
-        pltpu.make_async_copy(own_out, strips_ref.at[z], local.at[GROUP]),
-        pltpu.make_async_copy(w_all_ref.at[:, :FIRST], weights_ref.at[me], local.at[GROUP + 1]),
-    ]
-    for move in own_moves:
-        move.start()
-    core, side, row = place.near
-    across = flip(side, 4)
-    order = [me, side, row, across, core, flip(side, 1), flip(row, 1), flip(across, 1)]
-
-    def to_normed(owner):
-        return pltpu.make_async_copy(held_ref.at[owner], normed_ref.at[owner], local.at[owner])
-
-    def project(i, _):
-        for at, slots in ((4, (4, 5)), (5, (6, 7)), (6, (8, 9)), (7, (12, 13))):
-
-            @pl.when(i == at)
-            def _(slots=slots):
-                spread.wait(*slots)
-
-        pl.when(i == 5)(weights.step1)
-        pl.when(i == 7)(weights.step2)
-        owner = order[-1]
-        for at in range(GROUP - 1):
-            owner = jnp.where(i == at, order[at], owner)
-        to_normed(owner).start()
-        linear = None
-        for s in range(w_all_ref.shape[0]):
-            size = w_all_ref.shape[2]
-            term = dot(
-                w_all_ref[s, :HW, :], held_ref[owner, :, s * size : (s + 1) * size], ((1,), (1,))
-            )
-            linear = term if linear is None else linear + term
-        tokens = block(owner)
-        cosine, sine = cos_ref[:, tokens], sin_ref[:, tokens]
-        queries = turned(linear[:QW], cosine, sine) * HEAD_DIM ** (-0.5)
-        qt_ref[:, tokens] = queries.astype(bf16)
-        keys = turned(linear[QW : QW + HEAD_DIM], cosine, sine)
-        kt_ref[:, tokens] = keys.astype(bf16)
-        k_ref[tokens, :] = keys.T.astype(bf16)
-        values = linear[QW + HEAD_DIM :]
-        vt_ref[:, tokens] = values.astype(bf16)
-        v_ref[tokens, :] = values.T.astype(bf16)
-        return 0
-
-    lax.fori_loop(0, GROUP, project, 0)
-    stage.put(qt_ref, kt_ref, vt_ref, k_ref, v_ref)
-    weights.step3()
-    for copy in sent:
-        copy.wait_send()
-    for copy in others:
         copy.wait()
-    for move in own_moves:
-        move.wait()
-    for owner in range(GROUP):
-        to_normed(owner).wait()
+    move.wait()
+    for line in lines:
+        line.sent()
     spread.sent()
-    weights.last()
-    weights.sent()
-
-
-def project_call(
-    tokens, gain, router, cosine, sine, docs, routes, order, w_out, w_query, key_matrix,
-    value_matrix, depth,
+
+
+def gather_call(
+    tokens, gain, router, docs, routes, order, w_query, key_matrix, value_matrix, w_out, depth
 ):
     rows, width = tokens.shape
-    span = GROUP * rows
     strip = w_out.shape[0] // GROUP
-    size = w_out.shape[0]
+    size = w_query.shape[0]
     return staged_call(
-        project_kernel,
-        "project",
+        gather_kernel,
+        "gather",
         1,
         [
             ("h", tokens),
             ("v", gain),
             ("v", router),
-            ("h", cosine),
-            ("h", sine),
             ("v", docs),
             ("v", routes),
             ("v", order),
-            ("a", w_out),
             ("a", w_query),
             ("a", key_matrix),
             ("a", value_matrix),
+            ("a", w_out),
         ],
         [
-            ("h", shape((depth, ALL, size), bf16)),
-            ("h", shape((QW, span), bf16)),
-            ("h", shape((HEAD_DIM, span), bf16)),
-            ("h", shape((HEAD_DIM, span), bf16)),
-            ("h", shape((span, HEAD_DIM), bf16)),
-            ("h", shape((span, HEAD_DIM), bf16)),
             ("v", shape((GROUP,) + docs.shape, jnp.int32)),
             ("h", shape((EXP_WIN, CAP, rows), bf16)),
             ("h", shape((rows, EXP_WIN * CAP), bf16)),
             ("a", shape((GROUP, rows, width), bf16)),
-            ("a", shape((depth, strip, w_out.shape[1]), bf16)),
-            ("a", shape((GROUP, depth, FIRST, size), bf16)),
+            ("h", shape((depth, ALL, size), bf16)),
+            ("h", shape((depth, strip, width), bf16)),
         ],
         [
-            VMEM((GROUP, rows, width), bf16),
-            VMEM((strip, width), bf16),
+            VMEM((rows, width), bf16),
             VMEM((size, 2 * 128), bf16),
             VMEM((size, 128), bf16),
             VMEM((size, 128), bf16),
         ]
-        + [DMA((depth - 1,))] * 4
+        + [DMA((2, depth - 1))] * 4
         + [DMA((GROUP - 1,))] * 2
-        + [DMA((Spread.SEMS,))] * 4
-        + [DMA((GROUP + 4,))],
+        + [DMA((Spread.SEMS,))] * 2
+        + [DMA((5,))],
+    )
+
+
+def turned(values, cosine, sine):
+    half = HEAD_DIM // 2
+    out = []
+    for at in range(0, values.shape[0], HEAD_DIM):
+        low, high = values[at : at + half], values[at + half : at + HEAD_DIM]
+        out += [low * cosine - high * sine, high * cosine + low * sine]
+    return jnp.concatenate(out, axis=0)
+
+
+def project_block(
+    owner, normed_ref, w_all_ref, cos_ref, sin_ref, qt_ref, kt_ref, vt_ref, k_ref, v_ref
+):
+    linear = None
+    for s in range(w_all_ref.shape[0]):
+        size = w_all_ref.shape[2]
+        term = dot(
+            w_all_ref[s, :HW, :], normed_ref[owner, :, s * size : (s + 1) * size], ((1,), (1,))
+        )
+        linear = term if linear is None else linear + term
+    tokens = block(owner)
+    cosine, sine = cos_ref[:, tokens], sin_ref[:, tokens]
+    queries = turned(linear[:QW], cosine, sine) * HEAD_DIM ** (-0.5)
+    qt_ref[:, tokens] = queries.astype(bf16)
+    keys = turned(linear[QW : QW + HEAD_DIM], cosine, sine)
+    kt_ref[:, tokens] = keys.astype(bf16)
+    k_ref[tokens, :] = keys.T.astype(bf16)
+    values = linear[QW + HEAD_DIM :]
+    vt_ref[:, tokens] = values.astype(bf16)
+    v_ref[tokens, :] = values.T.astype(bf16)
+
+
+def projected(span):
+    return [
+        ("h", shape((QW, span), bf16)),
+        ("h", shape((HEAD_DIM, span), bf16)),
+        ("h", shape((HEAD_DIM, span), bf16)),
+        ("h", shape((span, HEAD_DIM), bf16)),
+        ("h", shape((span, HEAD_DIM), bf16)),
+    ]
+
+
+def project_kernel(stage, normed_ref, w_all_ref, cos_ref, sin_ref, *outs):
+    stage.need(normed_ref, w_all_ref, cos_ref, sin_ref)
+
+    def project(i, _):
+        project_block(i, normed_ref, w_all_ref, cos_ref, sin_ref, *outs)
+        return 0
+
+    lax.fori_loop(0, GROUP, project, 0)
+
+
+def project_call(normed, w_all, cosine, sine):
+    return staged_call(
+        project_kernel,
+        "project",
+        None,
+        [("h", normed), ("h", w_all), ("h", cosine), ("h", sine)],
+        projected(normed.shape[0] * normed.shape[1]),
+        [],
     )
 
 
@@ -461,44 +485,75 @@
     return jnp.broadcast_to(row.astype(f32), (8, row.shape[1])).T[:, :1]
 
 
-def attend_kernel(
-    n_blocks, stage, qt_ref, k_ref, vt_ref, docs_ref, strips_ref, w_all_ref,
-    o_ref, lse_ref, attended_ref, out_weight_ref, weights_ref,
-    staged_ref, docs_col_ref, top_ref, sum_ref, acc_ref,
+def attend_after_project(
+    n_blocks, stage, w_all_ref, normed_ref, cos_ref, sin_ref, *rest,
+):
+    given, (qt_ref, kt_ref, vt_ref, k_ref, v_ref), rest = rest[:6], rest[6:11], rest[11:]
+
+    def project_all():
+        stage.need(normed_ref, cos_ref, sin_ref)
+
+        def project(i, _):
+            project_block(
+                i, normed_ref, w_all_ref, cos_ref, sin_ref, qt_ref, kt_ref, vt_ref, k_ref, v_ref
+            )
+            return 0
+
+        lax.fori_loop(0, GROUP, project, 0)
+        stage.put(qt_ref, kt_ref, vt_ref, k_ref, v_ref)
+
+    attend_body(n_blocks, stage, project_all, w_all_ref, qt_ref, k_ref, vt_ref, *given, *rest)
+
+
+def attend_kernel(n_blocks, stage, w_all_ref, qt_ref, k_ref, vt_ref, *rest):
+    def fetch_all():
+        stage.need(qt_ref, k_ref, vt_ref)
+
+    attend_body(n_blocks, stage, fetch_all, w_all_ref, qt_ref, k_ref, vt_ref, *rest)
+
+
+def router_of(w_all_ref):
+    return [w_all_ref[s, HW:, :] for s in range(w_all_ref.shape[0])]
+
+
+def attend_body(
+    n_blocks, stage, prepare, w_all_ref, qt_ref, k_ref, vt_ref,
+    docs_ref, strips_ref, tokens_ref, gain_ref, routes_ref, placed_ref,
+    o_ref, lse_ref, attended_ref, out_weight_ref, weights_ref, residual_ref, normed2_ref, gates_ref,
+    slot_gates_ref, rows_ref,
+    staged_ref, docs_col_ref, top_ref, sum_ref, acc_ref, mixed_ref,
     a_send, a_recv, s_send, s_recv, w_send, w_recv, local,
 ):
     T = TOK_DEV
     place = Place()
-    me = place.me
+    me, z = place.me, place.z
     first = place.base
     met = greet(place.others())
-    depth = strips_ref.shape[0]
-    moves = [
-        pltpu.make_async_copy(strips_ref, out_weight_ref.at[:, me], local.at[0]),
-        pltpu.make_async_copy(w_all_ref.at[:, FIRST:HW], weights_ref.at[me], local.at[1]),
-    ]
+    depth, strip, _ = strips_ref.shape
+    move = pltpu.make_async_copy(w_all_ref.at[:, :HW], weights_ref.at[me], local.at[1])
 
     def layers(ref, h):
         return ref.at[pl.ds(h * (depth // 2), depth // 2)]
 
-    spreads = [
-        Spread(place, strips_ref, lambda owner: out_weight_ref.at[:, owner], layers, s_send, s_recv),
-        Spread(
-            place, w_all_ref.at[:, FIRST:HW], lambda owner: weights_ref.at[owner], layers, w_send, w_recv
-        ),
-    ]
-
+    weights = Spread(
+        place, w_all_ref.at[:, :HW], lambda owner: weights_ref.at[owner], layers, w_send, w_recv
+    )
+    strips = Spread(
+        place, strips_ref, lambda owner: out_weight_ref.at[:, owner], layers, s_send, s_recv
+    )
     def turn(i, _):
         docs_col_ref[i] = docs_column(docs_ref[i])
         return 0
 
     lax.fori_loop(0, n_blocks, turn, 0)
-    stage.need(strips_ref, w_all_ref)
+    stage.need(strips_ref)
     met()
-    spreads[0].start()
-    for move in moves:
-        move.start()
-    stage.need(qt_ref, k_ref, vt_ref)
+    strips.start()
+    out_weight_ref[:, me] = strips_ref[...]
+    stage.need(w_all_ref)
+    move.start()
+    prepare()
+    weights.start()
 
     def tile(kb, qb, mask):
         kt = k_ref[block(kb), :]
@@ -524,16 +579,17 @@
     def same(kb, gq):
         return docs_col_ref[kb] == docs_ref[gq].astype(f32)
 
+    def head_rows(head):
+        per = GROUP * depth // GROUP
+        return attended_ref.at[lax.div(head * depth, GROUP), pl.ds(lax.rem(head * depth, GROUP), per)]
+
     def attended_copy(to, slot):
         return remote(
-            staged_ref.at[to], attended_ref.at[slot], a_send.at[to], a_recv.at[slot], place.ctx(to)
+            staged_ref.at[to], head_rows(slot), a_send.at[to], a_recv.at[slot], place.ctx(to)
         )
 
     def q_block(j, _):
-        for at, act in (
-            (2, spreads[0].step1), (4, spreads[0].step2), (4, spreads[1].start),
-            (6, spreads[0].step3),
-        ):
+        for at, act in ((1, strips.step1), (2, strips.step2), (5, strips.step3)):
             pl.when(j == at)(act)
         qb = GROUP - 1 - j
         gq = first + qb
@@ -562,9 +618,9 @@
         lse_ref[qb] = top_ref[...] + jnp.log(sum_ref[...])
         for h in range(HEADS):
             part = slice(h * HEAD_DIM, (h + 1) * HEAD_DIM)
-            mixed = acc_ref[part, :] / sum_ref[h : h + 1, :]
-            o_ref[part, block(qb)] = mixed
-            staged_ref[qb, part, :] = mixed.astype(bf16)
+            acc_ref[part, :] = acc_ref[part, :] / sum_ref[h : h + 1, :]
+        o_ref[:, block(qb)] = acc_ref[...]
+        staged_ref[qb] = acc_ref[...].astype(bf16).reshape(depth, strip, T)
 
         @pl.when(qb != me)
         def _():
@@ -574,123 +630,39 @@
 
     lax.fori_loop(0, GROUP, q_block, 0)
     stage.put(o_ref, lse_ref)
-    own = pltpu.make_async_copy(staged_ref.at[me], attended_ref.at[me], local.at[2])
+    own = pltpu.make_async_copy(staged_ref.at[me], head_rows(me), local.at[2])
     own.start()
-    spreads[1].step1()
-    spreads[1].step2()
-    spreads[1].step3()
+    own.wait()
+    weights.step1()
+    weights.step2()
     for j in range(1, GROUP):
         other = lax.rem(me + j, GROUP)
         attended_copy(other, other).wait()
-    for spread in spreads:
-        spread.last()
-        spread.sent()
-    for move in moves:
-        move.wait()
-    own.wait()
-
-
-def attend_call(qt, k, vt, docs, strips, w_all):
-    n = k.shape[0] // TOK_DEV
-    span = qt.shape[1]
-    depth, _, size = w_all.shape
-    return staged_call(
-        functools.partial(attend_kernel, n),
-        "attend",
-        2,
-        [
-            ("h", qt),
-            ("h", k),
-            ("h", vt),
-            ("v", docs),
-            ("h", strips),
-            ("h", w_all),
-        ],
-        [
-            ("h", shape((QW, span), f32)),
-            ("h", shape((GROUP, 8, TOK_DEV), f32)),
-            ("a", shape((GROUP, QW, TOK_DEV), bf16)),
-            ("a", shape((depth, GROUP) + strips.shape[1:], bf16)),
-            ("a", shape((GROUP, depth, HW - FIRST, size), bf16)),
-        ],
-        [
-            VMEM((GROUP, QW, TOK_DEV), bf16),
-            VMEM((n, TOK_DEV, 1), f32),
-            VMEM((8, TOK_DEV), f32),
-            VMEM((8, TOK_DEV), f32),
-            VMEM((QW, TOK_DEV), f32),
-            DMA((GROUP,)),
-            DMA((GROUP,)),
-        ]
-        + [DMA((Spread.SEMS,))] * 4
-        + [DMA((3,))],
-    )
-
-
-def router_of(w_all_ref):
-    return [w_all_ref[s, HW:, :] for s in range(w_all_ref.shape[0])]
-
-
-def dispatch_kernel(
-    stage, attended_ref, weight_ref, gate_up_ref, tokens_ref, gain_ref, w_all_ref, routes_ref, placed_ref,
-    cotangent_ref,
-    residual_ref, normed_ref, gates_ref, slot_gates_ref, rows_ref, grads_ref, gate_ref, up_ref,
-    active_ref, grad_down_ref, columns_ref,
-    held_ref, weight_held, gate_up_held, mixed_ref, own_rows, own_grads,
-    r_send, r_recv, g_send, g_recv, c_send, c_recv, local,
-):
-    place = Place()
-    me = place.me
-    fetches = [
-        pltpu.make_async_copy(attended_ref, held_ref, local.at[0]),
-        pltpu.make_async_copy(weight_ref, weight_held, local.at[1]),
-        pltpu.make_async_copy(gate_up_ref, gate_up_held, local.at[3]),
-    ]
-    met = greet(place.others())
-    for fetch in fetches:
-        fetch.start()
+    stage.put(attended_ref)
+    strips.last()
+    stage.put(out_weight_ref)
+
     rows, width = tokens_ref.shape
-    experts_wide = gates_ref.shape[0]
-
-    def copy(source, target, send, receive, j):
-        to = lax.rem(me + j, GROUP)
-        return remote(source.at[to], target.at[me], send.at[j], receive.at[j], place.ctx(to))
-
-    def strip_copy(j):
-        to = lax.rem(me + j, GROUP)
-        return remote(
-            attended_ref.at[:, to], columns_ref.at[me], c_send.at[j], c_recv.at[j], place.ctx(to)
-        )
-
-    fetches[0].wait()
-    met()
-    for j in range(1, GROUP):
-        strip_copy(j).start()
-    own_strip = pltpu.make_async_copy(held_ref.at[:, me], columns_ref.at[me], local.at[2])
-    own_strip.start()
-    mixed_ref[...] = held_ref[...].reshape(width, rows).T
-    fetches[1].wait()
-    stage.need(tokens_ref)
+    stage.need(tokens_ref, placed_ref)
+    mixed_ref[...] = attended_ref[...].reshape(width, rows).T
 
     def out_columns(i, _):
         columns = block(i)
-        residual_ref[:, columns] = tokens_ref[:, columns].astype(f32) + dot(
-            mixed_ref[...], weight_held[:, columns]
-        )
-        return 0
-
-    lax.fori_loop(0, width // TOK_DEV, out_columns, 0)
+        weight = out_weight_ref[:, :, :, columns].reshape(width, T)
+        residual_ref[:, columns] = tokens_ref[:, columns].astype(f32) + dot(mixed_ref[...], weight)
+        return 0
+
+    lax.fori_loop(0, width // T, out_columns, 0)
     residual = residual_ref[...]
     scale = lax.rsqrt(jnp.mean(residual * residual, axis=-1, keepdims=True) + epsilon)
-    normed_ref[...] = (residual * scale * gain_ref[...].reshape(1, -1)).astype(bf16)
-    stage.put(residual_ref, normed_ref)
-    stage.need(w_all_ref)
+    normed2_ref[...] = (residual * scale * gain_ref[...].reshape(1, -1)).astype(bf16)
+    stage.put(residual_ref, normed2_ref)
     logits = None
     for s, router in enumerate(router_of(w_all_ref)):
         size = router.shape[1]
-        term = dot(router, normed_ref[:, s * size : (s + 1) * size], ((1,), (1,)))
+        term = dot(router, normed2_ref[:, s * size : (s + 1) * size], ((1,), (1,)))
         logits = term if logits is None else logits + term
-    expert = lax.broadcasted_iota(jnp.int32, (experts_wide, rows), 0)
+    expert = lax.broadcasted_iota(jnp.int32, gates_ref.shape, 0)
     chosen = expert < 0
     for k in range(TOPK):
         chosen = chosen | (expert == routes_ref[k : k + 1, :])
@@ -699,21 +671,86 @@
     gates = jnp.where(chosen, jnp.exp(logits - top), 0.0)
     gates = gates / jnp.sum(gates, axis=0, keepdims=True)
     gates_ref[...] = gates
-    stage.need(placed_ref, cotangent_ref)
     for e in range(EXP_WIN):
         slot_gates_ref[e] = jnp.sum(
             placed_ref[e].astype(f32) * gates[e : e + 1, :], axis=1, keepdims=True
         )
 
-    def send_rows(j, _):
+    def pick_rows(e, _):
+        rows_ref[e] = dot(placed_ref[e], normed2_ref[...]).astype(bf16)
+        return 0
+
+    lax.fori_loop(0, EXP_WIN, pick_rows, 0)
+    stage.put(gates_ref, slot_gates_ref, rows_ref)
+    weights.step3()
+    weights.last()
+    weights.sent()
+    strips.sent()
+    move.wait()
+
+
+def attend_call(
+    kernel, ins, docs, strips, tokens, gain, routes, placed, w_all, span, projections
+):
+    n = docs.shape[0]
+    rows, width = tokens.shape
+    depth, _, size = w_all.shape
+    strip = strips.shape[1]
+    return staged_call(
+        functools.partial(kernel, n),
+        "attend",
+        2,
+        [("h", one) for one in ins]
+        + [("v", docs), ("h", strips), ("h", tokens), ("v", gain), ("v", routes), ("h", placed)],
+        projections
+        + [
+            ("h", shape((QW, span), f32)),
+            ("h", shape((GROUP, 8, TOK_DEV), f32)),
+            ("h", shape((depth, GROUP, strip, TOK_DEV), bf16)),
+            ("h", shape((depth, GROUP) + strips.shape[1:], bf16)),
+            ("a", shape((GROUP, depth, HW, size), bf16)),
+            ("h", shape((rows, width), f32)),
+            ("h", shape((rows, width), bf16)),
+            ("h", shape((ROUTER, rows), f32)),
+            ("h", shape((EXP_WIN, CAP, 1), f32)),
+            ("h", shape((EXP_WIN, CAP, width), bf16)),
+        ],
+        [
+            VMEM((GROUP, depth, strip, TOK_DEV), bf16),
+            VMEM((n, TOK_DEV, 1), f32),
+            VMEM((8, TOK_DEV), f32),
+            VMEM((8, TOK_DEV), f32),
+            VMEM((QW, TOK_DEV), f32),
+            VMEM((rows, width), bf16),
+        ]
+        + [DMA((GROUP,))] * 2
+        + [DMA((Spread.SEMS,))] * 4
+        + [DMA((3,))],
+    )
+
+
+def dispatch_kernel(
+    stage, sent_rows_ref, gate_up_ref, placed_ref, cotangent_ref, slot_gates_ref,
+    rows_ref, grads_ref, gate_ref, up_ref, active_ref, grad_down_ref,
+    gate_up_held, own_grads, r_send, r_recv, g_send, g_recv, local,
+):
+    place = Place()
+    me = place.me
+    met = greet(place.others())
+    width = cotangent_ref.shape[1]
+
+    def copy(source, target, send, receive, j):
         to = lax.rem(me + j, GROUP)
-        own_rows[to] = dot(placed_ref[to], normed_ref[...]).astype(bf16)
-
-        @pl.when(j < GROUP)
-        def _():
-            copy(own_rows, rows_ref, r_send, r_recv, j).start()
-
-        return 0
+        return remote(source.at[to], target.at[me], send.at[j], receive.at[j], place.ctx(to))
+
+    met()
+    for j in range(1, GROUP):
+        copy(sent_rows_ref, rows_ref, r_send, r_recv, j).start()
+    own = pltpu.make_async_copy(sent_rows_ref.at[me], rows_ref.at[me], local.at[0])
+    own.start()
+    fetch = pltpu.make_async_copy(gate_up_ref, gate_up_held, local.at[1])
+    fetch.start()
+    stage.need(placed_ref, cotangent_ref, slot_gates_ref)
 
     def send_grads(j, _):
         to = lax.rem(me + j, GROUP)
@@ -726,14 +763,12 @@
 
         return 0
 
-    lax.fori_loop(1, GROUP + 1, send_rows, 0)
     lax.fori_loop(1, GROUP + 1, send_grads, 0)
-    stage.put(gates_ref, slot_gates_ref)
-    rows_ref[me] = own_rows[me]
     grads_ref[me] = own_grads[me]
-    fetches[2].wait()
+    fetch.wait()
+    own.wait()
     for j in range(1, GROUP):
-        copy(own_rows, rows_ref, r_send, r_recv, j).wait_recv()
+        copy(sent_rows_ref, rows_ref, r_send, r_recv, j).wait_recv()
     stage.put(rows_ref)
     slots = GROUP * CAP
     hidden = gate_ref.shape[1]
@@ -763,57 +798,34 @@
     lax.fori_loop(0, width // TOK_DEV, expert_over, 0)
     stage.put(grad_down_ref)
     for j in range(1, GROUP):
-        strip_copy(j).wait()
-        copy(own_rows, rows_ref, r_send, r_recv, j).wait_send()
+        copy(sent_rows_ref, rows_ref, r_send, r_recv, j).wait_send()
         copy(own_grads, grads_ref, g_send, g_recv, j).wait_send()
-    own_strip.wait()
-
-
-def dispatch_call(attended, weight, gate_up, tokens, gain, w_all, routes, placed, cotangent):
-    rows, width = tokens.shape
+
+
+def dispatch_call(sent_rows, gate_up, placed, cotangent, slot_gates):
+    slots = sent_rows.shape
+    count, width = GROUP * CAP, slots[2]
     hidden = gate_up.shape[1] // 2
-    count = GROUP * CAP
-    slots = (GROUP, CAP, width)
-    depth = w_all.shape[0]
-    attended = attended.reshape(depth, GROUP, -1, rows)
     return staged_call(
         dispatch_kernel,
         "dispatch",
         3,
         [
-            ("a", attended),
-            ("a", weight),
+            ("a", sent_rows),
             ("a", gate_up),
-            ("h", tokens),
-            ("v", gain),
-            ("h", w_all),
-            ("v", routes),
             ("h", placed),
             ("h", cotangent),
+            ("h", slot_gates),
         ],
         [
-            ("h", shape((rows, width), f32)),
-            ("h", shape((rows, width), bf16)),
-            ("h", shape((ROUTER, rows), f32)),
-            ("h", shape((EXP_WIN, CAP, 1), f32)),
             ("h", shape(slots, bf16)),
             ("h", shape(slots, bf16)),
             ("h", shape((count, hidden), f32)),
             ("h", shape((count, hidden), f32)),
             ("h", shape((count, hidden), bf16)),
             ("h", shape((hidden, width), bf16)),
-            ("a", shape((GROUP, depth) + attended.shape[2:], bf16)),
         ],
-        [
-            VMEM(attended.shape, bf16),
-            VMEM(weight.shape, bf16),
-            VMEM(gate_up.shape, bf16),
-            VMEM((rows, width), bf16),
-            VMEM(slots, bf16),
-            VMEM(slots, bf16),
-        ]
-        + [DMA((GROUP,))] * 6
-        + [DMA((4,))],
+        [VMEM(gate_up.shape, bf16), VMEM(slots, bf16)] + [DMA((GROUP,))] * 4 + [DMA((2,))],
     )
 
 
@@ -1069,32 +1081,73 @@
 
 
 def backward_kernel(
-    n_blocks, stage, qt_ref, k_ref, kt_ref, v_ref, heads_ref, o_ref, lse_ref, docs_ref, attn_ref,
-    columns_ref, down_ref,
+    n_blocks, stage, attn_ref, attended_ref, down_ref, heads_ref, o_ref, lse_ref, qt_ref, k_ref,
+    kt_ref, v_ref, docs_ref,
     dq_ref, dk_ref, dv_ref, grad_out_ref, down_all_ref,
-    attn_all_ref, docs_col_ref, delta_ref, dk_acc, dv_acc, a_send, a_recv, e_send, e_recv, local,
+    part_ref, pair_ref, strip_ref, came_ref, docs_col_ref, delta_ref, dk_acc, dv_acc,
+    p_send, p_recv, s_send, s_recv, e_send, e_recv, local,
 ):
     T = TOK_DEV
     place = Place()
     me = place.me
     first = place.base
-    met = greet([place.ctx(i) for i in place.near])
-    stage.need(attn_ref)
-    move = pltpu.make_async_copy(attn_ref, attn_all_ref.at[me], local.at[0])
-    move.start()
-    spread = Spread(
-        place, attn_ref, lambda owner: attn_all_ref.at[owner],
-        halves(T), a_send, a_recv,
-    )
+    core, side, row = place.near
+    across = flip(side, 4)
+    met = greet([place.ctx(i) for i in (core, side, row, across)])
+    half = GROUP // 2
+    depth, strip, width = grad_out_ref.shape
+    parity = lax.rem(me, 2)
+
+    def strip_of(n, parity):
+        return 2 * n + parity
+
+    def part(n, parity):
+        rows = attended_ref[:, strip_of(n, parity)].reshape(depth * strip, T)
+        return dot(rows, attn_ref[...])
+
+    def pair_copy(n):
+        return remote(
+            part_ref.at[n], pair_ref.at[n], p_send.at[n], p_recv.at[n], place.ctx(core)
+        )
+
+    def pair_part(n, _):
+        part_ref[n] = part(n, 1 - parity).astype(bf16)
+        pair_copy(n).start()
+        return 0
+
+    down_move = pltpu.make_async_copy(down_ref, down_all_ref.at[me], local.at[0])
+    down_spread = Spread(
+        place, down_ref, lambda owner: down_all_ref.at[owner], halves(down_ref.shape[0]), e_send, e_recv
+    )
+    stage.need(attn_ref, attended_ref)
     met()
-    spread.start()
-    down_move = pltpu.make_async_copy(down_ref, down_all_ref.at[me], local.at[1])
+    lax.fori_loop(0, half, pair_part, 0)
     stage.need(down_ref)
+    down_spread.start()
     down_move.start()
-    down_spread = Spread(
-        place, down_ref, lambda owner: down_all_ref.at[owner],
-        halves(down_ref.shape[0]), e_send, e_recv,
-    )
+
+    def own_part(n, _):
+        strip_ref[n] = part(n, parity).astype(bf16)
+        return 0
+
+    lax.fori_loop(0, half, own_part, 0)
+    for n in range(half):
+        pair_copy(n).wait_recv()
+
+    def add_pair(n, _):
+        strip_ref[n] = (strip_ref[n].astype(f32) + pair_ref[n].astype(f32)).astype(bf16)
+        return 0
+
+    lax.fori_loop(0, half, add_pair, 0)
+    strips = [
+        remote(
+            strip_ref.at[lax.div(device, 2)], came_ref.at[n], s_send.at[n], s_recv.at[n],
+            place.ctx(device),
+        )
+        for n, device in enumerate((across, side, row))
+    ]
+    for copy in strips:
+        copy.start()
 
     def turn(i, _):
         docs_col_ref[i] = docs_column(docs_ref[i])
@@ -1104,7 +1157,7 @@
     heads = range(HEADS)
     parts = [slice(h * HEAD_DIM, (h + 1) * HEAD_DIM) for h in heads]
 
-    stage.need(heads_ref, o_ref, lse_ref, qt_ref, k_ref, kt_ref, v_ref, columns_ref)
+    stage.need(heads_ref, o_ref, lse_ref, qt_ref, k_ref, kt_ref, v_ref)
 
     def prepare(i, _):
         for h in heads:
@@ -1137,26 +1190,9 @@
     def same(kb, gq):
         return docs_col_ref[kb] == docs_ref[gq].astype(f32)
 
-    depth, strip, width = grad_out_ref.shape
-
-    def out_weights():
-        move.wait()
-        spread.last()
-
-        def columns(i, _):
-            total = None
-            for b in range(GROUP):
-                term = dot(columns_ref[b].reshape(depth * strip, T), attn_all_ref[b, :, block(i)])
-                total = term if total is None else total + term
-            grad_out_ref[:, :, block(i)] = total.astype(bf16).reshape(depth, strip, T)
-            return 0
-
-        lax.fori_loop(0, width // T, columns, 0)
-
     def k_block(kb, _):
         for at, act in (
-            (2, spread.step1), (3, spread.step2), (3, down_spread.start), (5, spread.step3),
-            (6, down_spread.step1), (7, out_weights),
+            (2, down_spread.step1), (4, down_spread.step2), (7, down_spread.step3),
         ):
             pl.when(kb == first + at)(act)
         dk_acc[...] = jnp.zeros_like(dk_acc)
@@ -1195,37 +1231,35 @@
         return 0
 
     lax.fori_loop(first + GROUP, n_blocks, clear, 0)
-    stage.put(dq_ref, dk_ref, dv_ref, grad_out_ref)
-    down_spread.step2()
-    down_spread.step3()
+    stage.put(dq_ref, dk_ref, dv_ref)
+    for copy in strips:
+        copy.wait_recv()
+    total = strip_ref[lax.div(me, 2)].astype(f32)
+    for n in range(len(strips)):
+        total = total + came_ref[n].astype(f32)
+    grad_out_ref[...] = total.astype(bf16).reshape(depth, strip, width)
+    stage.put(grad_out_ref)
     down_spread.last()
     down_spread.sent()
+    for n in range(half):
+        pair_copy(n).wait_send()
+    for copy in strips:
+        copy.wait_send()
     down_move.wait()
-    spread.sent()
-
-
-def backward_call(qt, k, kt, v, heads, o, lse, docs, attn, columns, down):
+
+
+def backward_call(attn, attended, down, heads, o, lse, qt, k, kt, v, docs):
     n = k.shape[0] // TOK_DEV
     span = qt.shape[1]
     rows, width = attn.shape
-    _, depth, strip, _ = columns.shape
+    depth, _, strip, _ = attended.shape
+    block_rows = depth * strip
+    half = GROUP // 2
     return staged_call(
         functools.partial(backward_kernel, n),
         "backward",
         5,
-        [
-            ("h", qt),
-            ("h", k),
-            ("h", kt),
-            ("h", v),
-            ("h", heads),
-            ("h", o),
-            ("h", lse),
-            ("v", docs),
-            ("h", attn),
-            ("h", columns),
-            ("h", down),
-        ],
+        [("h", one) for one in (attn, attended, down, heads, o, lse, qt, k, kt, v)] + [("v", docs)],
         [
             ("h", shape((QW, span), f32)),
             ("h", shape(kt.shape, f32)),
@@ -1234,22 +1268,27 @@
             ("a", shape((GROUP,) + down.shape, bf16)),
         ],
         [
-            VMEM((GROUP, rows, width), bf16),
+            VMEM((half, block_rows, width), bf16),
+            VMEM((half, block_rows, width), bf16),
+            VMEM((half, block_rows, width), bf16),
+            VMEM((3, block_rows, width), bf16),
             VMEM((n, TOK_DEV, 1), f32),
             VMEM((GROUP, 8, TOK_DEV), f32),
             VMEM((TOK_DEV, HEAD_DIM), f32),
             VMEM((TOK_DEV, HEAD_DIM), f32),
         ]
-        + [DMA((Spread.SEMS,))] * 4
-        + [DMA((2,))],
+        + [DMA((half,))] * 2
+        + [DMA((3,))] * 2
+        + [DMA((Spread.SEMS,))] * 2
+        + [DMA((1,))],
     )
 
 
 def finish_kernel(
-    stage, normed_ref, first_ref, others_ref, gate_up_ref, grad_out_ref, dq_ref, dk_ref, dv_ref, cos_ref,
+    stage, normed_ref, weights_ref, gate_up_ref, grad_out_ref, dq_ref, dk_ref, dv_ref, cos_ref,
     sin_ref, tokens_ref, gain_ref, grad_residual_ref, grad_router_ref, grad_gain2_ref,
     input_grad_ref, shared_ref, small_all_ref, out_all_ref, gate_up_all_ref,
-    normed_held, first_held, others_held, linear_ref, came_ref, first_t, others_t, sum_ref, part_ref,
+    normed_held, weights_held, linear_ref, came_ref, came_t, sum_ref, part_ref,
     small_ref, head_in, small_in, out_in, shard_ref, small_shard_ref, out_shard_ref,
     g_send, g_recv, h_send, h_recv, s_send, s_recv, o_send, o_recv, e_send, e_recv, f_send, f_recv,
     m_send, m_recv, c_send, c_recv, local,
@@ -1259,8 +1298,7 @@
     met = greet(place.others() + place.layers())
     fetches = [
         pltpu.make_async_copy(normed_ref, normed_held, local.at[0]),
-        pltpu.make_async_copy(first_ref, first_held, local.at[1]),
-        pltpu.make_async_copy(others_ref, others_held, local.at[2]),
+        pltpu.make_async_copy(weights_ref, weights_held, local.at[1]),
     ]
     for fetch in fetches:
         fetch.start()
@@ -1354,13 +1392,11 @@
     out_spread.start()
     moves[1].start()
     fetches[1].wait()
-    fetches[2].wait()
     for j in range(1, GROUP):
         copy(j).wait_recv()
 
     def turn(j, _):
-        first_t[j] = came_ref[j, :FIRST, :].T
-        others_t[j] = came_ref[j, FIRST:, :].T
+        came_t[j] = came_ref[j].T
         return 0
 
     lax.fori_loop(0, GROUP, turn, 0)
@@ -1368,7 +1404,7 @@
     def add_heads(s, _):
         total = None
         for j in range(GROUP):
-            term = dot(first_t[j], first_held[j, s]) + dot(others_t[j], others_held[j, s])
+            term = dot(came_t[j], weights_held[j, s])
             total = term if total is None else total + term
         sum_ref[:, block(s, size)] = total
         return 0
@@ -1429,7 +1465,7 @@
 
 
 def finish_call(
-    normed, first, others, gate_up, grad_out, dq, dk, dv, cosine, sine, tokens, gain, grad_residual,
+    normed, weights, gate_up, grad_out, dq, dk, dv, cosine, sine, tokens, gain, grad_residual,
     grad_router, grad_gain2,
 ):
     rows, width = tokens.shape
@@ -1441,8 +1477,7 @@
         6,
         [
             ("a", normed),
-            ("a", first),
-            ("a", others),
+            ("a", weights),
             ("h", gate_up),
             ("h", grad_out),
             ("h", dq),
@@ -1465,12 +1500,10 @@
         ],
         [
             VMEM(normed.shape, bf16),
-            VMEM(first.shape, bf16),
-            VMEM(others.shape, bf16),
+            VMEM(weights.shape, bf16),
             VMEM((GROUP, HW, rows), bf16),
             VMEM((GROUP, HW, rows), bf16),
-            VMEM((GROUP, rows, FIRST), bf16),
-            VMEM((GROUP, rows, HW - FIRST), bf16),
+            VMEM((GROUP, rows, HW), bf16),
             VMEM((rows, width), f32),
             VMEM((depth, HW, size), bf16),
             VMEM((depth, ROUTER, size), bf16),
@@ -1629,12 +1662,9 @@
     own_tokens, own_cotangent = tokens[0], cotangent[0]
 
     route_rows, order_rows = routes[0].T, slot_order[0].T
-    (
-        w_all, queries, keys_t, values_t, keys, values, docs, placed, placed_t, normed1, strips,
-        first_all,
-    ) = project_call(
-        own_tokens, norm1_gain, w_router.T, cosine, sine, doc_ids,
-        route_rows, order_rows, w_out, w_query, key_matrix, value_matrix, depth,
+    docs, placed, placed_t, normed1, w_all, strips = gather_call(
+        own_tokens, norm1_gain, w_router.T, doc_ids, route_rows, order_rows, w_query, key_matrix,
+        value_matrix, w_out, depth,
     )
     w_gate, w_up, w_down, docs = lax.optimization_barrier((w_gate, w_up, w_down, docs))
     gate_up = gather_z(
@@ -1652,17 +1682,25 @@
         def gather_far(value, axis):
             return lax.all_gather(value, "ctx", axis=axis, axis_index_groups=far, tiled=True)
 
+        queries, keys_t, values_t, keys, values = project_call(normed1, w_all, cosine, sine)
         keys, values, docs = gather_far(keys, 0), gather_far(values, 0), gather_far(docs, 0)
         keys_t, values_t = gather_far(keys_t, 1), gather_far(values_t, 1)
-    attended_f32, log_total, attended, out_weight, others_all = attend_call(
-        queries, keys, values_t, docs, strips, w_all
-    )
+        after = attend_call(
+            attend_kernel, [w_all, queries, keys, values_t], docs, strips, own_tokens, norm2_gain,
+            route_rows, placed, w_all, span, [],
+        )
+    else:
+        queries, keys_t, values_t, keys, values, *after = attend_call(
+            attend_after_project, [w_all, normed1, cosine, sine], docs, strips, own_tokens, norm2_gain,
+            route_rows, placed, w_all, span, projected(span),
+        )
+    (
+        attended_f32, log_total, attended, out_weight, weights_all, residual, normed2, gates,
+        slot_gates, rows_out,
+    ) = after
     out_weight = out_weight.reshape(width, width)
-    (
-        residual, normed2, gates, slot_gates, sent_rows, sent_grads, gate, up, active, grad_w_down,
-        columns,
-    ) = dispatch_call(
-        attended, out_weight, gate_up, own_tokens, norm2_gain, w_all, route_rows, placed, own_cotangent
+    sent_rows, sent_grads, gate, up, active, grad_w_down = dispatch_call(
+        rows_out, gate_up, placed, own_cotangent, slot_gates
     )
     grad_w_down = reduce_z(grad_w_down)
     expert_out, grad_buffer, grad_w_gate_up = expert_call(
@@ -1675,14 +1713,14 @@
         residual, normed2, gates, placed, placed_t, slot_gates, own_cotangent, norm2_gain, w_all,
     )
     dq, dk, dv, grad_out, down_w = backward_call(
-        queries, keys, keys_t, values, heads, attended_f32, log_total, docs, attn, columns,
-        grad_w_down,
+        attn, attended, grad_w_down, heads, attended_f32, log_total, queries, keys, keys_t, values,
+        docs,
     )
     if parts > 1:
         dk = lax.psum_scatter(dk, "ctx", scatter_dimension=1, axis_index_groups=far, tiled=True)
         dv = lax.psum_scatter(dv, "ctx", scatter_dimension=1, axis_index_groups=far, tiled=True)
     input_grad, shared, small, out_w, gate_up_w = finish_call(
-        normed1, first_all, others_all, grad_w_gate_up, grad_out, dq, dk, dv, cosine, sine,
+        normed1, weights_all, grad_w_gate_up, grad_out, dq, dk, dv, cosine, sine,
         own_tokens, norm1_gain, grad_residual, grad_router, grad_gain2,
     )
     if parts > 1:

time: 358 us -> 350 us (0.978)
  waiting for transfers between devices: 5.41 us -> 0.15 us
    all_gather x2, waiting for transfers between devices: 5.3 us -> 0.04 us  [gather_z(): return lax.all_gather(value, 'fsdp', axis=0, tiled=True)]
  transfers between devices with their start and end apart: 4 -> 4, of which waited for: 1 -> 0; matrix products, arithmetic and copies ran while one was open for 0% -> 0% of each run, Pallas kernels for 58% -> 61%
where the time goes in v3:
time: 350 us; the launch traced here: 349 us
  Pallas kernels  332 us (95%)
  between operations  13.9 us (4%)
    pallas_call x7, Pallas kernels, staged_call(): pl.pallas_call(kernel, out_shape=tuple((one for _, one in outs)), in_spec...  316 us
    pallas_call x1, Pallas kernels, output_call(): pl.pallas_call(output_kernel, grid=(count,), out_shape=(shape((size, coun...  16.2 us
  transfers between devices with their start and end apart: 4, of which 0 were waited for; matrix products, arithmetic and copies ran while one was open for 0% of the time, Pallas kernels for 61%

profile of v3, /device:TPU:0, one launch (start us, length us, event | category | flops | bytes accessed | tf_op | source)
XLA Modules:
  0.0 349.1 jit_solution(15226918924864429665)
XLA Ops:
  7.2 0.0 copy-start
  7.2 0.0 all-gather.4.cloned.1.call-start
  7.3 37.8 %gather.1 = (s32[8,1,256]{2,1,0:T(1,128)}, bf16[8,64,256]{2,1,0:T(8,128)(2,1)}, bf16[256,512]{1,0:T(8,128)(2,1)}, bf16[8,256,1536]{2,1,0:T(8,128)(2,1)}, bf16[4,...) custom-call(bf16[256,1536]{1,0:T(8,128)(2,1)} %bitcast.22, f32[1536]{0:T(1024)} %refs_10_.3, ...), custom_call_target="tpu_custom_call" | custom-call | tf_op jit(solution)/shard_map/gather/pallas_call | solution.py:104
  45.0 1.2 dynamic-slice_bitcast_fusion
  46.2 1.0 pad_maximum_fusion
  47.2 0.0 all-gather.4.cloned.1.call-update
  47.2 0.0 all-gather.6.cloned.1.call-start
  47.3 0.8 constant_dynamic-slice_fusion
  48.1 0.0 all-gather.6.cloned.1.call-update
  48.1 0.0 reduce-scatter.5.cloned.1.call-start
  48.1 72.3 %attend.1 = (bf16[192,2048]{1,0:T(8,128)(2,1)}, bf16[64,2048]{1,0:T(8,128)(2,1)}, bf16[64,2048]{1,0:T(8,128)(2,1)}, bf16[2048,64]{1,0:T(8,128)(2,1)}, bf16[2048,...) custom-call(bf16[4,368,384]{2,1,0:T(8,128)(2,1)} %get-tuple-element., ...), custom_call_target="tpu_custom_call" | custom-call | tf_op jit(solution)/shard_map/attend/pallas_call | solution.py:104
  120.4 0.0 all-gather.4.cloned.1.call-done.refs_1_.refs_6_
  120.5 38.8 %dispatch.1 = (bf16[8,64,1536]{2,1,0:T(8,128)(2,1)}, bf16[8,64,1536]{2,1,0:T(8,128)(2,1)}, f32[512,512]{1,0:T(8,128)}, f32[512,512]{1,0:T(8,128)}, bf16[512,512]{1,0:T(8,128)(2,1)}, /*index=5*/bf16[512,1536]{1,0:T(8,128)(2,1)}) custom-call(bf16[8,64,1536]{2,1,0:T(8,128)(2,1)} %get-tuple-element.80.refs_0_, ...), custom_call_target="tpu_custom_call" | custom-call | tf_op jit(solution)/shard_map/dispatch/pallas_call | solution.py:104
  159.3 0.0 reduce-scatter.5.cloned.1.call-update
  159.3 0.0 reduce-scatter.3.cloned.1.call-start
  159.3 0.0 all-gather.6.cloned.1.call-done
  159.4 22.6 %expert.1 = (bf16[8,64,1536]{2,1,0:T(8,128)(2,1)}, bf16[512,1536]{1,0:T(8,128)(2,1)}, bf16[1536,1024]{1,0:T(8,128)(2,1)}) custom-call(bf16[512,512]{1,0:T(8,128)(2,1)} %get-tuple-element.84.refs_0_, bf16[512,1536]{1,0:T(8,128)(2,1)} %bitcast.28, bf16[512,1536]{1,0:T(8,128)(2,1)} %bitcast.30, bf16[512,1536]{1,0:T(8,128)(2,1)} %bitcast.29, ...), custom_call_target="tpu_custom_call" | custom-call | tf_op jit(solution)/shard_map/expert/pallas_call | solution.py:104
  182.0 0.0 reduce-scatter.3.cloned.1.call-update
  182.0 32.9 %combine.1 = (bf16[256,1536]{1,0:T(8,128)(2,1)}, f32[256,1536]{1,0:T(8,128)}, bf16[8,192,256]{2,1,0:T(8,128)(2,1)}, bf16[256,1536]{1,0:T(8,128)(2,1)}, f32[48,1536]{1,0:T(8,128)}, /*index=5*/f32[1,1536]{1,0:T(1,128)}) custom-call(bf16[8,64,1536]{2,1,0:T(8,128)(2,1)} %get-tuple-element.91.refs_0_, bf16[8,64,1536]{2,1,0:T(8,128)(2,1)} %bitcast.31, ...), custom_call_target="tpu_custom_call" | custom-call | tf_op jit(solution)/shard_map/combine/pallas_call | solution.py:104
  214.9 0.0 reduce-scatter.5.cloned.1.call-done.refs_2_
  215.0 47.2 %backward.1 = (f32[192,2048]{1,0:T(8,128)}, f32[64,2048]{1,0:T(8,128)}, f32[64,2048]{1,0:T(8,128)}, bf16[4,48,1536]{2,1,0:T(8,128)(2,1)}, bf16[8,128,1536]{2,1,0:T(8,128)(2,1)}) custom-call(bf16[256,1536]{1,0:T(8,128)(2,1)} %get-tuple-element.98.refs_0_, bf16[4,8,48,256]{3,2,1,0:T(8,128)(2,1)} %get-tuple-element.99.refs_1_, ...), custom_call_target="tpu_custom_call" | custom-call | tf_op jit(solution)/shard_map/backward/pallas_call | solution.py:104
  262.2 0.0 reduce-scatter.3.cloned.1.call-done.refs_2_
  262.2 64.1 %finish.1 = (f32[256,1536]{1,0:T(8,128)}, bf16[8,320,384]{2,1,0:T(8,128)(2,1)}, bf16[8,48,384]{2,1,0:T(8,128)(2,1)}, bf16[8,48,1536]{2,1,0:T(8,128)(2,1)}, bf16[8,384,1024]{2,1,0:T(8,128)(2,1)}) custom-call(bf16[8,256,1536]{2,1,0:T(8,128)(2,1)} %get-tuple-element.73.refs_1_.refs_0_, bf16[8,4,320,384]{3,2,1,0:T(8,128)(2,1)} %get-tuple-element.79.refs_1_, ...), custom_call_target="tpu_custom_call" | custom-call | tf_op jit(solution)/shard_map/finish/pallas_call | solution.py:104
  326.4 16.2 %output.1 = (f32[384,1536]{1,0:T(8,128)}, f32[384,512]{1,0:T(8,128)}, f32[384,512]{1,0:T(8,128)}, f32[8,48,1536]{2,1,0:T(8,128)}, f32[40,384]{1,0:T(8,128)}, /*i...) custom-call(bf16[8,320,384]{2,1,0:T(8,128)(2,1)} %get-tuple-element., ...), custom_call_target="tpu_custom_call" | custom-call | tf_op jit(solution)/shard_map/output/pallas_call | solution.py:1574
  (3 shorter events, 0.0 us)
Async XLA Ops:
  7.2 40.1 %copy-start = (bf16[8,128,1536]{2,1,0:T(8,128)(2,1)S(1)}, bf16[8,128,1536]{2,1,0:T(8,128)(2,1)}, u32[]{:S(2)}) copy-start(bf16[8,128,1536]{2,1,0:T(8,128)(2,1)} %param.30) | copy-start | bytes 9437188
  7.2 113.3 %all-gather.4.cloned.1.call-start = ((), (), s32[]{:S(2)}) async-start(), calls=%async_computation.2 | async-start | bytes 3932160 | tf_op jit(solution)/shard_map/all_gather | solution.py:1650
  47.2 112.1 %all-gather.6.cloned.1.call-start = ((), (), s32[]{:S(2)}) async-start(), calls=%async_computation.5 | async-start | bytes 1966080 | tf_op jit(solution)/shard_map/all_gather | solution.py:1650
  48.1 166.9 %reduce-scatter.5.cloned.1.call-start = ((), (), s32[]{:S(2)}) async-start(), calls=%async_computation.4 | async-start | bytes 1966080 | tf_op jit(solution)/shard_map/reduce_scatter | solution.py:1653
  159.3 102.9 %reduce-scatter.3.cloned.1.call-start = ((), (), s32[]{:S(2)}) async-start(), calls=%async_computation.3 | async-start | bytes 3932160 | tf_op jit(solution)/shard_map/reduce_scatter | solution.py:1653
  326.4 16.2 %copy-start.1 = (bf16[8,128,1536]{2,1,0:T(8,128)(2,1)S(1)}, bf16[8,128,1536]{2,1,0:T(8,128)(2,1)}, u32[]{:S(2)}) copy-start(bf16[8,128,1536]{2,1,0:T(8,128)(2,1)} %param.30) | copy-start | bytes 9437188
Sparse Core Ops, SparseCore 0:
  47.4 62.8 all-gather.3
  112.3 35.7 all-gather.5
  159.4 36.7 reduce-scatter.4
  198.3 59.2 reduce-scatter.2

commit v4 on v3

--- a/solution.py
+++ b/solution.py
@@ -55,8 +55,13 @@
 
 
 class Staged:
-    def __init__(self, fetches, puts):
-        self.fetches, self.puts, self.out = fetches, puts, []
+    def __init__(self, fetches, later, puts):
+        self.fetches, self.later, self.puts, self.out = fetches, later, puts, []
+
+    def begin(self):
+        for copy in self.later:
+            copy.start()
+        self.later = []
 
     def need(self, *refs):
         for ref in refs:
@@ -69,6 +74,7 @@
             self.out.append(copy)
 
     def finish(self):
+        self.begin()
         for copy in self.fetches.values():
             copy.wait()
         for copy in self.puts.values():
@@ -78,7 +84,7 @@
 
 
 def staged_call(body, name, collective_id, ins, outs, scratch):
-    held_in = [i for i, (how, _) in enumerate(ins) if how == "h"]
+    held_in = [i for i, (how, _) in enumerate(ins) if how in "hl"]
     held_out = [i for i, (how, _) in enumerate(outs) if how == "h"]
 
     def kernel(*refs):
@@ -88,16 +94,19 @@
         own, refs = refs[: len(scratch)], refs[len(scratch) :]
         in_held, refs = refs[: len(held_in)], refs[len(held_in) :]
         out_held, (in_sems, out_sems) = refs[: len(held_out)], refs[len(held_out) :]
-        fetches, puts = {}, {}
+        fetches, later, puts = {}, [], {}
         for n, i in enumerate(held_in):
             copy = pltpu.make_async_copy(given[i], in_held[n], in_sems.at[n])
-            copy.start()
+            if ins[i][0] == "l":
+                later.append(copy)
+            else:
+                copy.start()
             given[i] = in_held[n]
             fetches[id(given[i])] = copy
         for n, i in enumerate(held_out):
             puts[id(out_held[n])] = pltpu.make_async_copy(out_held[n], results[i], out_sems.at[n])
             results[i] = out_held[n]
-        stage = Staged(fetches, puts)
+        stage = Staged(fetches, later, puts)
         body(stage, *given, *results, *own)
         stage.finish()
 
@@ -286,9 +295,9 @@
 
 
 def gather_kernel(
-    stage, tokens_ref, gain_ref, router_ref, docs_ref, routes_ref, order_ref, w_query_ref,
-    key_matrix_ref, value_matrix_ref, w_out_ref,
-    docs_all_ref, placed_ref, turned_ref, normed_ref, w_all_ref, strips_ref,
+    stage, tokens_ref, router_ref, docs_ref, routes_ref, order_ref, w_query_ref,
+    key_matrix_ref, value_matrix_ref, w_out_ref, w_gate_ref, w_up_ref, w_down_ref,
+    docs_all_ref, placed_ref, turned_ref, tokens_all_ref, w_all_ref, strips_ref, gate_up_ref, down_ref,
     held_ref, query_held, key_held, value_held,
     w_send, w_recv, o_send, o_recv, d_send, d_recv, c_send, c_recv, local,
 ):
@@ -312,19 +321,28 @@
             w_out_ref.at[pl.ds(pl.multiple_of(me * strip, strip), strip), :], strips_ref.at[z],
             local.at[3],
         ),
+        pltpu.make_async_copy(tokens_ref, held_ref, local.at[4]),
+    ]
+    hidden = w_gate_ref.shape[2]
+    shards = [
+        pltpu.make_async_copy(w_gate_ref.at[me], gate_up_ref.at[:, pl.ds(0, hidden)], local.at[5]),
+        pltpu.make_async_copy(w_up_ref.at[me], gate_up_ref.at[:, pl.ds(hidden, hidden)], local.at[6]),
+        pltpu.make_async_copy(w_down_ref.at[me], down_ref, local.at[7]),
     ]
     for fetch in fetches:
         fetch.start()
-    stage.need(tokens_ref)
-    x = tokens_ref[...].astype(f32)
-    scale = lax.rsqrt(jnp.mean(x * x, axis=-1, keepdims=True) + epsilon)
-    held_ref[...] = (x * scale * gain_ref[...].reshape(1, -1)).astype(bf16)
     met()
     spread = Spread(
-        place, held_ref, lambda owner: normed_ref.at[owner], halves(TOK_DEV), c_send, c_recv
+        place, tokens_ref, lambda owner: tokens_all_ref.at[owner], halves(TOK_DEV), c_send, c_recv
     )
     spread.start()
-    for fetch in fetches:
+    lines = [
+        Line(place, lambda layer: strips_ref.at[layer], o_send, o_recv),
+        Line(place, lambda layer: w_all_ref.at[layer], w_send, w_recv),
+    ]
+    fetches[3].wait()
+    lines[0].start()
+    for fetch in fetches[:3] + fetches[4:]:
         fetch.wait()
 
     def half(held, columns):
@@ -338,23 +356,23 @@
     router = router_ref[...].astype(f32)
     empty = jnp.zeros((ROUTER - router.shape[0], router.shape[1]), f32)
     own[HW:, :] = jnp.concatenate([router, empty], axis=0).astype(bf16)
-    lines = [
-        Line(place, lambda layer: w_all_ref.at[layer], w_send, w_recv),
-        Line(place, lambda layer: strips_ref.at[layer], o_send, o_recv),
-    ]
-    for line in lines:
-        line.start()
+    lines[1].start()
+    for shard in shards:
+        shard.start()
     docs_all_ref[me] = docs_ref[...]
     sent = []
     for j, device in enumerate(place.others()):
         sent.append(remote(docs_ref, docs_all_ref.at[me], d_send.at[j], d_recv.at[j], device))
     for copy in sent:
         copy.start()
-    move = pltpu.make_async_copy(held_ref, normed_ref.at[me], local.at[4])
+    move = pltpu.make_async_copy(held_ref, tokens_all_ref.at[me], local.at[8])
     move.start()
     place_slots(routes_ref, order_ref, placed_ref)
     turned_ref[...] = placed_ref[...].reshape(EXP_WIN * CAP, -1).T
     stage.put(placed_ref, turned_ref)
+    for shard in shards:
+        shard.wait()
+    stage.put(gate_up_ref, down_ref)
     steps = (spread.step1, spread.step2)
     for step in range(1, depth - 1):
         for act in steps[step - 1 : step]:
@@ -377,7 +395,8 @@
 
 
 def gather_call(
-    tokens, gain, router, docs, routes, order, w_query, key_matrix, value_matrix, w_out, depth
+    tokens, router, docs, routes, order, w_query, key_matrix, value_matrix, w_out, w_gate, w_up, w_down,
+    depth,
 ):
     rows, width = tokens.shape
     strip = w_out.shape[0] // GROUP
@@ -387,8 +406,7 @@
         "gather",
         1,
         [
-            ("h", tokens),
-            ("v", gain),
+            ("a", tokens),
             ("v", router),
             ("v", docs),
             ("v", routes),
@@ -397,6 +415,9 @@
             ("a", key_matrix),
             ("a", value_matrix),
             ("a", w_out),
+            ("a", w_gate),
+            ("a", w_up),
+            ("a", w_down),
         ],
         [
             ("v", shape((GROUP,) + docs.shape, jnp.int32)),
@@ -405,6 +426,8 @@
             ("a", shape((GROUP, rows, width), bf16)),
             ("h", shape((depth, ALL, size), bf16)),
             ("h", shape((depth, strip, width), bf16)),
+            ("h", shape((w_gate.shape[1], 2 * w_gate.shape[2]), bf16)),
+            ("h", shape(w_down.shape[1:], bf16)),
         ],
         [
             VMEM((rows, width), bf16),
@@ -415,7 +438,7 @@
         + [DMA((2, depth - 1))] * 4
         + [DMA((GROUP - 1,))] * 2
         + [DMA((Spread.SEMS,))] * 2
-        + [DMA((5,))],
+        + [DMA((9,))],
     )
 
 
@@ -429,8 +452,12 @@
 
 
 def project_block(
-    owner, normed_ref, w_all_ref, cos_ref, sin_ref, qt_ref, kt_ref, vt_ref, k_ref, v_ref
+    owner, tokens_ref, gain_ref, w_all_ref, cos_ref, sin_ref,
+    normed_ref, qt_ref, kt_ref, vt_ref, k_ref, v_ref,
 ):
+    x = tokens_ref[owner].astype(f32)
+    scale = lax.rsqrt(jnp.mean(x * x, axis=-1, keepdims=True) + epsilon)
+    normed_ref[owner] = (x * scale * gain_ref[...].reshape(1, -1)).astype(bf16)
     linear = None
     for s in range(w_all_ref.shape[0]):
         size = w_all_ref.shape[2]
@@ -450,8 +477,10 @@
     v_ref[tokens, :] = values.T.astype(bf16)
 
 
-def projected(span):
+def projected(tokens):
+    span = tokens.shape[0] * tokens.shape[1]
     return [
+        ("h", shape(tokens.shape, bf16)),
         ("h", shape((QW, span), bf16)),
         ("h", shape((HEAD_DIM, span), bf16)),
         ("h", shape((HEAD_DIM, span), bf16)),
@@ -460,23 +489,23 @@
     ]
 
 
-def project_kernel(stage, normed_ref, w_all_ref, cos_ref, sin_ref, *outs):
-    stage.need(normed_ref, w_all_ref, cos_ref, sin_ref)
+def project_kernel(stage, tokens_ref, gain_ref, w_all_ref, cos_ref, sin_ref, *outs):
+    stage.need(tokens_ref, w_all_ref, cos_ref, sin_ref)
 
     def project(i, _):
-        project_block(i, normed_ref, w_all_ref, cos_ref, sin_ref, *outs)
+        project_block(i, tokens_ref, gain_ref, w_all_ref, cos_ref, sin_ref, *outs)
         return 0
 
     lax.fori_loop(0, GROUP, project, 0)
 
 
-def project_call(normed, w_all, cosine, sine):
+def project_call(tokens, gain, w_all, cosine, sine):
     return staged_call(
         project_kernel,
         "project",
         None,
-        [("h", normed), ("h", w_all), ("h", cosine), ("h", sine)],
-        projected(normed.shape[0] * normed.shape[1]),
+        [("h", tokens), ("v", gain), ("h", w_all), ("h", cosine), ("h", sine)],
+        projected(tokens),
         [],
     )
 
@@ -486,21 +515,20 @@
 
 
 def attend_after_project(
-    n_blocks, stage, w_all_ref, normed_ref, cos_ref, sin_ref, *rest,
+    n_blocks, stage, w_all_ref, tokens_ref, cos_ref, sin_ref, gain_ref, *rest,
 ):
-    given, (qt_ref, kt_ref, vt_ref, k_ref, v_ref), rest = rest[:6], rest[6:11], rest[11:]
+    given, outs, rest = rest[:6], rest[6:12], rest[12:]
+    _, qt_ref, _, vt_ref, k_ref, _ = outs
 
     def project_all():
-        stage.need(normed_ref, cos_ref, sin_ref)
+        stage.need(tokens_ref, cos_ref, sin_ref)
 
         def project(i, _):
-            project_block(
-                i, normed_ref, w_all_ref, cos_ref, sin_ref, qt_ref, kt_ref, vt_ref, k_ref, v_ref
-            )
+            project_block(i, tokens_ref, gain_ref, w_all_ref, cos_ref, sin_ref, *outs)
             return 0
 
         lax.fori_loop(0, GROUP, project, 0)
-        stage.put(qt_ref, kt_ref, vt_ref, k_ref, v_ref)
+        stage.put(*outs)
 
     attend_body(n_blocks, stage, project_all, w_all_ref, qt_ref, k_ref, vt_ref, *given, *rest)
 
@@ -547,6 +575,7 @@
 
     lax.fori_loop(0, n_blocks, turn, 0)
     stage.need(strips_ref)
+    stage.begin()
     met()
     strips.start()
     out_weight_ref[:, me] = strips_ref[...]
@@ -690,7 +719,7 @@
 
 
 def attend_call(
-    kernel, ins, docs, strips, tokens, gain, routes, placed, w_all, span, projections
+    kernel, ins, gains, docs, strips, tokens, gain, routes, placed, w_all, span, projections
 ):
     n = docs.shape[0]
     rows, width = tokens.shape
@@ -700,8 +729,9 @@
         functools.partial(kernel, n),
         "attend",
         2,
-        [("h", one) for one in ins]
-        + [("v", docs), ("h", strips), ("h", tokens), ("v", gain), ("v", routes), ("h", placed)],
+        [("l", one) for one in ins]
+        + [("v", one) for one in gains]
+        + [("v", docs), ("h", strips), ("l", tokens), ("v", gain), ("v", routes), ("l", placed)],
         projections
         + [
             ("h", shape((QW, span), f32)),
@@ -752,12 +782,13 @@
     fetch.start()
     stage.need(placed_ref, cotangent_ref, slot_gates_ref)
 
-    def send_grads(j, _):
+    def send_grads(n, _):
+        j = GROUP - n
         to = lax.rem(me + j, GROUP)
         routed = dot(placed_ref[to], cotangent_ref[...])
         own_grads[to] = (routed * slot_gates_ref[to]).astype(bf16)
 
-        @pl.when(j < GROUP)
+        @pl.when(j > 0)
         def _():
             copy(own_grads, grads_ref, g_send, g_recv, j).start()
 
@@ -842,28 +873,36 @@
         pltpu.make_async_copy(rows_ref, rows_held, local.at[1]),
         pltpu.make_async_copy(gate_up_ref, gate_up_held, local.at[2]),
     ]
-    for fetch in fetches:
-        fetch.start()
     count, hidden = active_ref.shape
     width = down_ref.shape[1]
     T = TOK_DEV
     tiles = hidden // T
 
-    def copy(j):
+    def copy(j, half):
         to = lax.rem(me + j, GROUP)
-        return remote(own_ref.at[to], out_ref.at[me], send.at[j], receive.at[j], place.ctx(to))
+        columns = pl.ds(half * (width // 2), width // 2)
+        return remote(
+            own_ref.at[to, :, columns], out_ref.at[me, :, columns], send.at[half, j],
+            receive.at[half, j], place.ctx(to),
+        )
 
     stage.need(active_ref, down_ref)
+    for fetch in fetches:
+        fetch.start()
+    stage.begin()
 
     def out(i, _):
         value = dot(active_ref[...], down_ref[:, block(i)]).astype(bf16)
         own_ref[:, :, block(i)] = value.reshape(GROUP, CAP, T)
         return 0
 
-    lax.fori_loop(0, width // T, out, 0)
-    met()
-    for j in range(1, GROUP):
-        copy(j).start()
+    for half in range(2):
+        tiles_half = width // T // 2
+        lax.fori_loop(half * tiles_half, (half + 1) * tiles_half, out, 0)
+        if half == 0:
+            met()
+        for j in range(1, GROUP):
+            copy(j, half).start()
     move = pltpu.make_async_copy(own_ref.at[me], out_ref.at[me], local.at[3])
     move.start()
     fetches[0].wait()
@@ -893,8 +932,9 @@
 
     lax.fori_loop(0, width // T, over, 0)
     stage.put(back_ref, grad_gate_up_ref)
-    for j in range(1, GROUP):
-        copy(j).wait()
+    for half in range(2):
+        for j in range(1, GROUP):
+            copy(j, half).wait()
     move.wait()
 
 
@@ -911,8 +951,8 @@
             ("h", down),
             ("a", grads),
             ("a", rows),
-            ("h", gate),
-            ("h", up),
+            ("l", gate),
+            ("l", up),
             ("a", gate_up),
         ],
         [
@@ -926,8 +966,8 @@
             VMEM(gate_up.shape, bf16),
             VMEM(slots, bf16),
             VMEM((count, 2 * hidden), bf16),
-            DMA((GROUP,)),
-            DMA((GROUP,)),
+            DMA((2, GROUP)),
+            DMA((2, GROUP)),
             DMA((4,)),
         ],
     )
@@ -944,7 +984,6 @@
     me = place.me
     met = greet(place.others())
     fetch = pltpu.make_async_copy(weight_ref, weight_held, local.at[0])
-    fetch.start()
     rows, width = residual_ref.shape
 
     def copy(source, target, send, receive, j):
@@ -959,6 +998,8 @@
     move.start()
     turned_ref[...] = jnp.zeros_like(turned_ref)
     stage.need(out_ref, placed_ref, slot_gates_ref, cotangent_ref)
+    stage.begin()
+    fetch.start()
 
     def add_expert(e, _):
         came = out_ref[e].astype(f32)
@@ -1049,15 +1090,15 @@
             ("h", out),
             ("a", sent_grad),
             ("a", weight),
-            ("h", residual),
-            ("h", normed),
-            ("h", gates),
+            ("l", residual),
+            ("l", normed),
+            ("l", gates),
             ("h", placed),
-            ("h", placed_t),
+            ("l", placed_t),
             ("h", slot_gates),
             ("h", cotangent),
             ("v", gain),
-            ("h", w_all),
+            ("l", w_all),
         ],
         [
             ("h", shape((rows, width), bf16)),
@@ -1120,22 +1161,29 @@
         place, down_ref, lambda owner: down_all_ref.at[owner], halves(down_ref.shape[0]), e_send, e_recv
     )
     stage.need(attn_ref, attended_ref)
+    stage.begin()
     met()
     lax.fori_loop(0, half, pair_part, 0)
     stage.need(down_ref)
     down_spread.start()
     down_move.start()
 
-    def own_part(n, _):
-        strip_ref[n] = part(n, parity).astype(bf16)
-        return 0
-
-    lax.fori_loop(0, half, own_part, 0)
+    heads = range(HEADS)
+    parts = [slice(h * HEAD_DIM, (h + 1) * HEAD_DIM) for h in heads]
+    stage.need(heads_ref, o_ref)
+
+    def prepare(i, _):
+        for h in heads:
+            product = o_ref[parts[h], block(i)] * heads_ref[i, parts[h], :].astype(f32)
+            delta_ref[i, h : h + 1, :] = jnp.sum(product, axis=0, keepdims=True)
+        return 0
+
+    lax.fori_loop(0, GROUP, prepare, 0)
     for n in range(half):
         pair_copy(n).wait_recv()
 
     def add_pair(n, _):
-        strip_ref[n] = (strip_ref[n].astype(f32) + pair_ref[n].astype(f32)).astype(bf16)
+        strip_ref[n] = (part(n, parity) + pair_ref[n].astype(f32)).astype(bf16)
         return 0
 
     lax.fori_loop(0, half, add_pair, 0)
@@ -1154,18 +1202,7 @@
         return 0
 
     lax.fori_loop(0, n_blocks, turn, 0)
-    heads = range(HEADS)
-    parts = [slice(h * HEAD_DIM, (h + 1) * HEAD_DIM) for h in heads]
-
-    stage.need(heads_ref, o_ref, lse_ref, qt_ref, k_ref, kt_ref, v_ref)
-
-    def prepare(i, _):
-        for h in heads:
-            product = o_ref[parts[h], block(i)] * heads_ref[i, parts[h], :].astype(f32)
-            delta_ref[i, h : h + 1, :] = jnp.sum(product, axis=0, keepdims=True)
-        return 0
-
-    lax.fori_loop(0, GROUP, prepare, 0)
+    stage.need(lse_ref, qt_ref, k_ref, kt_ref, v_ref)
     dq_ref[...] = jnp.zeros_like(dq_ref)
 
     def tile(kb, qb, mask):
@@ -1259,7 +1296,9 @@
         functools.partial(backward_kernel, n),
         "backward",
         5,
-        [("h", one) for one in (attn, attended, down, heads, o, lse, qt, k, kt, v)] + [("v", docs)],
+        [("h", attn), ("h", attended)]
+        + [("l", one) for one in (down, heads, o, lse, qt, k, kt, v)]
+        + [("v", docs)],
         [
             ("h", shape((QW, span), f32)),
             ("h", shape(kt.shape, f32)),
@@ -1300,8 +1339,6 @@
         pltpu.make_async_copy(normed_ref, normed_held, local.at[0]),
         pltpu.make_async_copy(weights_ref, weights_held, local.at[1]),
     ]
-    for fetch in fetches:
-        fetch.start()
     rows, width = tokens_ref.shape
     size = width // depth
 
@@ -1320,8 +1357,6 @@
         pltpu.make_async_copy(shard_ref, shared_ref.at[me], local.at[5]),
         pltpu.make_async_copy(small_shard_ref, small_all_ref.at[me], local.at[6]),
     ]
-    stage.need(gate_up_ref)
-    moves[0].start()
 
     def copy(j):
         to = lax.rem(me + j, GROUP)
@@ -1334,6 +1369,9 @@
         return remote(source.at[to], target.at[z], send.at[j], receive.at[j], place.fsdp(to))
 
     stage.need(dq_ref, dk_ref, dv_ref, cos_ref, sin_ref)
+    stage.begin()
+    for fetch in fetches:
+        fetch.start()
 
     def turn_back(j, _):
         to = lax.rem(me + j, GROUP)
@@ -1352,7 +1390,8 @@
         return 0
 
     lax.fori_loop(1, GROUP + 1, turn_back, 0)
-    stage.need(grad_out_ref)
+    stage.need(gate_up_ref, grad_out_ref)
+    moves[0].start()
     outs = [down(grad_out_ref, out_in, o_send, o_recv, j) for j in range(1, depth)]
     for one in outs:
         one.start()
@@ -1478,18 +1517,18 @@
         [
             ("a", normed),
             ("a", weights),
-            ("h", gate_up),
-            ("h", grad_out),
+            ("l", gate_up),
+            ("l", grad_out),
             ("h", dq),
             ("h", dk),
             ("h", dv),
             ("h", cosine),
             ("h", sine),
-            ("h", tokens),
+            ("l", tokens),
             ("v", gain),
-            ("h", grad_residual),
-            ("h", grad_router),
-            ("h", grad_gain2),
+            ("l", grad_residual),
+            ("l", grad_router),
+            ("l", grad_gain2),
         ],
         [
             ("h", shape((rows, width), f32)),
@@ -1662,37 +1701,29 @@
     own_tokens, own_cotangent = tokens[0], cotangent[0]
 
     route_rows, order_rows = routes[0].T, slot_order[0].T
-    docs, placed, placed_t, normed1, w_all, strips = gather_call(
-        own_tokens, norm1_gain, w_router.T, doc_ids, route_rows, order_rows, w_query, key_matrix,
-        value_matrix, w_out, depth,
-    )
-    w_gate, w_up, w_down, docs = lax.optimization_barrier((w_gate, w_up, w_down, docs))
-    gate_up = gather_z(
-        jnp.concatenate(
-            [
-                lax.dynamic_index_in_dim(w_gate, head, 0, False),
-                lax.dynamic_index_in_dim(w_up, head, 0, False),
-            ],
-            axis=1,
-        )
-    )
-    down = gather_z(lax.dynamic_index_in_dim(w_down, head, 0, False))
+    docs, placed, placed_t, tokens_all, w_all, strips, gate_up, down = gather_call(
+        own_tokens, w_router.T, doc_ids, route_rows, order_rows, w_query, key_matrix, value_matrix,
+        w_out, w_gate, w_up, w_down, depth,
+    )
+    gate_up, down = gather_z(gate_up), gather_z(down)
     if parts > 1:
 
         def gather_far(value, axis):
             return lax.all_gather(value, "ctx", axis=axis, axis_index_groups=far, tiled=True)
 
-        queries, keys_t, values_t, keys, values = project_call(normed1, w_all, cosine, sine)
+        normed1, queries, keys_t, values_t, keys, values = project_call(
+            tokens_all, norm1_gain, w_all, cosine, sine
+        )
         keys, values, docs = gather_far(keys, 0), gather_far(values, 0), gather_far(docs, 0)
         keys_t, values_t = gather_far(keys_t, 1), gather_far(values_t, 1)
         after = attend_call(
-            attend_kernel, [w_all, queries, keys, values_t], docs, strips, own_tokens, norm2_gain,
+            attend_kernel, [w_all, queries, keys, values_t], [], docs, strips, own_tokens, norm2_gain,
             route_rows, placed, w_all, span, [],
         )
     else:
-        queries, keys_t, values_t, keys, values, *after = attend_call(
-            attend_after_project, [w_all, normed1, cosine, sine], docs, strips, own_tokens, norm2_gain,
-            route_rows, placed, w_all, span, projected(span),
+        normed1, queries, keys_t, values_t, keys, values, *after = attend_call(
+            attend_after_project, [w_all, tokens_all, cosine, sine], [norm1_gain], docs, strips,
+            own_tokens, norm2_gain, route_rows, placed, w_all, span, projected(tokens_all),
         )
     (
         attended_f32, log_total, attended, out_weight, weights_all, residual, normed2, gates,

time: 350 us -> 347 us (level)
  transfers between devices with their start and end apart: 4 -> 4, of which waited for: 0 -> 0; matrix products, arithmetic and copies ran while one was open for 0% -> 0% of each run, Pallas kernels for 61% -> 62%
where the time goes in v4:
time: 347 us
  Pallas kernels  332 us (96%)
  between operations  13.9 us (4%)
    pallas_call x7, Pallas kernels, staged_call(): pl.pallas_call(kernel, out_shape=tuple((one for _, one in outs)), in_spec...  316 us
    pallas_call x1, Pallas kernels, output_call(): pl.pallas_call(output_kernel, grid=(count,), out_shape=(shape((size, coun...  16 us
  transfers between devices with their start and end apart: 4, of which 0 were waited for; matrix products, arithmetic and copies ran while one was open for 0% of the time, Pallas kernels for 62%

profile of v4, /device:TPU:0, one launch (start us, length us, event | category | flops | bytes accessed | tf_op | source)
XLA Modules:
  0.0 346.6 jit_solution(3105788754883668761)
XLA Ops:
  7.2 0.0 all-gather.3.cloned.1.call-start
  7.2 38.1 %gather.1 = (s32[8,1,256]{2,1,0:T(1,128)}, bf16[8,64,256]{2,1,0:T(8,128)(2,1)}, bf16[256,512]{1,0:T(8,128)(2,1)}, bf16[8,256,1536]{2,1,0:T(8,128)(2,1)}, bf16[4,...) custom-call(bf16[256,1536]{1,0:T(8,128)(2,1)} %bitcast.17, ...), custom_call_target="tpu_custom_call" | custom-call | tf_op jit(solution)/shard_map/gather/pallas_call | solution.py:113
  45.3 0.0 all-gather.3.cloned.1.call-update
  45.3 0.0 all-gather.5.cloned.1.call-start
  45.4 0.7 all-gather.5.cloned.1.call-update
  46.1 0.0 reduce-scatter.5.cloned.1.call-start
  46.1 71.1 %attend.1 = (bf16[8,256,1536]{2,1,0:T(8,128)(2,1)}, bf16[192,2048]{1,0:T(8,128)(2,1)}, bf16[64,2048]{1,0:T(8,128)(2,1)}, bf16[64,2048]{1,0:T(8,128)(2,1)}, bf16[...) custom-call(bf16[4,368,384]{2,1,0:T(8,128)(2,1)} %get-tuple-element., ...), custom_call_target="tpu_custom_call" | custom-call | tf_op jit(solution)/shard_map/attend/pallas_call | solution.py:113
  117.3 0.0 all-gather.3.cloned.1.call-done.refs_1_.refs_6_
  117.3 43.0 %dispatch.1 = (bf16[8,64,1536]{2,1,0:T(8,128)(2,1)}, bf16[8,64,1536]{2,1,0:T(8,128)(2,1)}, f32[512,512]{1,0:T(8,128)}, f32[512,512]{1,0:T(8,128)}, bf16[512,512]{1,0:T(8,128)(2,1)}, /*index=5*/bf16[512,1536]{1,0:T(8,128)(2,1)}) custom-call(bf16[8,64,1536]{2,1,0:T(8,128)(2,1)} %get-tuple-element.79.refs_0_, ...), custom_call_target="tpu_custom_call" | custom-call | tf_op jit(solution)/shard_map/dispatch/pallas_call | solution.py:113
  160.3 0.0 reduce-scatter.5.cloned.1.call-update
  160.3 0.0 reduce-scatter.3.cloned.1.call-start
  160.3 0.0 all-gather.5.cloned.1.call-done.refs_1_
  160.4 19.9 %expert.1 = (bf16[8,64,1536]{2,1,0:T(8,128)(2,1)}, bf16[512,1536]{1,0:T(8,128)(2,1)}, bf16[1536,1024]{1,0:T(8,128)(2,1)}) custom-call(bf16[512,512]{1,0:T(8,128)(2,1)} %get-tuple-element.82.refs_0_, bf16[512,1536]{1,0:T(8,128)(2,1)} %all-gather.5.cloned.1.call-done.refs_1_, bf16[512,1536]{1,0:T(8,128)(2,1)} %bitcast.24, bf16[512,1536]{1,0:T(8,128)(2,1)} %bitcast.23, ...), custom_call_target="tpu_custom_call" | custom-call | tf_op jit(solution)/shard_map/expert/pallas_call | solution.py:113
  180.3 0.0 reduce-scatter.3.cloned.1.call-update
  180.3 32.7 %combine.1 = (bf16[256,1536]{1,0:T(8,128)(2,1)}, f32[256,1536]{1,0:T(8,128)}, bf16[8,192,256]{2,1,0:T(8,128)(2,1)}, bf16[256,1536]{1,0:T(8,128)(2,1)}, f32[48,1536]{1,0:T(8,128)}, /*index=5*/f32[1,1536]{1,0:T(1,128)}) custom-call(bf16[8,64,1536]{2,1,0:T(8,128)(2,1)} %get-tuple-element.89.refs_0_, bf16[8,64,1536]{2,1,0:T(8,128)(2,1)} %bitcast.25, ...), custom_call_target="tpu_custom_call" | custom-call | tf_op jit(solution)/shard_map/combine/pallas_call | solution.py:113
  213.0 0.0 reduce-scatter.5.cloned.1.call-done.refs_2_
  213.0 47.1 %backward.1 = (f32[192,2048]{1,0:T(8,128)}, f32[64,2048]{1,0:T(8,128)}, f32[64,2048]{1,0:T(8,128)}, bf16[4,48,1536]{2,1,0:T(8,128)(2,1)}, bf16[8,128,1536]{2,1,0:T(8,128)(2,1)}) custom-call(bf16[256,1536]{1,0:T(8,128)(2,1)} %get-tuple-element.96.refs_0_, bf16[4,8,48,256]{3,2,1,0:T(8,128)(2,1)} %get-tuple-element.97.refs_1_, ...), custom_call_target="tpu_custom_call" | custom-call | tf_op jit(solution)/shard_map/backward/pallas_call | solution.py:113
  260.1 0.0 reduce-scatter.3.cloned.1.call-done.refs_2_
  260.1 63.9 %finish.1 = (f32[256,1536]{1,0:T(8,128)}, bf16[8,320,384]{2,1,0:T(8,128)(2,1)}, bf16[8,48,384]{2,1,0:T(8,128)(2,1)}, bf16[8,48,1536]{2,1,0:T(8,128)(2,1)}, bf16[8,384,1024]{2,1,0:T(8,128)(2,1)}) custom-call(bf16[8,256,1536]{2,1,0:T(8,128)(2,1)} %get-tuple-element.77.refs_0_, bf16[8,4,320,384]{3,2,1,0:T(8,128)(2,1)} %get-tuple-element.78.refs_1_, ...), custom_call_target="tpu_custom_call" | custom-call | tf_op jit(solution)/shard_map/finish/pallas_call | solution.py:113
  324.0 16.0 %output.1 = (f32[384,1536]{1,0:T(8,128)}, f32[384,512]{1,0:T(8,128)}, f32[384,512]{1,0:T(8,128)}, f32[8,48,1536]{2,1,0:T(8,128)}, f32[40,384]{1,0:T(8,128)}, /*i...) custom-call(bf16[8,320,384]{2,1,0:T(8,128)(2,1)} %get-tuple-element., ...), custom_call_target="tpu_custom_call" | custom-call | tf_op jit(solution)/shard_map/output/pallas_call | solution.py:1613
Async XLA Ops:
  7.2 110.1 %all-gather.3.cloned.1.call-start = ((), (), s32[]{:S(2)}) async-start(), calls=%async_computation.2 | async-start | bytes 3932160 | tf_op jit(solution)/shard_map/all_gather | solution.py:1689
  45.3 115.0 %all-gather.5.cloned.1.call-start = ((), (), s32[]{:S(2)}) async-start(), calls=%async_computation.3 | async-start | bytes 1966080 | tf_op jit(solution)/shard_map/all_gather | solution.py:1689
  46.1 166.9 %reduce-scatter.5.cloned.1.call-start = ((), (), s32[]{:S(2)}) async-start(), calls=%async_computation.5 | async-start | bytes 1966080 | tf_op jit(solution)/shard_map/reduce_scatter | solution.py:1692
  160.3 99.8 %reduce-scatter.3.cloned.1.call-start = ((), (), s32[]{:S(2)}) async-start(), calls=%async_computation.4 | async-start | bytes 3932160 | tf_op jit(solution)/shard_map/reduce_scatter | solution.py:1692
Sparse Core Ops, SparseCore 0:
  45.5 62.6 all-gather.2
  109.7 35.7 all-gather.4
  160.4 34.5 reduce-scatter.4
  197.2 59.3 reduce-scatter.2

commit v5 on v4

--- a/solution.py
+++ b/solution.py
@@ -581,8 +581,8 @@
     out_weight_ref[:, me] = strips_ref[...]
     stage.need(w_all_ref)
     move.start()
+    weights.start()
     prepare()
-    weights.start()
 
     def tile(kb, qb, mask):
         kt = k_ref[block(kb), :]
@@ -620,7 +620,7 @@
     def q_block(j, _):
         for at, act in ((1, strips.step1), (2, strips.step2), (5, strips.step3)):
             pl.when(j == at)(act)
-        qb = GROUP - 1 - j
+        qb = jnp.where(j < GROUP // 2, GROUP - 1 - 2 * j, 2 * GROUP - 2 - 2 * j)
         gq = first + qb
         top_ref[...] = jnp.full_like(top_ref, score_masked)
         sum_ref[...] = jnp.ones_like(sum_ref)
@@ -1393,8 +1393,6 @@
     stage.need(gate_up_ref, grad_out_ref)
     moves[0].start()
     outs = [down(grad_out_ref, out_in, o_send, o_recv, j) for j in range(1, depth)]
-    for one in outs:
-        one.start()
     out_in[z] = grad_out_ref[z]
     came_ref[me] = linear_ref[me]
     fetches[0].wait()
@@ -1415,6 +1413,8 @@
         return 0
 
     lax.fori_loop(1, depth + 1, own_weights, 0)
+    for one in outs:
+        one.start()
 
     def total(ref):
         value = ref[0].astype(f32)
@@ -1422,14 +1422,9 @@
             value = value + ref[s].astype(f32)
         return value.astype(bf16)
 
+    expert_spread.start()
     for j in range(1, GROUP):
         copy(j).wait_send()
-    expert_spread.start()
-    for one in outs:
-        one.wait_recv()
-    out_shard_ref[...] = total(out_in)
-    out_spread.start()
-    moves[1].start()
     fetches[1].wait()
     for j in range(1, GROUP):
         copy(j).wait_recv()
@@ -1449,7 +1444,6 @@
         return 0
 
     lax.fori_loop(0, depth, add_heads, 0)
-    out_spread.step1()
     stage.need(tokens_ref, grad_residual_ref, grad_router_ref, grad_gain2_ref)
     x = tokens_ref[...].astype(f32)
     grad_normed = sum_ref[...]
@@ -1477,7 +1471,11 @@
         one.wait_recv()
     shard_ref[...] = total(head_in)
     head_spread.start()
-    out_spread.step2()
+    for one in outs:
+        one.wait_recv()
+    out_shard_ref[...] = total(out_in)
+    out_spread.start()
+    moves[1].start()
     expert_spread.step2()
     for one in smalls:
         one.wait_recv()
@@ -1485,9 +1483,8 @@
     small_spread.start()
     moves[2].start()
     moves[3].start()
-    out_spread.step3()
     expert_spread.step3()
-    spreads = (head_spread, small_spread)
+    spreads = (head_spread, out_spread, small_spread)
     for spread in spreads:
         spread.step1()
     for spread in spreads:

time: 347 us -> 344 us (level)
  Pallas kernels: 332 us -> 328 us
where the time goes in v5:
time: 344 us; the launch traced here: 343 us
  Pallas kernels  328 us (95%)
  between operations  13.9 us (4%)
    pallas_call x7, Pallas kernels, staged_call(): pl.pallas_call(kernel, out_shape=tuple((one for _, one in outs)), in_spec...  312 us
    pallas_call x1, Pallas kernels, output_call(): pl.pallas_call(output_kernel, grid=(count,), out_shape=(shape((size, coun...  16 us
  transfers between devices with their start and end apart: 4, of which 0 were waited for; matrix products, arithmetic and copies ran while one was open for 0% of the time, Pallas kernels for 62%

profile of v5, /device:TPU:0, one launch (start us, length us, event | category | flops | bytes accessed | tf_op | source)
XLA Modules:
  0.0 343.3 jit_solution(5370967827386026592)
XLA Ops:
  7.2 0.0 all-gather.3.cloned.1.call-start
  7.2 38.1 %gather.1 = (s32[8,1,256]{2,1,0:T(1,128)}, bf16[8,64,256]{2,1,0:T(8,128)(2,1)}, bf16[256,512]{1,0:T(8,128)(2,1)}, bf16[8,256,1536]{2,1,0:T(8,128)(2,1)}, bf16[4,...) custom-call(bf16[256,1536]{1,0:T(8,128)(2,1)} %bitcast.17, ...), custom_call_target="tpu_custom_call" | custom-call | tf_op jit(solution)/shard_map/gather/pallas_call | solution.py:113
  45.3 0.0 all-gather.3.cloned.1.call-update
  45.3 0.0 all-gather.5.cloned.1.call-start
  45.4 0.7 all-gather.5.cloned.1.call-update
  46.1 0.0 reduce-scatter.5.cloned.1.call-start
  46.1 70.2 %attend.1 = (bf16[8,256,1536]{2,1,0:T(8,128)(2,1)}, bf16[192,2048]{1,0:T(8,128)(2,1)}, bf16[64,2048]{1,0:T(8,128)(2,1)}, bf16[64,2048]{1,0:T(8,128)(2,1)}, bf16[...) custom-call(bf16[4,368,384]{2,1,0:T(8,128)(2,1)} %get-tuple-element., ...), custom_call_target="tpu_custom_call" | custom-call | tf_op jit(solution)/shard_map/attend/pallas_call | solution.py:113
  116.4 0.0 all-gather.3.cloned.1.call-done.refs_1_.refs_6_
  116.4 42.8 %dispatch.1 = (bf16[8,64,1536]{2,1,0:T(8,128)(2,1)}, bf16[8,64,1536]{2,1,0:T(8,128)(2,1)}, f32[512,512]{1,0:T(8,128)}, f32[512,512]{1,0:T(8,128)}, bf16[512,512]{1,0:T(8,128)(2,1)}, /*index=5*/bf16[512,1536]{1,0:T(8,128)(2,1)}) custom-call(bf16[8,64,1536]{2,1,0:T(8,128)(2,1)} %get-tuple-element.79.refs_0_, ...), custom_call_target="tpu_custom_call" | custom-call | tf_op jit(solution)/shard_map/dispatch/pallas_call | solution.py:113
  159.2 0.0 reduce-scatter.5.cloned.1.call-update
  159.3 0.0 reduce-scatter.3.cloned.1.call-start
  159.3 0.0 all-gather.5.cloned.1.call-done.refs_1_
  159.3 19.9 %expert.1 = (bf16[8,64,1536]{2,1,0:T(8,128)(2,1)}, bf16[512,1536]{1,0:T(8,128)(2,1)}, bf16[1536,1024]{1,0:T(8,128)(2,1)}) custom-call(bf16[512,512]{1,0:T(8,128)(2,1)} %get-tuple-element.82.refs_0_, bf16[512,1536]{1,0:T(8,128)(2,1)} %all-gather.5.cloned.1.call-done.refs_1_, bf16[512,1536]{1,0:T(8,128)(2,1)} %bitcast.24, bf16[512,1536]{1,0:T(8,128)(2,1)} %bitcast.23, ...), custom_call_target="tpu_custom_call" | custom-call | tf_op jit(solution)/shard_map/expert/pallas_call | solution.py:113
  179.2 0.0 reduce-scatter.3.cloned.1.call-update
  179.3 32.7 %combine.1 = (bf16[256,1536]{1,0:T(8,128)(2,1)}, f32[256,1536]{1,0:T(8,128)}, bf16[8,192,256]{2,1,0:T(8,128)(2,1)}, bf16[256,1536]{1,0:T(8,128)(2,1)}, f32[48,1536]{1,0:T(8,128)}, /*index=5*/f32[1,1536]{1,0:T(1,128)}) custom-call(bf16[8,64,1536]{2,1,0:T(8,128)(2,1)} %get-tuple-element.89.refs_0_, bf16[8,64,1536]{2,1,0:T(8,128)(2,1)} %bitcast.25, ...), custom_call_target="tpu_custom_call" | custom-call | tf_op jit(solution)/shard_map/combine/pallas_call | solution.py:113
  211.9 0.0 reduce-scatter.5.cloned.1.call-done.refs_2_
  212.0 47.1 %backward.1 = (f32[192,2048]{1,0:T(8,128)}, f32[64,2048]{1,0:T(8,128)}, f32[64,2048]{1,0:T(8,128)}, bf16[4,48,1536]{2,1,0:T(8,128)(2,1)}, bf16[8,128,1536]{2,1,0:T(8,128)(2,1)}) custom-call(bf16[256,1536]{1,0:T(8,128)(2,1)} %get-tuple-element.96.refs_0_, bf16[4,8,48,256]{3,2,1,0:T(8,128)(2,1)} %get-tuple-element.97.refs_1_, ...), custom_call_target="tpu_custom_call" | custom-call | tf_op jit(solution)/shard_map/backward/pallas_call | solution.py:113
  259.1 0.0 reduce-scatter.3.cloned.1.call-done.refs_2_
  259.1 61.6 %finish.1 = (f32[256,1536]{1,0:T(8,128)}, bf16[8,320,384]{2,1,0:T(8,128)(2,1)}, bf16[8,48,384]{2,1,0:T(8,128)(2,1)}, bf16[8,48,1536]{2,1,0:T(8,128)(2,1)}, bf16[8,384,1024]{2,1,0:T(8,128)(2,1)}) custom-call(bf16[8,256,1536]{2,1,0:T(8,128)(2,1)} %get-tuple-element.77.refs_0_, bf16[8,4,320,384]{3,2,1,0:T(8,128)(2,1)} %get-tuple-element.78.refs_1_, ...), custom_call_target="tpu_custom_call" | custom-call | tf_op jit(solution)/shard_map/finish/pallas_call | solution.py:113
  320.7 16.0 %output.1 = (f32[384,1536]{1,0:T(8,128)}, f32[384,512]{1,0:T(8,128)}, f32[384,512]{1,0:T(8,128)}, f32[8,48,1536]{2,1,0:T(8,128)}, f32[40,384]{1,0:T(8,128)}, /*i...) custom-call(bf16[8,320,384]{2,1,0:T(8,128)(2,1)} %get-tuple-element., ...), custom_call_target="tpu_custom_call" | custom-call | tf_op jit(solution)/shard_map/output/pallas_call | solution.py:1610
Async XLA Ops:
  7.2 109.2 %all-gather.3.cloned.1.call-start = ((), (), s32[]{:S(2)}) async-start(), calls=%async_computation.2 | async-start | bytes 3932160 | tf_op jit(solution)/shard_map/all_gather | solution.py:1686
  45.3 114.0 %all-gather.5.cloned.1.call-start = ((), (), s32[]{:S(2)}) async-start(), calls=%async_computation.3 | async-start | bytes 1966080 | tf_op jit(solution)/shard_map/all_gather | solution.py:1686
  46.1 165.9 %reduce-scatter.5.cloned.1.call-start = ((), (), s32[]{:S(2)}) async-start(), calls=%async_computation.5 | async-start | bytes 1966080 | tf_op jit(solution)/shard_map/reduce_scatter | solution.py:1689
  159.3 99.8 %reduce-scatter.3.cloned.1.call-start = ((), (), s32[]{:S(2)}) async-start(), calls=%async_computation.4 | async-start | bytes 3932160 | tf_op jit(solution)/shard_map/reduce_scatter | solution.py:1689
Sparse Core Ops, SparseCore 0:
  45.5 62.6 all-gather.2
  109.7 35.7 all-gather.4
  159.4 34.6 reduce-scatter.4
  196.2 59.2 reduce-scatter.2

commit v6 on v5

--- a/solution.py
+++ b/solution.py
@@ -1471,21 +1471,21 @@
         one.wait_recv()
     shard_ref[...] = total(head_in)
     head_spread.start()
+    expert_spread.step2()
     for one in outs:
         one.wait_recv()
     out_shard_ref[...] = total(out_in)
     out_spread.start()
-    moves[1].start()
-    expert_spread.step2()
     for one in smalls:
         one.wait_recv()
     small_shard_ref[...] = total(small_in)
     small_spread.start()
-    moves[2].start()
-    moves[3].start()
+    head_spread.step1()
+    for move in moves[1:]:
+        move.start()
     expert_spread.step3()
     spreads = (head_spread, out_spread, small_spread)
-    for spread in spreads:
+    for spread in spreads[1:]:
         spread.step1()
     for spread in spreads:
         spread.step2()

time: 344 us -> 344 us (level)
  no operation moved by 1% of the time
where the time goes in v6:
time: 344 us; the launch traced here: 343 us
  Pallas kernels  328 us (95%)
  between operations  13.9 us (4%)
    pallas_call x7, Pallas kernels, staged_call(): pl.pallas_call(kernel, out_shape=tuple((one for _, one in outs)), in_spec...  312 us
    pallas_call x1, Pallas kernels, output_call(): pl.pallas_call(output_kernel, grid=(count,), out_shape=(shape((size, coun...  16 us
  transfers between devices with their start and end apart: 4, of which 0 were waited for; matrix products, arithmetic and copies ran while one was open for 0% of the time, Pallas kernels for 62%

profile of v6, /device:TPU:0, one launch (start us, length us, event | category | flops | bytes accessed | tf_op | source)
XLA Modules:
  0.0 343.3 jit_solution(9176635459870664900)
XLA Ops:
  7.2 0.0 all-gather.3.cloned.1.call-start
  7.2 38.1 %gather.1 = (s32[8,1,256]{2,1,0:T(1,128)}, bf16[8,64,256]{2,1,0:T(8,128)(2,1)}, bf16[256,512]{1,0:T(8,128)(2,1)}, bf16[8,256,1536]{2,1,0:T(8,128)(2,1)}, bf16[4,...) custom-call(bf16[256,1536]{1,0:T(8,128)(2,1)} %bitcast.17, ...), custom_call_target="tpu_custom_call" | custom-call | tf_op jit(solution)/shard_map/gather/pallas_call | solution.py:113
  45.3 0.0 all-gather.3.cloned.1.call-update
  45.3 0.0 all-gather.5.cloned.1.call-start
  45.4 0.7 all-gather.5.cloned.1.call-update
  46.1 0.0 reduce-scatter.5.cloned.1.call-start
  46.1 70.2 %attend.1 = (bf16[8,256,1536]{2,1,0:T(8,128)(2,1)}, bf16[192,2048]{1,0:T(8,128)(2,1)}, bf16[64,2048]{1,0:T(8,128)(2,1)}, bf16[64,2048]{1,0:T(8,128)(2,1)}, bf16[...) custom-call(bf16[4,368,384]{2,1,0:T(8,128)(2,1)} %get-tuple-element., ...), custom_call_target="tpu_custom_call" | custom-call | tf_op jit(solution)/shard_map/attend/pallas_call | solution.py:113
  116.4 0.0 all-gather.3.cloned.1.call-done.refs_1_.refs_6_
  116.4 42.8 %dispatch.1 = (bf16[8,64,1536]{2,1,0:T(8,128)(2,1)}, bf16[8,64,1536]{2,1,0:T(8,128)(2,1)}, f32[512,512]{1,0:T(8,128)}, f32[512,512]{1,0:T(8,128)}, bf16[512,512]{1,0:T(8,128)(2,1)}, /*index=5*/bf16[512,1536]{1,0:T(8,128)(2,1)}) custom-call(bf16[8,64,1536]{2,1,0:T(8,128)(2,1)} %get-tuple-element.79.refs_0_, ...), custom_call_target="tpu_custom_call" | custom-call | tf_op jit(solution)/shard_map/dispatch/pallas_call | solution.py:113
  159.2 0.0 reduce-scatter.5.cloned.1.call-update
  159.3 0.0 reduce-scatter.3.cloned.1.call-start
  159.3 0.0 all-gather.5.cloned.1.call-done.refs_1_
  159.3 19.9 %expert.1 = (bf16[8,64,1536]{2,1,0:T(8,128)(2,1)}, bf16[512,1536]{1,0:T(8,128)(2,1)}, bf16[1536,1024]{1,0:T(8,128)(2,1)}) custom-call(bf16[512,512]{1,0:T(8,128)(2,1)} %get-tuple-element.82.refs_0_, bf16[512,1536]{1,0:T(8,128)(2,1)} %all-gather.5.cloned.1.call-done.refs_1_, bf16[512,1536]{1,0:T(8,128)(2,1)} %bitcast.24, bf16[512,1536]{1,0:T(8,128)(2,1)} %bitcast.23, ...), custom_call_target="tpu_custom_call" | custom-call | tf_op jit(solution)/shard_map/expert/pallas_call | solution.py:113
  179.2 0.0 reduce-scatter.3.cloned.1.call-update
  179.3 32.7 %combine.1 = (bf16[256,1536]{1,0:T(8,128)(2,1)}, f32[256,1536]{1,0:T(8,128)}, bf16[8,192,256]{2,1,0:T(8,128)(2,1)}, bf16[256,1536]{1,0:T(8,128)(2,1)}, f32[48,1536]{1,0:T(8,128)}, /*index=5*/f32[1,1536]{1,0:T(1,128)}) custom-call(bf16[8,64,1536]{2,1,0:T(8,128)(2,1)} %get-tuple-element.89.refs_0_, bf16[8,64,1536]{2,1,0:T(8,128)(2,1)} %bitcast.25, ...), custom_call_target="tpu_custom_call" | custom-call | tf_op jit(solution)/shard_map/combine/pallas_call | solution.py:113
  211.9 0.0 reduce-scatter.5.cloned.1.call-done.refs_2_
  212.0 47.1 %backward.1 = (f32[192,2048]{1,0:T(8,128)}, f32[64,2048]{1,0:T(8,128)}, f32[64,2048]{1,0:T(8,128)}, bf16[4,48,1536]{2,1,0:T(8,128)(2,1)}, bf16[8,128,1536]{2,1,0:T(8,128)(2,1)}) custom-call(bf16[256,1536]{1,0:T(8,128)(2,1)} %get-tuple-element.96.refs_0_, bf16[4,8,48,256]{3,2,1,0:T(8,128)(2,1)} %get-tuple-element.97.refs_1_, ...), custom_call_target="tpu_custom_call" | custom-call | tf_op jit(solution)/shard_map/backward/pallas_call | solution.py:113
  259.1 0.0 reduce-scatter.3.cloned.1.call-done.refs_2_
  259.1 61.6 %finish.1 = (f32[256,1536]{1,0:T(8,128)}, bf16[8,320,384]{2,1,0:T(8,128)(2,1)}, bf16[8,48,384]{2,1,0:T(8,128)(2,1)}, bf16[8,48,1536]{2,1,0:T(8,128)(2,1)}, bf16[8,384,1024]{2,1,0:T(8,128)(2,1)}) custom-call(bf16[8,256,1536]{2,1,0:T(8,128)(2,1)} %get-tuple-element.77.refs_0_, bf16[8,4,320,384]{3,2,1,0:T(8,128)(2,1)} %get-tuple-element.78.refs_1_, ...), custom_call_target="tpu_custom_call" | custom-call | tf_op jit(solution)/shard_map/finish/pallas_call | solution.py:113
  320.7 16.0 %output.1 = (f32[384,1536]{1,0:T(8,128)}, f32[384,512]{1,0:T(8,128)}, f32[384,512]{1,0:T(8,128)}, f32[8,48,1536]{2,1,0:T(8,128)}, f32[40,384]{1,0:T(8,128)}, /*i...) custom-call(bf16[8,320,384]{2,1,0:T(8,128)(2,1)} %get-tuple-element., ...), custom_call_target="tpu_custom_call" | custom-call | tf_op jit(solution)/shard_map/output/pallas_call | solution.py:1610
Async XLA Ops:
  7.2 109.2 %all-gather.3.cloned.1.call-start = ((), (), s32[]{:S(2)}) async-start(), calls=%async_computation.2 | async-start | bytes 3932160 | tf_op jit(solution)/shard_map/all_gather | solution.py:1686
  45.3 114.0 %all-gather.5.cloned.1.call-start = ((), (), s32[]{:S(2)}) async-start(), calls=%async_computation.3 | async-start | bytes 1966080 | tf_op jit(solution)/shard_map/all_gather | solution.py:1686
  46.1 165.9 %reduce-scatter.5.cloned.1.call-start = ((), (), s32[]{:S(2)}) async-start(), calls=%async_computation.5 | async-start | bytes 1966080 | tf_op jit(solution)/shard_map/reduce_scatter | solution.py:1689
  159.3 99.8 %reduce-scatter.3.cloned.1.call-start = ((), (), s32[]{:S(2)}) async-start(), calls=%async_computation.4 | async-start | bytes 3932160 | tf_op jit(solution)/shard_map/reduce_scatter | solution.py:1689
Sparse Core Ops, SparseCore 0:
  45.5 62.6 all-gather.2
  109.7 35.7 all-gather.4
  159.4 34.6 reduce-scatter.4
  196.2 59.2 reduce-scatter.2
